TPU v7x, 32 devices: a whole 2x2x4 slice. The times are simulated.
32 devices in a mesh: rows: 16 (over z, y, core), protos: 2 (over x).
Axes of the slice: x: 2, y: 2, z: 4, core: 2. Of those that a mesh axis runs over, the one named last changes fastest.
Arguments:
- teacher: bfloat16 [1024, 256], P('rows')
- students: bfloat16 [4096, 256], P('rows')
- prototypes: bfloat16 [256, 65536], P(None, 'protos')
- pairing: int32 [4096], P('rows'), may hold values from 0 to 63
- layout: int32 [4096], P('rows'), may hold values from 0 to 15, as said below
Outputs:
- grad_students: float32 [4096, 256], P('rows')
- grad_protos: float32 [256, 65536], P('rows', 'protos')
Inputs may be any that keep to these rules, and one draw needn't show every extreme that they name: `layout`: in each aligned block of 256 rows, every value appears exactly 16 times.
All inputs are finite; a program needn't handle non-finite values.
Results may differ from a plain program's by a relative error of at most 0.0003.
The roundings to bfloat16 on the way count: a program that leaves them out, or rounds other values in their place, can miss the bound.
Values may be sent and summed in bfloat16 or wider, within the bound.
No kernel may reach another device: no remote copies, remote signals or barrier semaphores. Data moves between devices by JAX's collectives and lax.ppermute only.
A program may use at most 192 MiB of HBM per device.

v0:
```python
import jax
import jax.numpy as jnp
from jax import lax
from jax.sharding import PartitionSpec as P

PROTOS = 65536
ITERS = 2


epsilon = 1e-06
teacher_temp = 0.07
student_temp = 0.1
loss_scale = 16.0


def body(teacher, students, prototypes, pairing, layout):
    row_devices = lax.axis_size("rows")
    tea_count = teacher.shape[0]
    total_teachers = tea_count * row_devices
    local_protos = prototypes.shape[1]
    weights = prototypes.astype(jnp.float32)
    w_norm = jnp.sqrt(jnp.sum(weights * weights, 0) + epsilon)
    w_unit = weights / w_norm
    w_unit_b = w_unit.astype(jnp.bfloat16)
    tea_full = teacher.astype(jnp.float32)
    tea_unit_b = (
        tea_full / jnp.sqrt(jnp.sum(tea_full * tea_full, 1, keepdims=True) + epsilon)
    ).astype(jnp.bfloat16)
    exp_scores = jnp.exp(
        jnp.dot(tea_unit_b, w_unit_b, preferred_element_type=jnp.float32) / teacher_temp
    )
    row_factor = jnp.ones((tea_count,), jnp.float32)
    col_factor = jnp.ones((local_protos,), jnp.float32)
    for sweep in range(ITERS):
        colsum = lax.psum(jnp.sum(exp_scores * row_factor[:, None], 0), "rows")
        col_factor = 1.0 / (PROTOS * colsum)
        rowsum = lax.psum(jnp.sum(exp_scores * col_factor[None, :], 1), "protos")
        row_factor = 1.0 / (total_teachers * rowsum)
    send_order = jnp.argsort(layout, stable=True)
    moved_rows, moved_pairs = (
        lax.all_to_all(students[send_order], "rows", split_axis=0, concat_axis=0, tiled=True),
        lax.all_to_all(pairing[send_order], "rows", split_axis=0, concat_axis=0, tiled=True),
    )
    balanced = total_teachers * exp_scores * row_factor[:, None] * col_factor[None, :]
    target_rows = balanced[moved_pairs]
    stu_full = moved_rows.astype(jnp.float32)
    u_norm = jnp.sqrt(jnp.sum(stu_full * stu_full, 1, keepdims=True) + epsilon)
    stu_unit = stu_full / u_norm
    stu_unit_b = stu_unit.astype(jnp.bfloat16)
    logits = jnp.dot(stu_unit_b, w_unit_b, preferred_element_type=jnp.float32) / student_temp
    exp_logits = jnp.exp(logits)
    denominator = lax.psum(jnp.sum(exp_logits, 1), "protos")
    grad_logits = (
        loss_scale / student_temp * (exp_logits / denominator[:, None] - target_rows)
    ).astype(jnp.bfloat16)
    partial_unit = jnp.einsum(
        "sk,dk->sd", grad_logits, w_unit_b, preferred_element_type=jnp.float32
    )
    grad_unit = lax.psum(partial_unit, "protos")
    grad_rows = (grad_unit - stu_unit * jnp.sum(stu_unit * grad_unit, 1, keepdims=True)) / u_norm
    returned = lax.all_to_all(grad_rows, "rows", split_axis=0, concat_axis=0, tiled=True)
    grad_students = returned[jnp.argsort(send_order)]
    feature_share = prototypes.shape[0] // row_devices
    local_grad = jnp.einsum(
        "sd,sk->dk", stu_unit_b, grad_logits, preferred_element_type=jnp.float32
    )
    projected = (local_grad - w_unit * jnp.sum(w_unit * local_grad, 0)) / w_norm
    grad_protos = lax.psum_scatter(
        lax.slice_in_dim(projected, 0, feature_share * lax.axis_size("rows"), axis=0),
        "rows",
        scatter_dimension=0,
        tiled=True,
    )
    return (grad_students, grad_protos)


def solution(mesh):
    in_specs = (P("rows", None), P("rows", None), P(None, "protos"), P("rows"), P("rows"))
    out_specs = (P("rows", None), P("rows", "protos"))
    return jax.shard_map(body, mesh=mesh, in_specs=in_specs, out_specs=out_specs, check_vma=False)
```

profile of v0, /device:TPU:0, one launch (start us, length us, event | category | flops | bytes accessed | tf_op | source)
XLA Modules:
  0.0 743.1 jit_solution(10115091476078021919)
XLA Ops:
  7.2 3.9 sort.34
  11.1 2.0 gather_fusion.1
  13.8 7.4 all-to-all-start.1
  21.2 7.3 fusion.2
  28.7 3.1 copy-done.2
  31.9 7.5 %fusion.15 = (f32[32768]{0:T(1024)}, f32[64,32768]{1,0:T(8,128)}) fusion(f32[32768]{0:T(1024)S(1)} %add_sqrt_fusion, bf16[256,32768]{1,0:T(8,128)(2,1)S(1)} %copy-done.2, bf16[64,256]{1,0:T(8,128)(2,1)S(1)} %copy-done.5, f32[64]{0:T(128)S(1)} %add_sqrt_fusion.2), kind=kOutput, calls=%fused_computation.45 | convolution fusion | flops 1103118336 | bytes 25460992 | tf_op jit(solution)/shard_map/dot_general | solution.py:30
  39.4 1.8 gather_fusion
  41.2 6.0 all-to-all-start
  48.5 79.9 %all-reduce.5.cloned.1.call-done = f32[32768]{0:T(1024)} async-done(((f32[32768]{0:T(1024)}), f32[32768]{0:T(1024)}) %all-reduce.5.cloned.1.call-update) | async-done | bytes 131088 | tf_op jit(solution)/shard_map/psum | solution.py:35
  128.4 0.9 multiply_divide_fusion.1
  129.3 4.1 multiply_reduce_fusion.3
  133.4 4.9 psum.44
  138.4 4.9 multiply_reduce_fusion.2
  143.3 88.7 %all-reduce.7.cloned.1.call-done = f32[32768]{0:T(1024)} async-done(((f32[32768]{0:T(1024)}), f32[32768]{0:T(1024)}) %all-reduce.7.cloned.1.call-update) | async-done | bytes 131088 | tf_op jit(solution)/shard_map/psum | solution.py:35
  232.1 0.9 multiply_divide_fusion
  233.0 4.0 multiply_reduce_fusion.1
  237.4 18.5 %fusion.16 = (f32[256]{0:T(256)S(1)}, f32[256,32768]{1,0:T(8,128)}) fusion(bf16[256,256]{1,0:T(8,128)(2,1)S(1)} %bitcast_divide_fusion, f32[32768]{0:T(1024)S(1)} %add_sqrt_fusion, bf16[256,32768]{1,0:T(8,128)(2,1)} %param.7), kind=kOutput, calls=%fused_computation.46 | convolution fusion | flops 4336910336 | bytes 50594816 | tf_op jit(solution)/shard_map/dot_general | solution.py:50
  255.9 5.1 all-reduce
  261.0 7.3 multiply_multiply_fusion
  268.3 38.7 %gather_fusion.2 = f32[256,32768]{1,0:T(8,128)} fusion(f32[64,32768]{1,0:T(8,128)} %multiply_multiply_fusion, s32[1024]{0:T(1024)S(1)} %pad_clamp_fusion.1), kind=kCustom, calls=%fused_computation.2 | custom fusion | bytes 67109888 | tf_op jit(solution)/shard_map/gather | solution.py:45
  307.0 27.5 %multiply_convert_fusion = bf16[256,32768]{1,0:T(8,128)(2,1)} fusion(f32[256,32768]{1,0:T(8,128)} %gather_fusion.2, f32[256,32768]{1,0:T(8,128)} %get-tuple-element.11, f32[256]{0:T(256)S(1)} %get-tuple-element.7), kind=kLoop, calls=%fused_computation.13 | loop fusion | flops 33554432 | bytes 83887104 | tf_op jit(solution)/shard_map/convert_element_type | solution.py:55
  334.5 24.8 %multiply_reduce_fusion = (f32[32768]{0:T(1024)S(1)}, f32[256,32768]{1,0:T(8,128)}) fusion(f32[32768]{0:T(1024)S(1)} %add_sqrt_fusion, bf16[256,32768]{1,0:T(8,128)(2,1)} %param.7, bf16[256,256]{1,0:T(8,128)(2,1)S(1)} %bitcast_divide_fusion, bf16[256,32768]{1,0:T(8,128)(2,1)} %multiply_convert_fusion), kind=kOutput, calls=%fused_computation.12 | convolution fusion | flops 4328488960 | bytes 67502080 | tf_op jit(solution)/shard_map/sd,sk->dk/dot_general | solution.py:64
  359.3 13.6 %fusion.11 = f32[256,256]{1,0:T(8,128)} fusion(bf16[256,32768]{1,0:T(8,128)(2,1)} %multiply_convert_fusion, f32[32768]{0:T(1024)S(1)} %add_sqrt_fusion, bf16[256,32768]{1,0:T(8,128)(2,1)} %param.7), kind=kOutput, calls=%fused_computation.44 | convolution fusion | flops 4320133120 | bytes 33947648 | tf_op jit(solution)/shard_map/sk,dk->sd/dot_general | solution.py:56
  373.0 28.0 %subtract_divide_fusion = f32[256,32768]{1,0:T(8,128)} fusion(f32[256,32768]{1,0:T(8,128)} %get-tuple-element.13, f32[32768]{0:T(1024)S(1)} %get-tuple-element.12, f32[32768]{0:T(1024)S(1)} %add_sqrt_fusion, bf16[256,32768]{1,0:T(8,128)(2,1)} %param.7), kind=kLoop, calls=%fused_computation.11 | loop fusion | flops 41943040 | bytes 84148224 | tf_op jit(solution)/shard_map/div | solution.py:67
  401.1 0.9 copy-done.4
  402.0 1.1 multiply_reduce_fusion.4
  403.1 1.8 subtract_divide_fusion.1
  404.9 6.4 all-to-all-start.2
  411.3 3.2 sort.35
  414.5 6.8 all-to-all-done.2
  421.4 1.7 gather_fusion.3
  423.0 313.1 %reduce-scatter.2.cloned.1.call-done = f32[16,32768]{1,0:T(8,128)} async-done(((f32[256,32768]{1,0:T(8,128)}), f32[16,32768]{1,0:T(8,128)}) %reduce-scatter.2.cloned.1.call-update) | async-done | bytes 2097168 | tf_op jit(solution)/shard_map/reduce_scatter | solution.py:68
  (50 shorter events, 2.7 us)
Async XLA Ops:
  7.2 32.3 %copy-start = (bf16[256,256]{1,0:T(8,128)(2,1)S(1)}, bf16[256,256]{1,0:T(8,128)(2,1)}, u32[]{:S(2)}) copy-start(bf16[256,256]{1,0:T(8,128)(2,1)} %param.6) | copy-start | bytes 393220
  7.2 21.4 %copy-start.5 = (bf16[64,256]{1,0:T(8,128)(2,1)S(1)}, bf16[64,256]{1,0:T(8,128)(2,1)}, u32[]{:S(2)}) copy-start(bf16[64,256]{1,0:T(8,128)(2,1)} %param.5) | copy-start | bytes 98308
  11.1 2.7 copy-start.8
  13.8 27.5 %all-to-all-start.1 = ((s32[16,16,1]{1,2,0:T(1,128)}), s32[16,16,1]{1,2,0:T(1,128)S(1)}, u32[]{:S(2)}, u32[]{:S(2)}) async-start(s32[16,16,1]{1,2,0:T(1,128)} %bitcast.2), calls=%async_computation.1 | async-start | bytes 16384 | tf_op jit(solution)/shard_map/all_to_all | solution.py:42
  21.1 107.2 %all-reduce.5.cloned.1.call-start = ((), (), s32[]{:S(2)}) async-start(), calls=%async_computation.4 | async-start | bytes 262144 | tf_op jit(solution)/shard_map/psum | solution.py:35
  21.2 10.7 %copy-start.2 = (bf16[256,32768]{1,0:T(8,128)(2,1)S(1)}, bf16[256,32768]{1,0:T(8,128)(2,1)}, u32[]{:S(2)}) copy-start(bf16[256,32768]{1,0:T(8,128)(2,1)} %param.7) | copy-start | bytes 50331652
  41.2 195.8 %all-to-all-start = ((bf16[16,16,256]{2,1,0:T(8,128)(2,1)}), bf16[16,16,256]{2,1,0:T(8,128)(2,1)S(1)}, u32[]{:S(2)}, u32[]{:S(2)}) async-start(bf16[16,16,256]{2,1,0:T(8,128)(2,1)} %bitcast), calls=%async_computation | async-start | bytes 262144 | tf_op jit(solution)/shard_map/all_to_all | solution.py:41
  47.3 184.8 %all-reduce.7.cloned.1.call-start = ((), (), s32[]{:S(2)}) async-start(), calls=%async_computation.5 | async-start | bytes 262144 | tf_op jit(solution)/shard_map/psum | solution.py:35
  143.3 257.8 %all-reduce.9.cloned.1.call-start = ((), (), s32[]{:S(2)}) async-start(), calls=%async_computation.6 | async-start | bytes 524288 | tf_op jit(solution)/shard_map/psum | solution.py:59
  237.0 18.8 %copy-start.3 = (bf16[16,16,256]{2,1,0:T(8,128)(2,1)}, bf16[16,16,256]{2,1,0:T(8,128)(2,1)S(1)}, u32[]{:S(2)}) copy-start(bf16[16,16,256]{2,1,0:T(8,128)(2,1)S(1)} %all-to-all-done) | copy-start | bytes 393220
  237.3 18.6 %copy-start.6 = (f32[256]{0:T(256)}, f32[256]{0:T(256)S(1)}, u32[]{:S(2)}) copy-start(f32[256]{0:T(256)S(1)} %sqrt.27) | copy-start | bytes 3076
  373.0 363.1 %reduce-scatter.2.cloned.1.call-start = ((), (), s32[]{:S(2)}) async-start(), calls=%async_computation.7 | async-start | bytes 35651584 | tf_op jit(solution)/shard_map/reduce_scatter | solution.py:68
  401.1 335.0 %copy-start.1 = (bf16[256,256]{1,0:T(8,128)(2,1)S(1)}, bf16[256,256]{1,0:T(8,128)(2,1)}, u32[]{:S(2)}) copy-start(bf16[256,256]{1,0:T(8,128)(2,1)} %param.6) | copy-start | bytes 393220
  401.1 0.9 copy-start.4
  401.1 0.9 copy-start.7
  401.1 10.2 %copy-start.9 = (s32[256]{0:T(256)S(1)}, s32[256]{0:T(256)}, u32[]{:S(2)}) copy-start(s32[256]{0:T(256)} %copy-done.8) | copy-start | bytes 3076
  404.9 16.4 %all-to-all-start.2 = ((f32[16,16,256]{2,1,0:T(8,128)}), f32[16,16,256]{2,1,0:T(8,128)S(1)}, u32[]{:S(2)}, u32[]{:S(2)}) async-start(f32[16,16,256]{2,1,0:T(8,128)} %bitcast.4), calls=%async_computation.2 | async-start | bytes 524288 | tf_op jit(solution)/shard_map/all_to_all | solution.py:61
Sparse Core Ops, SparseCore 0:
  39.5 88.8 all-reduce.4
  143.4 88.6 all-reduce.6
  373.1 24.8 all-reduce.8
  403.2 332.8 reduce-scatter.1
where the time goes:
time: 751 us; the launch traced here: 743 us
  waiting for transfers between devices  489 us (65%)
  other arithmetic  96 us (13%)
  matrix products  64.5 us (9%)
  local copies, waits for them, and re-layouts  49.6 us (7%)
  starting transfers between devices  19.9 us (3%)
  between operations  14.4 us (2%)
  blocking collectives  10 us (1%)
    reduce_scatter x1, waiting for transfers between devices, body(): lax.psum_scatter(lax.slice_in_dim(projected, 0, feature_share * lax.axis_...  313 us
    psum x2, waiting for transfers between devices, body(): colsum = lax.psum(jnp.sum(exp_scores * row_factor[:, None], 0), 'rows')  169 us
    gather x1, local copies, waits for them, and re-layouts, body(): target_rows = balanced[moved_pairs]  38.7 us
    div x1, other arithmetic, body(): projected = (local_grad - w_unit * jnp.sum(w_unit * local_grad, 0)) / w_norm  28 us
    convert_element_type x1, other arithmetic, body(): grad_logits = (loss_scale / student_temp * (exp_logits / denominator[:, N...  27.5 us
    dot_general x1, matrix products, body(): jnp.einsum('sd,sk->dk', stu_unit_b, grad_logits, preferred_element_type=j...  24.8 us
    dot_general x1, matrix products, body(): jnp.dot(stu_unit_b, w_unit_b, preferred_element_type=jnp.float32)  18.5 us
  transfers between devices with their start and end apart: 7, of which 4 were waited for; matrix products, arithmetic and copies ran while one was open for 9% of the time, Pallas kernels for 0%

commit v1 on v0

v1 whole, which is shorter than its diff:
```python
import functools

import jax
import jax.numpy as jnp
from jax import lax
from jax.experimental import pallas as pl
from jax.experimental.pallas import tpu as pltpu
from jax.sharding import Mesh, PartitionSpec as P

epsilon = 1e-06
teacher_temp = 0.07
student_temp = 0.1
loss_scale = 16.0

LOG2E = 1.4426950408889634
HALVES = 2
LANES = 128
VMEM = 56 * 1024 * 1024
F32 = jnp.float32
BF16 = jnp.bfloat16
F16 = jnp.float16


def params(*semantics):
    return pltpu.CompilerParams(vmem_limit_bytes=VMEM, dimension_semantics=semantics)


def tile_of(size, want):
    return want if size % want == 0 else size


def unit_rows(rows):
    full = rows.astype(F32)
    return full / jnp.sqrt(jnp.sum(full * full, 1, keepdims=True) + epsilon)


def lane_fold(block):
    total = block[:, :LANES]
    for start in range(LANES, block.shape[1], LANES):
        total = total + block[:, start : start + LANES]
    return total


def row_totals(folded):
    return jnp.sum(jnp.transpose(folded), 0, keepdims=True)


def as_column(row):
    return jnp.transpose(jnp.broadcast_to(row, (LANES, row.shape[1])))[:, :1]


def dot(a, b):
    return jnp.dot(a, b, preferred_element_type=F32)


def denominator_kernel(students_ref, weights_ref, total_ref, unit, folded):
    step = pl.program_id(0)

    @pl.when(step == 0)
    def _():
        unit[...] = unit_rows(students_ref[...]).astype(BF16)
        folded[...] = jnp.zeros_like(folded)

    weights = weights_ref[...].astype(F32)
    inverse = 1.0 / jnp.sqrt(jnp.sum(weights * weights, 0, keepdims=True) + epsilon)
    logits = dot(unit[...], (weights * inverse).astype(BF16))
    folded[...] += lane_fold(jnp.exp2(logits * (LOG2E / student_temp)))

    @pl.when(step == pl.num_programs(0) - 1)
    def _():
        total_ref[...] = row_totals(folded[...])


def local_denominator(students, prototypes):
    rows, width = students.shape
    columns = prototypes.shape[1]
    tile = tile_of(columns, 1024)
    return pl.pallas_call(
        denominator_kernel,
        out_shape=jax.ShapeDtypeStruct((1, rows), F32),
        grid=(columns // tile,),
        in_specs=[
            pl.BlockSpec((rows, width), lambda j: (0, 0)),
            pl.BlockSpec((width, tile), lambda j: (0, j)),
        ],
        out_specs=pl.BlockSpec((1, rows), lambda j: (0, 0)),
        scratch_shapes=[pltpu.VMEM((rows, width), BF16), pltpu.VMEM((rows, LANES), F32)],
        compiler_params=params("arbitrary"),
        cost_estimate=pl.CostEstimate(
            flops=2 * rows * width * columns,
            bytes_accessed=2 * width * columns,
            transcendentals=rows * columns,
        ),
        name="denominator",
    )(students, prototypes)


def sweep_kernel(own_ref, other_ref, weights_ref, *rest, first):
    if first:
        total_ref, factor_ref, unit_ref, folded = rest
    else:
        row_ref, total_ref, factor_ref, folded, column = rest
        unit_ref = None
    half = own_ref.shape[0]
    step = pl.program_id(0)

    @pl.when(step == 0)
    def _():
        if first:
            unit_ref[:half, :] = unit_rows(own_ref[...]).astype(BF16)
            unit_ref[half:, :] = unit_rows(other_ref[...]).astype(BF16)
        else:
            column[...] = jnp.transpose(jnp.broadcast_to(row_ref[...], (LANES, 2 * half)))
        folded[...] = jnp.zeros_like(folded)

    for part in range(2):
        span = slice(part * half, (part + 1) * half)
    units = unit_ref[...] if first else jnp.concatenate([own_ref[...], other_ref[...]], 0)
    scores = jnp.exp2(dot(units, weights_ref[...]) * (LOG2E / teacher_temp))
    weighted = scores if first else scores * column[:, :1]
    factor = 1.0 / jnp.sum(weighted, 0, keepdims=True)
    factor_ref[...] = factor
    folded[...] += lane_fold(scores * factor)

    @pl.when(step == pl.num_programs(0) - 1)
    def _():
        total_ref[...] = row_totals(folded[...])


def sweep(own, other, weights, row_factor=None):
    first = row_factor is None
    half, width = own.shape
    columns = weights.shape[1]
    tile = tile_of(columns, 512)
    whole = lambda j: (0, 0)
    out_shape = [
        jax.ShapeDtypeStruct((1, 2 * half), F32),
        jax.ShapeDtypeStruct((1, columns), F32),
    ]
    out_specs = [
        pl.BlockSpec((1, 2 * half), whole),
        pl.BlockSpec((1, tile), lambda j: (0, j)),
    ]
    in_specs = [
        pl.BlockSpec((half, width), whole),
        pl.BlockSpec((half, width), whole),
        pl.BlockSpec((width, tile), lambda j: (0, j)),
    ]
    scratch = [pltpu.VMEM((2 * half, LANES), F32)]
    operands = [own, other, weights]
    if first:
        out_shape.append(jax.ShapeDtypeStruct((2 * half, width), BF16))
        out_specs.append(pl.BlockSpec((2 * half, width), whole))
    else:
        operands.append(row_factor)
        in_specs.append(pl.BlockSpec((1, 2 * half), whole))
        scratch.append(pltpu.VMEM((2 * half, LANES), F32))
    return pl.pallas_call(
        functools.partial(sweep_kernel, first=first),
        out_shape=out_shape,
        grid=(columns // tile,),
        in_specs=in_specs,
        out_specs=out_specs,
        scratch_shapes=scratch,
        compiler_params=params("arbitrary"),
        cost_estimate=pl.CostEstimate(
            flops=4 * half * width * columns,
            bytes_accessed=2 * width * (columns + 2 * half),
            transcendentals=2 * half * columns,
        ),
        name="sweep",
    )(*operands)


def pair_kernel(half_ref, own_ref, other_ref, index_ref, teacher_ref, unit_ref, turned_ref, paired_ref):
    rows = own_ref.shape[1]
    teachers = teacher_ref.shape[0]
    places = lax.broadcasted_iota(jnp.int32, (rows, teachers), 1).astype(F32)
    for part, ref in enumerate((own_ref, other_ref)):
        unit = unit_rows(ref[0])
        unit_ref[0, part] = unit.astype(BF16)
        turned_ref[0, part] = jnp.transpose(unit).astype(BF16)
        chosen = as_column(index_ref[0, part]) == places
        paired_ref[0, part] = dot(
            jnp.where(chosen, 1.0, 0.0).astype(BF16), teacher_ref[...]
        ).astype(BF16)


def pair(half, own, other, index, teachers):
    groups, count, width = own.shape
    tile = tile_of(count, 256)
    held = lambda g, b, half_ref: (lax.rem(g + half_ref[0] + 1, groups), b, 0)
    rows = lambda g, b, half_ref: (g, 0, b, 0)
    lanes = lambda g, b, half_ref: (g, 0, 0, b)
    return pl.pallas_call(
        pair_kernel,
        out_shape=[
            jax.ShapeDtypeStruct((groups, 2, count, width), BF16),
            jax.ShapeDtypeStruct((groups, 2, width, count), BF16),
            jax.ShapeDtypeStruct((groups, 2, count, width), BF16),
        ],
        grid_spec=pltpu.PrefetchScalarGridSpec(
            num_scalar_prefetch=1,
            grid=(groups, count // tile),
            in_specs=[
                pl.BlockSpec((1, tile, width), held),
                pl.BlockSpec((1, tile, width), held),
                pl.BlockSpec((1, 2, 1, tile), lanes),
                pl.BlockSpec(teachers.shape, lambda g, b, half_ref: (0, 0)),
            ],
            out_specs=[
                pl.BlockSpec((1, 2, tile, width), rows),
                pl.BlockSpec((1, 2, width, tile), lanes),
                pl.BlockSpec((1, 2, tile, width), rows),
            ],
        ),
        compiler_params=params("arbitrary", "arbitrary"),
        cost_estimate=pl.CostEstimate(
            flops=4 * groups * count * width * teachers.shape[0],
            bytes_accessed=16 * groups * count * width,
            transcendentals=0,
        ),
        name="pair",
    )(half, own, other, index.reshape(groups, 2, 1, count), teachers)


def gradient_kernel(
    unit_ref,
    turned_ref,
    paired_ref,
    total_ref,
    index_ref,
    row_ref,
    column_ref,
    weights_ref,
    flipped_ref,
    raw_ref,
    norm_ref,
    student_ref,
    proto_ref,
    scale,
    *,
    tile,
    skipped,
):
    block, step = pl.program_id(0), pl.program_id(1)
    rows = unit_ref.shape[2]
    teachers = row_ref.shape[1]
    span = pl.ds(pl.multiple_of(step * tile, tile), tile)

    @pl.when(step == 0)
    def _():
        ones = jnp.ones((rows, LANES), F32)
        scale[0] = as_column(loss_scale / student_temp / total_ref[...]) * ones
        places = lax.broadcasted_iota(jnp.int32, (rows, teachers), 1).astype(F32)
        chosen = jnp.where(as_column(index_ref[...]) == places, row_ref[...], 0.0)
        scale[1] = jnp.sum(chosen, 1, keepdims=True) * (loss_scale / student_temp) * ones

    weights = weights_ref[:, span]
    student = jnp.exp2(dot(unit_ref[0, 0], weights) * (LOG2E / student_temp)) * scale[0][:, :1]
    target = jnp.exp2(dot(paired_ref[0, 0], weights) * (LOG2E / teacher_temp)) * scale[1][:, :1]
    grad = (student - target * column_ref[:, span]).astype(BF16)

    @pl.when(block >= skipped)
    def _():
        share = dot(grad, flipped_ref[span, :])

        @pl.when(step == 0)
        def _():
            student_ref[...] = share

        @pl.when(step > 0)
        def _():
            student_ref[...] += share

    share = dot(turned_ref[0, 0], grad)

    @pl.when(block == 0)
    def _():
        proto_ref[:, span] = share

    @pl.when(block > 0)
    def _():
        proto_ref[:, span] += share

    @pl.when(block == pl.num_programs(0) - 1)
    def _():
        norm = norm_ref[:, span]
        unit = raw_ref[:, span].astype(F32) / norm
        grads = proto_ref[:, span]
        proto_ref[:, span] = (grads - unit * jnp.sum(unit * grads, 0, keepdims=True)) / norm


def gradients(unit, turned, paired, total, index, row_factor, col_factor, weights, raw, norm):
    groups, _, count, width = unit.shape
    columns = weights.shape[1]
    size = tile_of(count, 512)
    tile = tile_of(columns, 512)
    each = count // size
    blocks = groups * 2 * each
    skipped = (groups - 1) * 2 * each
    place = lambda p, j: (p // (2 * each), (p // each) % 2, p % each, 0)
    across = lambda p, j: (p // (2 * each), (p // each) % 2, 0, p % each)
    whole = lambda p, j: (0, 0)
    return pl.pallas_call(
        functools.partial(gradient_kernel, tile=tile, skipped=skipped),
        out_shape=[
            jax.ShapeDtypeStruct((2 * count, width), F32),
            jax.ShapeDtypeStruct((width, columns), F32),
        ],
        grid=(blocks, columns // tile),
        in_specs=[
            pl.BlockSpec((1, 1, size, width), place),
            pl.BlockSpec((1, 1, width, size), across),
            pl.BlockSpec((1, 1, size, width), place),
            pl.BlockSpec((1, size), lambda p, j: (0, p)),
            pl.BlockSpec((1, size), lambda p, j: (0, p)),
            pl.BlockSpec(row_factor.shape, whole),
            pl.BlockSpec((1, columns), whole),
            pl.BlockSpec((width, columns), whole),
            pl.BlockSpec((columns, width), whole),
            pl.BlockSpec((width, columns), whole),
            pl.BlockSpec((1, columns), whole),
        ],
        out_specs=[
            pl.BlockSpec((size, width), lambda p, j: (jnp.maximum(p - skipped, 0), 0)),
            pl.BlockSpec((width, columns), whole),
        ],
        scratch_shapes=[pltpu.VMEM((2, size, LANES), F32)],
        compiler_params=params("arbitrary", "arbitrary"),
        cost_estimate=pl.CostEstimate(
            flops=8 * groups * 2 * count * width * columns,
            bytes_accessed=8 * width * columns,
            transcendentals=4 * groups * count * columns,
        ),
        name="gradients",
    )(
        unit,
        turned,
        paired,
        total.reshape(1, -1),
        index.reshape(1, -1),
        row_factor,
        col_factor,
        weights,
        jnp.transpose(weights),
        raw,
        norm,
    )


def swap(value, axis):
    return lax.ppermute(value, axis, [(0, 1), (1, 0)])


def exchange(value, axes):
    return lax.all_to_all(value, axes, split_axis=0, concat_axis=0, tiled=True)


def gather(value, axes, count):
    return exchange(jnp.tile(value, (count,) + (1,) * (value.ndim - 1)), axes)


def body(teacher, students, prototypes, pairing, layout):
    halves, chips, protos = lax.axis_size("half"), lax.axis_size("chip"), lax.axis_size("protos")
    half, chip, core, proto = (lax.axis_index(a) for a in ("half", "chip", "core", "protos"))
    everyone = ("half", "chip", "core", "protos")
    devices = halves * chips * 2 * protos
    all_chips = halves * chips
    width, held = prototypes.shape
    tea_count, stu_count = teacher.shape[0], students.shape[0]
    teachers = tea_count * all_chips * 2
    columns = held // (chips * 2)
    sweep_columns = columns // halves

    def mine_first(pair_of):
        return jnp.where(core == 0, pair_of, pair_of[::-1])

    tea_own = gather(teacher, ("half", "chip"), all_chips)
    tea_other = swap(tea_own, "core")
    stu_own = gather(students, ("half", "chip"), all_chips)
    stu_other = swap(stu_own, "core")

    raw = lax.dynamic_slice_in_dim(prototypes, (chip * 2 + core) * columns, columns, 1)
    full = raw.astype(F32)
    w_norm = jnp.sqrt(jnp.sum(full * full, 0, keepdims=True) + epsilon)
    weights = (full / w_norm).astype(BF16)
    sweep_weights = lax.dynamic_slice_in_dim(weights, half * sweep_columns, sweep_columns, 1)

    own_total = local_denominator(students, prototypes)
    own_index = (layout % 2) * (all_chips * tea_count) + (layout // 2) * tea_count + pairing

    row_part, _, tea_unit = sweep(tea_own, tea_other, sweep_weights)
    parcel = jnp.concatenate(
        [
            mine_first(row_part.reshape(2, -1)).reshape(-1),
            own_total.reshape(-1),
            own_index.astype(F32),
        ]
    )
    length = parcel.shape[0]
    parcel = jnp.broadcast_to(parcel.reshape(1, length // LANES, LANES), (devices, length // LANES, LANES))
    parcels = exchange(parcel, everyone).reshape(devices, length)
    row_factor = 1.0 / jnp.sum(parcels[:, :teachers], 0)
    row_factor = mine_first(row_factor.reshape(2, -1)).reshape(1, teachers)

    def in_order(values):
        values = jnp.transpose(values, (2, 0, 1, 3))
        values = mine_first(values)
        if halves > 1:
            values = jnp.roll(values, -(half + 1), 1)
        return jnp.transpose(values, (1, 0, 2, 3)).reshape(halves, 2, chips * stu_count)

    by_sender = parcels[:, teachers:].reshape(halves, chips, 2, protos, 2, stu_count)
    total = in_order(jnp.sum(by_sender[:, :, :, :, 0], 3))
    index = in_order(by_sender[:, :, :, 0, 1])
    index = jnp.where(core == 0, index, (index + teachers // 2) % teachers)

    tea_half = teachers // 2
    row_part, col_factor = sweep(tea_unit[:tea_half], tea_unit[tea_half:], sweep_weights, row_factor)
    parcel = mine_first(row_part.reshape(2, -1)).reshape(1, teachers // LANES, LANES)
    parcels = exchange(jnp.broadcast_to(parcel, (devices,) + parcel.shape[1:]), everyone)
    row_factor = 1.0 / jnp.sum(parcels.reshape(devices, teachers), 0)
    row_factor = mine_first(row_factor.reshape(2, -1)).reshape(1, teachers)
    if halves == 2:
        far = swap(col_factor, "half")
        col_factor = jnp.concatenate(
            [jnp.where(half == 0, col_factor, far), jnp.where(half == 0, far, col_factor)], 1
        )

    unit, turned, paired = pair(
        half.reshape(1),
        stu_own.reshape(halves, -1, width),
        stu_other.reshape(halves, -1, width),
        index,
        tea_unit,
    )
    student_part, proto_part = gradients(
        unit, turned, paired, total, index, row_factor, col_factor, weights, raw, w_norm
    )

    share = width // (all_chips * 2)
    kept = lax.dynamic_slice_in_dim(proto_part, half * (width // halves), width // halves, 0)
    power = jnp.floor(jnp.log2(jnp.maximum(jnp.max(jnp.abs(kept)), 1e-30))) - 13.0
    sent = (kept * jnp.exp2(-power)).astype(F16).reshape(chips * 2, share, columns)
    sent = jnp.concatenate(
        [sent, jnp.broadcast_to(power.astype(F16), (chips * 2, share, LANES))], 2
    )
    came = exchange(sent, ("chip", "core"))
    powers = jnp.exp2(came[:, :, columns : columns + 1].astype(F32))
    grad_protos = jnp.transpose(came[:, :, :columns].astype(F32) * powers, (1, 0, 2))
    grad_protos = grad_protos.reshape(share, held)

    student_part = student_part.reshape(2, chips * stu_count, width)
    summed = student_part[0] + swap(student_part[1], "core")
    near = lax.dynamic_slice_in_dim(stu_own, half * chips * stu_count, chips * stu_count, 0)
    near = unit_rows(near)
    summed = summed - near * jnp.sum(near * summed, 1, keepdims=True)
    sent = (summed * 128.0).astype(F16).reshape(chips * protos, stu_count // protos, width)
    came = exchange(sent, ("chip", "protos"))
    part = jnp.sum(came.astype(F32), 0) * (1.0 / 128.0)
    if protos == 2:
        far = swap(part, "protos")
        grad_unit = jnp.concatenate(
            [jnp.where(proto == 0, part, far), jnp.where(proto == 0, far, part)], 0
        )
    else:
        grad_unit = gather(part, "protos", protos)
    stu_full = students.astype(F32)
    u_norm = jnp.sqrt(jnp.sum(stu_full * stu_full, 1, keepdims=True) + epsilon)
    return (grad_unit / u_norm, grad_protos)


def solution(mesh):
    rows, protos = mesh.shape["rows"], mesh.shape["protos"]
    halves = HALVES
    split = Mesh(
        mesh.devices.reshape(halves, rows // (2 * halves), 2, protos),
        ("half", "chip", "core", "protos"),
    )
    over_rows = ("half", "chip", "core")
    in_specs = (
        P(over_rows, None),
        P(over_rows, None),
        P(None, "protos"),
        P(over_rows),
        P(over_rows),
    )
    out_specs = (P(over_rows, None), P(over_rows, "protos"))
    return jax.shard_map(
        body, mesh=split, in_specs=in_specs, out_specs=out_specs, check_vma=False
    )
```

time: 751 us -> 256 us (0.34)
  waiting for transfers between devices: 489 us -> 42.3 us
  Pallas kernels: 0 us -> 135 us
  other arithmetic: 96 us -> 22.4 us
  matrix products: 64.5 us -> 0 us
  local copies, waits for them, and re-layouts: 49.6 us -> 21.1 us
  between operations: 14.4 us -> 1.82 us
  starting transfers between devices: 19.9 us -> 31.4 us
  blocking collectives: 10 us -> 0 us
    reduce_scatter x1 -> x0, waiting for transfers between devices: 313 us -> none  [body(): lax.psum_scatter(lax.slice_in_dim(projected, 0, feature_share * lax.axis_...]
    psum x3 -> x0, waiting for transfers between devices: 169 us -> none  [the longest x2 169 us: body(): colsum = lax.psum(jnp.sum(exp_scores * row_factor[:, None], 0), 'rows')]
    pallas_call x0 -> x5, Pallas kernels: none -> 135 us  [the longest x1 87.5 us: gradients(): pl.pallas_call(functools.partial(gradient_kernel, tile=tile, skipped=skip...]
    dot_general x4 -> x0, matrix products: 64.5 us -> none  [the longest x1 24.8 us: body(): jnp.einsum('sd,sk->dk', stu_unit_b, grad_logits, preferred_element_type=j...]
    gather x4 -> x0, local copies, waits for them, and re-layouts: 44.2 us -> none  [the longest x1 38.7 us: body(): target_rows = balanced[moved_pairs]]
    all_to_all x3 -> x6, waiting for transfers between devices: 6.84 us -> 38.3 us  [exchange(): return lax.all_to_all(value, axes, split_axis=0, concat_axis=0, tiled=True)]
    div x6 -> x1, other arithmetic: 31.8 us -> 0.81 us  [body(): return (grad_unit / u_norm, grad_protos)]
    convert_element_type x1 -> x4, other arithmetic: 27.5 us -> 6.18 us  [the longest x1 2.4 us: body(): (summed * 128.0).astype(F16)]
  transfers between devices with their start and end apart: 7 -> 11, of which waited for: 4 -> 7; matrix products, arithmetic and copies ran while one was open for 9% -> 12% of each run, Pallas kernels for 0% -> 12%
where the time goes in v1:
time: 256 us; the launch traced here: 254 us
  Pallas kernels  135 us (53%)
  waiting for transfers between devices  42.3 us (17%)
  starting transfers between devices  31.4 us (12%)
  other arithmetic  22.4 us (9%)
  local copies, waits for them, and re-layouts  21.1 us (8%)
    pallas_call x1, Pallas kernels, gradients(): pl.pallas_call(functools.partial(gradient_kernel, tile=tile, skipped=skip...  87.5 us
    all_to_all x6, waiting for transfers between devices, exchange(): return lax.all_to_all(value, axes, split_axis=0, concat_axis=0, tiled=True)  38.3 us
    all_to_all x6, starting transfers between devices, exchange(): return lax.all_to_all(value, axes, split_axis=0, concat_axis=0, tiled=True)  27.5 us
    pallas_call x1, Pallas kernels, local_denominator(): pl.pallas_call(denominator_kernel, out_shape=jax.ShapeDtypeStruct((1, row...  25.3 us
    pallas_call x2, Pallas kernels, sweep(): pl.pallas_call(functools.partial(sweep_kernel, first=first), out_shape=ou...  12.3 us
    pallas_call x1, Pallas kernels, pair(): pl.pallas_call(pair_kernel, out_shape=[jax.ShapeDtypeStruct((groups, 2, c...  9.53 us
  transfers between devices with their start and end apart: 11, of which 7 were waited for; matrix products, arithmetic and copies ran while one was open for 12% of the time, Pallas kernels for 12%

profile of v1, /device:TPU:0, one launch (start us, length us, event | category | flops | bytes accessed | tf_op | source)
XLA Modules:
  0.0 253.6 jit_solution(14776243932885251597)
XLA Ops:
  0.6 1.5 tile.5
  2.1 7.3 %all-to-all-start.1 = ((bf16[8,64,256]{2,1,0:T(8,128)(2,1)}), bf16[8,64,256]{2,1,0:T(8,128)(2,1)S(1)}, u32[]{:S(2)}, u32[]{:S(2)}) async-start(bf16[8,64,256]{2,1,0:T(8,128)(2,1)} %tile.5), calls=%async_computation.1 | async-start | bytes 524288 | tf_op jit(solution)/shard_map/all_to_all | solution.py:357
  9.4 2.1 fusion
  11.5 2.0 fusion.1.weights_ref
  13.5 25.3 %denominator.1 = f32[1,256]{1,0:T(1,128)} custom-call(bf16[256,256]{1,0:T(8,128)(2,1)} %students_ref.1, bf16[256,32768]{1,0:T(8,128)(2,1)} %weights_ref.1), custom_call_target="tpu_custom_call" | custom-call | flops 4294967296 | bytes 16777216 | tf_op jit(solution)/shard_map/denominator/pallas_call | solution.py:78
  38.9 2.4 constant_dynamic-slice_fusion.weights_ref
  42.0 6.2 %sweep.2 = (f32[1,1024]{1,0:T(1,128)}, f32[1,2048]{1,0:T(1,128)}, bf16[1024,256]{1,0:T(8,128)(2,1)}) custom-call(bf16[512,256]{1,0:T(8,128)(2,1)} %bitcast.59, bf16[512,256]{1,0:T(8,128)(2,1)} %copy-done.12, bf16[256,2048]{1,0:T(8,128)(2,1)} %constant_dynamic-slice_fusion.weights_ref), custom_call_target="tpu_custom_call" | custom-call | flops 1073741824 | bytes 1572864 | tf_op jit(solution)/shard_map/sweep/pallas_call | solution.py:158
  48.7 1.3 reduce.8
  51.0 6.1 %all-to-all-start.2 = ((f32[32,12,128]{2,1,0:T(8,128)}), f32[32,12,128]{2,1,0:T(8,128)S(1)}, u32[]{:S(2)}, u32[]{:S(2)}) async-start(f32[32,12,128]{2,1,0:T(8,128)} %broadcast_in_dim.9), calls=%async_computation.2 | async-start | bytes 524288 | tf_op jit(solution)/shard_map/all_to_all | solution.py:357
  57.1 1.8 fusion.14
  58.9 4.2 %copy.24.flipped_ref = bf16[4096,256]{1,0:T(8,128)(2,1)} copy(bf16[4096,256]{0,1:T(8,128)(2,1)} %fusion.14) | data formatting | bytes 4194304 | tf_op jit(solution)/shard_map/transpose | solution.py:346
  63.9 3.8 %all-to-all-done.2 = f32[32,12,128]{2,1,0:T(8,128)S(1)} async-done(((f32[32,12,128]{2,1,0:T(8,128)}), f32[32,12,128]{2,1,0:T(8,128)S(1)}, u32[]{:S(2)}, u32[]{:S(2)}) %all-to-all-start.2) | async-done | bytes 196640 | tf_op jit(solution)/shard_map/all_to_all | solution.py:357
  68.8 3.6 %all-to-all-start = ((bf16[8,256,256]{2,1,0:T(8,128)(2,1)}), bf16[8,256,256]{2,1,0:T(8,128)(2,1)S(1)}, u32[]{:S(2)}, u32[]{:S(2)}) async-start(bf16[8,256,256]{2,1,0:T(8,128)(2,1)} %tile.4), calls=%async_computation | async-start | bytes 2097152 | tf_op jit(solution)/shard_map/all_to_all | solution.py:357
  73.8 6.1 %sweep.3 = (f32[1,1024]{1,0:T(1,128)}, f32[1,2048]{1,0:T(1,128)}) custom-call(bf16[512,256]{1,0:T(8,128)(2,1)} %get-tuple-element.24.own_ref, bf16[512,256]{1,0:T(8,128)(2,1)} %get-tuple-element.23.other_ref, bf16[256,2048]{1,0:T(8,128)(2,1)} %constant_dynamic-slice_fusion.weights_ref, f32[1,1024]{1,0:T(1,128)} %bitcast.66), custom_call_target="tpu_custom_call" | custom-call | flops 1073741824 | bytes 1572864 | tf_op jit(solution)/shard_map/sweep/pallas_call | solution.py:158
  79.9 2.8 %collective-permute-start.2 = (f32[1,2048]{1,0:T(1,128)}, f32[1,2048]{1,0:T(1,128)S(1)}, u32[]{:S(2)}, u32[]{:S(2)}) collective-permute-start(f32[1,2048]{1,0:T(1,128)} %get-tuple-element.18), channel_id=1, source_target_pairs={{0,16},{16,0},{1,17},{17,1},{2,18},{18,2},{3,19},{19,3},{4,20},{20... | collective-permute-start | bytes 24584 | tf_op jit(solution)/shard_map/ppermute | solution.py:353
  86.2 12.7 %all-to-all-done = bf16[8,256,256]{2,1,0:T(8,128)(2,1)S(1)} async-done(((bf16[8,256,256]{2,1,0:T(8,128)(2,1)}), bf16[8,256,256]{2,1,0:T(8,128)(2,1)S(1)}, u32[]{:S(2)}, u32[]{:S(2)}) %all-to-all-start) | async-done | bytes 1048608 | tf_op jit(solution)/shard_map/all_to_all | solution.py:357
  99.6 2.7 %all-to-all-start.3 = ((f32[32,8,128]{2,1,0:T(8,128)}), f32[32,8,128]{2,1,0:T(8,128)S(1)}, u32[]{:S(2)}, u32[]{:S(2)}) async-start(f32[32,8,128]{2,1,0:T(8,128)} %broadcast_in_dim.22), calls=%async_computation.3 | async-start | bytes 262144 | tf_op jit(solution)/shard_map/all_to_all | solution.py:357
  103.9 7.0 %all-to-all-done.3 = f32[32,8,128]{2,1,0:T(8,128)S(1)} async-done(((f32[32,8,128]{2,1,0:T(8,128)}), f32[32,8,128]{2,1,0:T(8,128)S(1)}, u32[]{:S(2)}, u32[]{:S(2)}) %all-to-all-start.3) | async-done | bytes 131104 | tf_op jit(solution)/shard_map/all_to_all | solution.py:357
  112.7 9.5 %pair.1 = (bf16[2,2,1024,256]{3,2,1,0:T(8,128)(2,1)}, bf16[2,2,256,1024]{3,2,1,0:T(8,128)(2,1)}, bf16[2,2,1024,256]{3,2,1,0:T(8,128)(2,1)}) custom-call(s32[1]{0:T(128)} %bitcast.half_ref, bf16[2,1024,256]{2,1,0:T(8,128)(2,1)} %bitcast.48, bf16[2,1024,256]{2,1,0:T(8,128)(2,1)} %bitcast.67, f32[2,2,1,1024]{3,2,1,0:T(1,128)} %broadcast_select_fusion.3.index_ref, ...), custom_call_target="tpu_custom_call" | custom-call | flops 2147483648 | bytes 8388608 | tf_op jit(solution)/shard_map/pair/pallas_call | solution.py:195
  122.3 87.5 %gradients.1 = (f32[2048,256]{1,0:T(8,128)}, f32[256,4096]{1,0:T(8,128)}) custom-call(bf16[2,2,1024,256]{3,2,1,0:T(8,128)(2,1)} %get-tuple-element.14.unit_ref, bf16[2,2,256,1024]{3,2,1,0:T(8,128)(2,1)} %get-tuple-element.15.turned_ref, bf16[2,2,1024,256]{3,2,1,0:T(8,128)(2,1)} %get-tuple-element.16.paired_ref, f32[1,4096]{1,0:T(1,128)} %reshape_reshape.3.total_ref, ...), custom_call_target="tpu_custom_call" | custom-call | flops 34359738368 | bytes 8388608 | tf_op jit(solution)/shard_map/gradients/pallas_call | solution.py:305
  209.8 2.3 abs_reduce_fusion
  212.8 1.8 multiply_convert_fusion
  215.8 4.4 %all-to-all-start.5 = ((f16[8,16,4224]{2,1,0:T(8,128)(2,1)}), f16[8,16,4224]{2,1,0:T(8,128)(2,1)}, u32[]{:S(2)}, u32[]{:S(2)}) async-start(f16[8,16,4224]{2,1,0:T(8,128)(2,1)} %concatenate.18), calls=%async_computation.5 | async-start | bytes 2162688 | tf_op jit(solution)/shard_map/all_to_all | solution.py:357
  221.9 2.4 collective-permute-done.3
  224.3 1.6 multiply_reduce_fusion
  225.9 2.4 multiply_convert_fusion.1
  228.3 6.7 %all-to-all-done.5 = f16[8,16,4224]{2,1,0:T(8,128)(2,1)} async-done(((f16[8,16,4224]{2,1,0:T(8,128)(2,1)}), f16[8,16,4224]{2,1,0:T(8,128)(2,1)}, u32[]{:S(2)}, u32[]{:S(2)}) %all-to-all-start.5) | async-done | bytes 1081376 | tf_op jit(solution)/shard_map/all_to_all | solution.py:357
  235.0 3.5 %all-to-all-start.4 = ((f16[8,128,256]{2,1,0:T(8,128)(2,1)}), f16[8,128,256]{2,1,0:T(8,128)(2,1)S(1)}, u32[]{:S(2)}, u32[]{:S(2)}) async-start(f16[8,128,256]{2,1,0:T(8,128)(2,1)} %bitcast.54), calls=%async_computation.4 | async-start | bytes 1048576 | tf_op jit(solution)/shard_map/all_to_all | solution.py:357
  239.5 8.1 %all-to-all-done.4 = f16[8,128,256]{2,1,0:T(8,128)(2,1)S(1)} async-done(((f16[8,128,256]{2,1,0:T(8,128)(2,1)}), f16[8,128,256]{2,1,0:T(8,128)(2,1)S(1)}, u32[]{:S(2)}, u32[]{:S(2)}) %all-to-all-start.4) | async-done | bytes 524320 | tf_op jit(solution)/shard_map/all_to_all | solution.py:357
  248.1 1.5 multiply_bitcast_fusion
  249.7 1.5 copy.29
  251.1 1.6 collective-permute-done.4
  (94 shorter events, 18.2 us)
Async XLA Ops:
  2.1 36.7 %all-to-all-start.1 = ((bf16[8,64,256]{2,1,0:T(8,128)(2,1)}), bf16[8,64,256]{2,1,0:T(8,128)(2,1)S(1)}, u32[]{:S(2)}, u32[]{:S(2)}) async-start(bf16[8,64,256]{2,1,0:T(8,128)(2,1)} %tile.5), calls=%async_computation.1 | async-start | bytes 524288 | tf_op jit(solution)/shard_map/all_to_all | solution.py:357
  11.5 45.6 %copy-start = (bf16[256,4096]{1,0:T(8,128)(2,1)}, bf16[256,4096]{1,0:T(8,128)(2,1)S(1)}, u32[]{:S(2)}) copy-start(bf16[256,4096]{1,0:T(8,128)(2,1)S(1)} %get-tuple-element.22.raw_ref) | copy-start | bytes 6291460
  11.5 45.5 %copy-start.7 = (f32[4096]{0:T(1024)}, f32[4096]{0:T(1024)S(1)}, u32[]{:S(2)}) copy-start(f32[4096]{0:T(1024)S(1)} %add_sqrt_fusion) | copy-start | bytes 49156
  13.5 25.3 %copy-start.9 = (s32[256]{0:T(256)S(1)}, s32[256]{0:T(256)}, u32[]{:S(2)}) copy-start(s32[256]{0:T(256)} %param.10) | copy-start | bytes 3076
  13.5 25.3 %copy-start.10 = (s32[256]{0:T(256)S(1)}, s32[256]{0:T(256)}, u32[]{:S(2)}) copy-start(s32[256]{0:T(256)} %param.11) | copy-start | bytes 3076
  38.8 2.5 copy-start.6
  38.8 2.5 collective-permute-start.1
  41.3 9.0 %copy-start.8 = (f32[1,256]{1,0:T(1,128)S(1)}, f32[1,256]{1,0:T(1,128)}, u32[]{:S(2)}) copy-start(f32[1,256]{1,0:T(1,128)} %denominator.1) | copy-start | bytes 3076
  41.3 0.7 copy-start.12
  51.0 16.8 %all-to-all-start.2 = ((f32[32,12,128]{2,1,0:T(8,128)}), f32[32,12,128]{2,1,0:T(8,128)S(1)}, u32[]{:S(2)}, u32[]{:S(2)}) async-start(f32[32,12,128]{2,1,0:T(8,128)} %broadcast_in_dim.9), calls=%async_computation.2 | async-start | bytes 524288 | tf_op jit(solution)/shard_map/all_to_all | solution.py:357
  58.9 4.2 %copy-start.5 = (bf16[1024,256]{1,0:T(8,128)(2,1)S(1)}, bf16[1024,256]{1,0:T(8,128)(2,1)}, u32[]{:S(2)}) copy-start(bf16[1024,256]{1,0:T(8,128)(2,1)} %get-tuple-element.13.teacher_ref) | copy-start | bytes 1572868
  58.9 8.8 %copy-start.4 = (bf16[256,256]{1,0:T(8,128)(2,1)S(1)}, bf16[256,256]{1,0:T(8,128)(2,1)}, u32[]{:S(2)}) copy-start(bf16[256,256]{1,0:T(8,128)(2,1)} %students_ref.1) | copy-start | bytes 393220
  68.8 30.1 %all-to-all-start = ((bf16[8,256,256]{2,1,0:T(8,128)(2,1)}), bf16[8,256,256]{2,1,0:T(8,128)(2,1)S(1)}, u32[]{:S(2)}, u32[]{:S(2)}) async-start(bf16[8,256,256]{2,1,0:T(8,128)(2,1)} %tile.4), calls=%async_computation | async-start | bytes 2097152 | tf_op jit(solution)/shard_map/all_to_all | solution.py:357
  79.9 22.7 %collective-permute-start.2 = (f32[1,2048]{1,0:T(1,128)}, f32[1,2048]{1,0:T(1,128)S(1)}, u32[]{:S(2)}, u32[]{:S(2)}) collective-permute-start(f32[1,2048]{1,0:T(1,128)} %get-tuple-element.18), channel_id=1, source_target_pairs={{0,16},{16,0},{1,17},{17,1},{2,18},{18,2},{3,19},{19,3},{4,20},{20... | collective-permute-start | bytes 24584 | tf_op jit(solution)/shard_map/ppermute | solution.py:353
  98.9 12.9 %copy-start.1 = (bf16[8,256,256]{2,1,0:T(8,128)(2,1)}, bf16[8,256,256]{2,1,0:T(8,128)(2,1)S(1)}, u32[]{:S(2)}) copy-start(bf16[8,256,256]{2,1,0:T(8,128)(2,1)S(1)} %all-to-all-done) | copy-start | bytes 3145732
  99.6 11.3 %all-to-all-start.3 = ((f32[32,8,128]{2,1,0:T(8,128)}), f32[32,8,128]{2,1,0:T(8,128)S(1)}, u32[]{:S(2)}, u32[]{:S(2)}) async-start(f32[32,8,128]{2,1,0:T(8,128)} %broadcast_in_dim.22), calls=%async_computation.3 | async-start | bytes 262144 | tf_op jit(solution)/shard_map/all_to_all | solution.py:357
  102.3 9.4 %collective-permute-start = (bf16[2048,256]{1,0:T(8,128)(2,1)S(1)}, bf16[2048,256]{1,0:T(8,128)(2,1)S(1)}, u32[]{:S(2)}, u32[]{:S(2)}) collective-permute-start(bf16[2048,256]{1,0:T(8,128)(2,1)S(1)} %bitcast.47), channel_id=1, source_target_pairs={{0,2},{2,0},{1,3},{3,1},{4,6},{6,4},{5,7},{7,5},{8,10},{10,8},{9,1... | collective-permute-start | bytes 3145736 | tf_op jit(solution)/shard_map/ppermute | solution.py:353
  111.7 1.0 copy-start.11
  214.6 5.6 %copy-start.3 = (f32[2048,256]{1,0:T(8,128)S(1)}, f32[2048,256]{1,0:T(8,128)}, u32[]{:S(2)}) copy-start(f32[2048,256]{1,0:T(8,128)} %get-tuple-element.19) | copy-start | bytes 6291460
  215.8 5.8 %copy-start.2 = (bf16[8,256,256]{2,1,0:T(8,128)(2,1)S(1)}, bf16[8,256,256]{2,1,0:T(8,128)(2,1)}, u32[]{:S(2)}) copy-start(bf16[8,256,256]{2,1,0:T(8,128)(2,1)} %copy-done.1) | copy-start | bytes 3145732
  215.8 19.2 %all-to-all-start.5 = ((f16[8,16,4224]{2,1,0:T(8,128)(2,1)}), f16[8,16,4224]{2,1,0:T(8,128)(2,1)}, u32[]{:S(2)}, u32[]{:S(2)}) async-start(f16[8,16,4224]{2,1,0:T(8,128)(2,1)} %concatenate.18), calls=%async_computation.5 | async-start | bytes 2162688 | tf_op jit(solution)/shard_map/all_to_all | solution.py:357
  221.2 3.0 %collective-permute-start.3 = (f32[1024,256]{1,0:T(8,128)}, f32[1024,256]{1,0:T(8,128)}, u32[]{:S(2)}, u32[]{:S(2)}) collective-permute-start(f32[1024,256]{1,0:T(8,128)} %slice.39), channel_id=1, source_target_pairs={{0,2},{2,0},{1,3},{3,1},{4,6},{6,4},{5,7},{7,5},{8,10},{10,8},{9,1... | collective-permute-start | bytes 3145736 | tf_op jit(solution)/shard_map/ppermute | solution.py:353
  235.0 12.6 %all-to-all-start.4 = ((f16[8,128,256]{2,1,0:T(8,128)(2,1)}), f16[8,128,256]{2,1,0:T(8,128)(2,1)S(1)}, u32[]{:S(2)}, u32[]{:S(2)}) async-start(f16[8,128,256]{2,1,0:T(8,128)(2,1)} %bitcast.54), calls=%async_computation.4 | async-start | bytes 1048576 | tf_op jit(solution)/shard_map/all_to_all | solution.py:357
  247.7 5.0 %collective-permute-start.4 = (f32[128,256]{1,0:T(8,128)S(1)}, f32[128,256]{1,0:T(8,128)S(1)}, u32[]{:S(2)}, u32[]{:S(2)}) collective-permute-start(f32[128,256]{1,0:T(8,128)S(1)} %broadcast_multiply_fusion), channel_id=1, source_target_pairs={{0,1},{1,0},{2,3},{3,2},{4,5},{5,4},{6,7},{7,6},{8,9},{9,8},{10,11... | collective-permute-start | bytes 393224 | tf_op jit(solution)/shard_map/ppermute | solution.py:353

commit v2 on v0

v2 whole, which is shorter than its diff:
```python
import functools

import jax
import jax.numpy as jnp
from jax import lax
from jax.experimental import pallas as pl
from jax.experimental.pallas import tpu as pltpu
from jax.sharding import Mesh, PartitionSpec as P

epsilon = 1e-06
teacher_temp = 0.07
student_temp = 0.1
loss_scale = 16.0

LOG2E = 1.4426950408889634
HALVES = 2
LANES = 128
MIB = 1024 * 1024
F32 = jnp.float32
BF16 = jnp.bfloat16
F16 = jnp.float16


def params(limit):
    return pltpu.CompilerParams(
        vmem_limit_bytes=limit * MIB, dimension_semantics=("arbitrary",)
    )


def tile_of(size, want):
    return want if size % want == 0 else size


def unit_rows(rows):
    full = rows.astype(F32)
    return full * (1.0 / jnp.sqrt(jnp.sum(full * full, 1, keepdims=True) + epsilon))


def lane_fold(block):
    total = block[:, :LANES]
    for start in range(LANES, block.shape[1], LANES):
        total = total + block[:, start : start + LANES]
    return total


def widen(column, width):
    return jnp.concatenate([column] * (width // LANES), 1)


def as_columns(values):
    return jnp.concatenate(
        [
            jnp.transpose(jnp.broadcast_to(values[i : i + 1], (LANES, LANES)))
            for i in range(values.shape[0])
        ],
        0,
    )


def as_rows(folded):
    return jnp.concatenate(
        [
            jnp.sum(jnp.transpose(folded[i : i + LANES]), 0, keepdims=True)
            for i in range(0, folded.shape[0], LANES)
        ],
        0,
    )


def dot(a, b):
    return jnp.dot(a, b, preferred_element_type=F32)


def reverse_bits(place, count):
    bits = count.bit_length() - 1
    return sum(((place >> i) & 1) << (bits - 1 - i) for i in range(bits))


class Layout:
    def __init__(self, halves, chips, protos, tea_count, stu_count):
        self.halves, self.chips, self.protos = halves, chips, protos
        self.devices = halves * chips * 2 * protos
        self.tea_rows = halves * chips * tea_count
        self.tea_lanes = 2 * self.tea_rows // LANES
        self.stu_lanes = stu_count // LANES
        self.stu_count = stu_count
        self.block = chips * stu_count

    def sender(self, where, other_half, other_core, place):
        half, chip, core = where[0], where[1], where[2]
        source = (half ^ other_half) * self.chips + (chip ^ reverse_bits(place, self.chips))
        return (source * 2 + (core ^ other_core)) * self.protos

    def teacher_totals(self, where, parcels_ref):
        sums = [None, None]
        for number in range(self.devices):
            side = (number // self.protos) % 2
            piece = parcels_ref[number, : self.tea_lanes]
            sums[side] = piece if sums[side] is None else sums[side] + piece
        cut = self.tea_lanes // 2
        turned = [jnp.concatenate([s[cut:], s[:cut]], 0) for s in sums]
        return jnp.where(where[2] == 0, sums[0] + turned[1], sums[1] + turned[0])


def columns_kernel(where_ref, raw_ref, unit_ref, flipped_ref, norm_ref, copy_ref):
    copy_ref[...] = raw_ref[...]
    full = raw_ref[...].astype(F32)
    norm = jnp.sqrt(jnp.sum(full * full, 0, keepdims=True) + epsilon)
    unit = full * (1.0 / norm)
    unit_ref[...] = unit.astype(BF16)
    flipped_ref[...] = jnp.transpose(unit.astype(BF16))
    norm_ref[...] = norm


def unit_columns(where, prototypes, columns):
    width = prototypes.shape[0]
    tile = tile_of(columns, 1024)
    steps = columns // tile
    return pl.pallas_call(
        columns_kernel,
        out_shape=[
            jax.ShapeDtypeStruct((width, columns), BF16),
            jax.ShapeDtypeStruct((columns, width), BF16),
            jax.ShapeDtypeStruct((1, columns), F32),
            jax.ShapeDtypeStruct((width, columns), BF16),
        ],
        grid_spec=pltpu.PrefetchScalarGridSpec(
            num_scalar_prefetch=1,
            grid=(steps,),
            in_specs=[
                pl.BlockSpec((width, tile), lambda j, w: (0, (w[1] * 2 + w[2]) * steps + j))
            ],
            out_specs=[
                pl.BlockSpec((width, tile), lambda j, w: (0, j)),
                pl.BlockSpec((tile, width), lambda j, w: (j, 0)),
                pl.BlockSpec((1, tile), lambda j, w: (0, j)),
                pl.BlockSpec((width, tile), lambda j, w: (0, j)),
            ],
        ),
        compiler_params=params(50),
        cost_estimate=pl.CostEstimate(
            flops=8 * width * columns, bytes_accessed=6 * width * columns, transcendentals=0
        ),
        name="unit_columns",
    )(where, prototypes)


def denominator_kernel(students_ref, weights_ref, total_ref, unit, folded, *, sub):
    step = pl.program_id(0)

    @pl.when(step == 0)
    def _():
        unit[...] = unit_rows(students_ref[...]).astype(BF16)
        folded[...] = jnp.zeros_like(folded)

    def scaled(start):
        weights = weights_ref[:, start : start + sub].astype(F32)
        inverse = 1.0 / jnp.sqrt(jnp.sum(weights * weights, 0, keepdims=True) + epsilon)
        return (weights * inverse).astype(BF16)

    total = folded[...]
    for start in range(0, weights_ref.shape[1], sub):
        logits = dot(unit[...], scaled(start))
        total = total + lane_fold(jnp.exp2(logits * (LOG2E / student_temp)))
    folded[...] = total

    @pl.when(step == pl.num_programs(0) - 1)
    def _():
        total_ref[...] = as_rows(folded[...])


def local_denominator(students, prototypes, part, parts):
    rows, width = students.shape
    columns = prototypes.shape[1] // parts
    tile = tile_of(columns, 4096)
    steps = columns // tile
    return pl.pallas_call(
        functools.partial(denominator_kernel, sub=tile_of(tile, 512)),
        out_shape=jax.ShapeDtypeStruct((rows // LANES, LANES), F32),
        grid=(steps,),
        in_specs=[
            pl.BlockSpec((rows, width), lambda j: (0, 0)),
            pl.BlockSpec((width, tile), lambda j: (0, part * steps + j)),
        ],
        out_specs=pl.BlockSpec((rows // LANES, LANES), lambda j: (0, 0)),
        scratch_shapes=[pltpu.VMEM((rows, width), BF16), pltpu.VMEM((rows, LANES), F32)],
        compiler_params=params(50),
        cost_estimate=pl.CostEstimate(
            flops=2 * rows * width * columns,
            bytes_accessed=2 * width * columns,
            transcendentals=rows * columns,
        ),
        name="denominator",
    )(students, prototypes)


def sweep_totals(units, weights_ref, column, sub, factor_ref):
    folded = jnp.zeros((units.shape[0], LANES), F32)
    for start in range(0, weights_ref.shape[1], sub):
        scores = jnp.exp2(dot(units, weights_ref[:, start : start + sub]) * (LOG2E / teacher_temp))
        weighted = scores if column is None else scores * widen(column, sub)
        factor = 1.0 / jnp.sum(weighted, 0, keepdims=True)
        if factor_ref is not None:
            factor_ref[:, start : start + sub] = factor
        folded = folded + lane_fold(scores * factor)
    return as_rows(folded)


def first_sweep_kernel(
    where_ref, own_ref, other_ref, weights_ref, pairing_ref, layout_ref, parcel_ref, unit_ref, *, plan, sub
):
    half = own_ref.shape[0]
    unit_ref[:half, :] = unit_rows(own_ref[...]).astype(BF16)
    unit_ref[half:, :] = unit_rows(other_ref[...]).astype(BF16)
    totals = sweep_totals(unit_ref[...], weights_ref, None, sub, None)
    parcel_ref[:, : plan.tea_lanes, :] = jnp.broadcast_to(
        totals[None], (plan.devices,) + totals.shape
    )
    each = plan.tea_rows // (plan.halves * plan.chips)
    layout = layout_ref[...]
    index = (layout & 1) * half + (layout >> 1) * each + pairing_ref[...]
    index = index.astype(F32)
    for i in range(plan.stu_lanes):
        parcel_ref[:, plan.tea_lanes + i, :] = jnp.broadcast_to(
            index[:, i * LANES : (i + 1) * LANES], (plan.devices, LANES)
        )


def second_sweep_kernel(
    where_ref, unit_ref, weights_ref, came_ref, near_ref, far_ref, parcel_ref, factor_ref, *, plan, sub
):
    where = (where_ref[0], where_ref[1], where_ref[2])
    column = as_columns(1.0 / plan.teacher_totals(where, came_ref))
    totals = sweep_totals(unit_ref[...], weights_ref, column, sub, factor_ref)
    totals = jnp.concatenate([totals, near_ref[...] + far_ref[...]], 0)
    parcel_ref[...] = jnp.broadcast_to(totals[None], (plan.devices,) + totals.shape)


def sweep_call(kernel, plan, where, operands, weights_at, columns, out_shape, name):
    width = operands[0].shape[1]

    def spec(number, array):
        if number == weights_at:
            return pl.BlockSpec((width, columns), lambda i, w: (0, w[0]))
        return pl.BlockSpec(array.shape, lambda i, w: (0,) * len(array.shape))

    return pl.pallas_call(
        functools.partial(kernel, plan=plan, sub=tile_of(columns, 256)),
        out_shape=out_shape,
        grid_spec=pltpu.PrefetchScalarGridSpec(
            num_scalar_prefetch=1,
            grid=(1,),
            in_specs=[spec(i, a) for i, a in enumerate(operands)],
            out_specs=[
                pl.BlockSpec(o.shape, functools.partial(lambda n, i, w: (0,) * n, len(o.shape)))
                for o in out_shape
            ],
        ),
        compiler_params=params(16),
        cost_estimate=pl.CostEstimate(
            flops=4 * plan.tea_rows * width * columns,
            bytes_accessed=2 * width * (columns + 2 * plan.tea_rows),
            transcendentals=2 * plan.tea_rows * columns,
        ),
        name=name,
    )(where, *operands)


def pair_kernel(where_ref, own_ref, other_ref, came_ref, teacher_ref, unit_ref, turned_ref, paired_ref, *, plan):
    where = (where_ref[0], where_ref[1], where_ref[2])
    apart = plan.halves - 1 - pl.program_id(0)
    teachers = teacher_ref.shape[0]
    count = plan.stu_count
    lane = lax.broadcasted_iota(jnp.int32, (count, LANES), 1).astype(F32)
    for side, ref in enumerate((own_ref, other_ref)):
        for place in range(plan.chips):
            rows = slice(place * count, (place + 1) * count)
            unit = unit_rows(ref[place, 0]).astype(BF16)
            unit_ref[0, side, rows, :] = unit
            turned_ref[0, side, :, rows] = jnp.transpose(unit)
            sender = plan.sender(where, apart, side, place)
            index = as_columns(came_ref[sender, plan.tea_lanes :, :])
            index = index + jnp.where(where[2] == 0, 0.0, float(teachers // 2))
            index = jnp.where(index >= teachers, index - teachers, index)
            chosen = jnp.concatenate(
                [
                    jnp.where(index == lane + start, 1.0, 0.0).astype(BF16)
                    for start in range(0, teachers, LANES)
                ],
                1,
            )
            paired_ref[0, side, rows, :] = dot(chosen, teacher_ref[...]).astype(BF16)


def pair(plan, where, own, other, came, teachers):
    width = own.shape[3]
    held = pl.BlockSpec(
        (plan.chips, 1, plan.stu_count, width), lambda g, w: (0, plan.halves - 1 - g, 0, 0)
    )
    rows = pl.BlockSpec((1, 2, plan.block, width), lambda g, w: (g, 0, 0, 0))
    return pl.pallas_call(
        functools.partial(pair_kernel, plan=plan),
        out_shape=[
            jax.ShapeDtypeStruct((plan.halves, 2, plan.block, width), BF16),
            jax.ShapeDtypeStruct((plan.halves, 2, width, plan.block), BF16),
            jax.ShapeDtypeStruct((plan.halves, 2, plan.block, width), BF16),
        ],
        grid_spec=pltpu.PrefetchScalarGridSpec(
            num_scalar_prefetch=1,
            grid=(plan.halves,),
            in_specs=[
                held,
                held,
                pl.BlockSpec(came.shape, lambda g, w: (0, 0, 0)),
                pl.BlockSpec(teachers.shape, lambda g, w: (0, 0)),
            ],
            out_specs=[
                rows,
                pl.BlockSpec((1, 2, width, plan.block), lambda g, w: (g, 0, 0, 0)),
                rows,
            ],
        ),
        compiler_params=params(56),
        cost_estimate=pl.CostEstimate(
            flops=4 * plan.halves * plan.block * width * teachers.shape[0],
            bytes_accessed=16 * plan.halves * plan.block * width,
            transcendentals=0,
        ),
        name="pair",
    )(where, own, other, came, teachers)


def fill_scale(plan, where, apart, side, first_ref, second_ref, row_factor, scale):
    teachers = plan.tea_lanes * LANES
    places = lax.broadcasted_iota(jnp.int32, (teachers, LANES), 0).astype(F32)
    own_first = jnp.where(where[2] == 0, 0.0, float(teachers // 2))
    for place in range(plan.chips):
        rows = slice(place * plan.stu_count, (place + 1) * plan.stu_count)
        sender = plan.sender(where, apart, side, place)
        total = second_ref[sender, plan.tea_lanes :, :]
        for proto in range(1, plan.protos):
            total = total + second_ref[sender + proto, plan.tea_lanes :, :]
        scale[0, rows, :] = as_columns((loss_scale / student_temp) / total)
        index = first_ref[sender, plan.tea_lanes :, :] + own_first
        index = jnp.where(index >= teachers, index - teachers, index)
        found = [
            jnp.sum(jnp.where(index[i : i + 1] == places, row_factor[...], 0.0), 0, keepdims=True)
            for i in range(plan.stu_lanes)
        ]
        scale[1, rows, :] = as_columns(jnp.concatenate(found, 0))


def gradient_products(
    unit_ref, turned_ref, paired_ref, factor_ref, weights_ref, flipped_ref, shares_ref, scale,
    grads, sub, fresh,
):
    columns = weights_ref.shape[1]
    tile = tile_of(columns, 4 * sub)

    def products(step, shares):
        base = pl.multiple_of(step * tile, tile)

        def logits(start):
            weights = weights_ref[:, pl.ds(base + start, sub)]
            return dot(unit_ref[0, 0], weights), dot(paired_ref[0, 0], weights)

        ahead = logits(0)
        for start in range(0, tile, sub):
            student, target = ahead
            if start + sub < tile:
                ahead = logits(start + sub)
            span = pl.ds(base + start, sub)
            student = jnp.exp2(student * (LOG2E / student_temp)) * widen(scale[0], sub)
            target = jnp.exp2(target * (LOG2E / teacher_temp)) * (
                widen(scale[1], sub) * factor_ref[:, span]
            )
            grad = (student - target).astype(BF16)
            if shares_ref is not None:
                share = dot(grad, flipped_ref[span, :])
                shares = share if shares is None else shares + share
            share = dot(turned_ref[0, 0], grad)
            grads[:, span] = jnp.where(fresh, 0.0, grads[:, span]) + share
        return shares

    @pl.loop(0, columns // tile)
    def _(step):
        shares = products(step, None)
        if shares_ref is not None:
            shares_ref[...] = jnp.where(step == 0, 0.0, shares_ref[...]) + shares


def near_kernel(
    where_ref,
    unit_ref,
    turned_ref,
    paired_ref,
    first_ref,
    second_ref,
    factor_ref,
    weights_ref,
    flipped_ref,
    own_raw_ref,
    other_raw_ref,
    own_ref,
    other_ref,
    grads_ref,
    scale,
    shares,
    row_factor,
    *,
    plan,
    sub,
):
    where = (where_ref[0], where_ref[1], where_ref[2])
    side = pl.program_id(0)
    count = plan.stu_count

    @pl.when(side == 0)
    def _():
        row_factor[...] = as_columns(
            (loss_scale / student_temp) / plan.teacher_totals(where, second_ref)
        )

    fill_scale(plan, where, 0, side, first_ref, second_ref, row_factor, scale)
    gradient_products(
        unit_ref, turned_ref, paired_ref, factor_ref, weights_ref, flipped_ref, shares, scale,
        grads_ref, sub, side == 0,
    )

    def finish(raw_ref, out_ref):
        for place in range(plan.chips):
            rows = slice(place * count, (place + 1) * count)
            chip = where[1] ^ reverse_bits(place, plan.chips)
            unit = unit_rows(raw_ref[place, 0])
            share = shares[rows]
            share = share - unit * jnp.sum(unit * share, 1, keepdims=True)
            out_ref[pl.ds(pl.multiple_of(chip * count, count), count), :] = share

    @pl.when(side == 0)
    def _():
        finish(own_raw_ref, own_ref)

    @pl.when(side == 1)
    def _():
        finish(other_raw_ref, other_ref)


def whole_spec(array):
    return pl.BlockSpec(
        array.shape, lambda p, w: (0,) * array.ndim, pipeline_mode=pl.Buffered(1)
    )


def near_gradients(plan, where, unit, turned, paired, first, second, factor, weights, flipped, own, other):
    width, columns = weights.shape
    last = plan.halves - 1
    rows = pl.BlockSpec((1, 1, plan.block, width), lambda p, w: (last, p, 0, 0))
    raw = pl.BlockSpec(
        (plan.chips, 1, plan.stu_count, width),
        lambda p, w: (0, 0, 0, 0),
        pipeline_mode=pl.Buffered(1),
    )
    students = jax.ShapeDtypeStruct((plan.block, width), F32)
    out_shape = [students, students, jax.ShapeDtypeStruct((width, columns), F32)]
    return pl.pallas_call(
        functools.partial(near_kernel, plan=plan, sub=tile_of(columns, 256)),
        out_shape=out_shape,
        grid_spec=pltpu.PrefetchScalarGridSpec(
            num_scalar_prefetch=1,
            grid=(2,),
            in_specs=[
                rows,
                pl.BlockSpec((1, 1, width, plan.block), lambda p, w: (last, p, 0, 0)),
                rows,
                whole_spec(first),
                whole_spec(second),
                whole_spec(factor),
                whole_spec(weights),
                whole_spec(flipped),
                raw,
                raw,
            ],
            out_specs=[whole_spec(o) for o in out_shape],
            scratch_shapes=[
                pltpu.VMEM((2, plan.block, LANES), F32),
                pltpu.VMEM((plan.block, width), F32),
                pltpu.VMEM((plan.tea_lanes * LANES, LANES), F32),
            ],
        ),
        compiler_params=params(56),
        cost_estimate=pl.CostEstimate(
            flops=16 * plan.block * width * columns,
            bytes_accessed=8 * width * columns,
            transcendentals=4 * plan.block * columns,
        ),
        name="near_gradients",
    )(where, unit, turned, paired, first, second, factor, weights, flipped, own, other)


def far_kernel(
    where_ref,
    unit_ref,
    turned_ref,
    paired_ref,
    first_ref,
    second_ref,
    factor_ref,
    weights_ref,
    raw_ref,
    norm_ref,
    before_ref,
    proto_ref,
    scale,
    grads,
    row_factor,
    *,
    plan,
    sub,
):
    where = (where_ref[0], where_ref[1], where_ref[2])
    block = pl.program_id(0)
    columns = weights_ref.shape[1]

    @pl.when(block == 0)
    def _():
        row_factor[...] = as_columns(
            (loss_scale / student_temp) / plan.teacher_totals(where, second_ref)
        )
        grads[...] = before_ref[...]

    fill_scale(
        plan, where, plan.halves - 1 - block // 2, block % 2, first_ref, second_ref, row_factor, scale
    )
    gradient_products(
        unit_ref, turned_ref, paired_ref, factor_ref, weights_ref, None, None, scale, grads, sub,
        False,
    )

    @pl.when(block == pl.num_programs(0) - 1)
    def _():
        kept = grads.shape[0] // plan.halves
        mine = pl.ds(pl.multiple_of(where[0] * kept, kept), kept)
        largest = jnp.zeros((kept, LANES), F32)
        for start in range(0, columns, sub):
            span = slice(start, start + sub)
            inverse = 1.0 / norm_ref[:, span]
            unit = raw_ref[:, span].astype(F32) * inverse
            along = jnp.sum(unit * grads[:, span], 0, keepdims=True)
            unit = raw_ref[mine, span].astype(F32) * inverse
            ready = (grads[mine, span] - unit * along) * inverse
            proto_ref[:, span] = ready
            ready = jnp.abs(ready)
            for i in range(0, sub, LANES):
                largest = jnp.maximum(largest, ready[:, i : i + LANES])
        largest = jnp.maximum(jnp.max(jnp.max(largest, 0, keepdims=True), 1, keepdims=True), 1e-30)
        power = jnp.floor(jnp.log2(largest)) - 13.0
        shrink = jnp.exp2(-power)
        for start in range(0, columns, sub):
            span = slice(start, start + sub)
            proto_ref[:, span] = proto_ref[:, span] * shrink
        proto_ref[:, columns:] = jnp.broadcast_to(power, (kept, LANES))


def far_gradients(
    plan, where, part, unit, turned, paired, first, second, factor, weights, raw, norm, before
):
    width = weights.shape[0]
    parts = plan.halves
    columns = weights.shape[1] // parts
    rows = pl.BlockSpec((1, 1, plan.block, width), lambda p, w: (p // 2, p % 2, 0, 0))
    span = lambda p, w: (0, part)
    kept = width // plan.halves
    return pl.pallas_call(
        functools.partial(far_kernel, plan=plan, sub=tile_of(columns, 256)),
        out_shape=jax.ShapeDtypeStruct((kept, columns + LANES), F32),
        grid_spec=pltpu.PrefetchScalarGridSpec(
            num_scalar_prefetch=1,
            grid=(2 * (plan.halves - 1),),
            in_specs=[
                rows,
                pl.BlockSpec((1, 1, width, plan.block), lambda p, w: (p // 2, p % 2, 0, 0)),
                rows,
                whole_spec(first),
                whole_spec(second),
                pl.BlockSpec((1, columns), span),
                pl.BlockSpec((width, columns), span),
                pl.BlockSpec((width, columns), span),
                pl.BlockSpec((1, columns), span),
                pl.BlockSpec((width, columns), span),
            ],
            out_specs=pl.BlockSpec((kept, columns + LANES), lambda p, w: (0, 0)),
            scratch_shapes=[
                pltpu.VMEM((2, plan.block, LANES), F32),
                pltpu.VMEM((width, columns), F32),
                pltpu.VMEM((plan.tea_lanes * LANES, LANES), F32),
            ],
        ),
        compiler_params=params(56),
        cost_estimate=pl.CostEstimate(
            flops=12 * (plan.halves - 1) * plan.block * width * columns,
            bytes_accessed=8 * width * columns,
            transcendentals=4 * (plan.halves - 1) * plan.block * columns,
        ),
        name="far_gradients",
    )(where, unit, turned, paired, first, second, factor, weights, raw, norm, before)


def join_kernel(*refs):
    out_ref = refs[-1]
    count, _, length = refs[0].shape
    columns = length - LANES
    start = 0
    for sender in range(count):
        for ref in refs[:-1]:
            factor = jnp.exp2(ref[sender, :, columns:])
            out_ref[:, start : start + columns] = ref[sender, :, :columns] * widen(factor, columns)
            start += columns


def join(pieces):
    senders, share, length = pieces[0].shape
    columns = (length - LANES) * len(pieces)
    each = tile_of(senders, 2)
    spec = pl.BlockSpec((each, share, length), lambda i: (i, 0, 0))
    return pl.pallas_call(
        join_kernel,
        out_shape=jax.ShapeDtypeStruct((share, senders * columns), F32),
        grid=(senders // each,),
        in_specs=[spec] * len(pieces),
        out_specs=pl.BlockSpec((share, each * columns), lambda i: (0, i)),
        compiler_params=params(16),
        cost_estimate=pl.CostEstimate(
            flops=share * senders * columns,
            bytes_accessed=8 * share * senders * columns,
            transcendentals=0,
        ),
        name="join",
    )(*pieces)


def swap(value, axis):
    return lax.ppermute(value, axis, [(0, 1), (1, 0)])


def exchange(value, axes):
    return lax.all_to_all(value, axes, split_axis=0, concat_axis=0, tiled=True)


def gather(value, axes, count):
    return exchange(jnp.tile(value, (count,) + (1,) * (value.ndim - 1)), axes)


def tie(value, *others):
    return lax.optimization_barrier((value,) + others)[0]


def body(teacher, students, prototypes, pairing, layout):
    halves, chips, protos = lax.axis_size("half"), lax.axis_size("chip"), lax.axis_size("protos")
    half, chip, core, proto = (lax.axis_index(a) for a in ("half", "chip", "core", "protos"))
    everyone = ("half", "chip", "core", "protos")
    all_chips = halves * chips
    width, held = prototypes.shape
    tea_count, stu_count = teacher.shape[0], students.shape[0]
    plan = Layout(halves, chips, protos, tea_count, stu_count)
    columns = held // (chips * 2)
    part_columns = columns // halves
    where = jnp.stack([half, chip, core]).astype(jnp.int32)
    parcel = lambda lanes: jax.ShapeDtypeStruct((plan.devices, lanes, LANES), F32)

    tea_own = gather(teacher, ("half", "chip"), all_chips)
    weights, flipped, norm, raw = unit_columns(where, prototypes, columns)
    near_total = local_denominator(tie(students, weights), prototypes, 0, 2)
    tea_own = tie(tea_own, near_total)
    tea_other = swap(tea_own, "core")
    parcel_one, tea_unit = sweep_call(
        first_sweep_kernel,
        plan,
        where,
        [tea_own, tea_other, weights, pairing.reshape(1, -1), layout.reshape(1, -1)],
        2,
        part_columns,
        [
            parcel(plan.tea_lanes + plan.stu_lanes),
            jax.ShapeDtypeStruct((2 * plan.tea_rows, width), BF16),
        ],
        "first_sweep",
    )
    first = exchange(parcel_one, everyone)
    far_total = local_denominator(tie(students, tea_unit), prototypes, 1, 2)

    markers = [weights, near_total, parcel_one]
    gathered = students[None]
    bit = all_chips // 2
    while bit:
        came = lax.ppermute(
            gathered, ("half", "chip"), [(q, q ^ bit) for q in range(all_chips)]
        )
        if markers:
            came = tie(came, markers.pop(0))
        gathered = jnp.concatenate([gathered, came], 0)
        bit //= 2
    stu_own = gathered.reshape(chips, halves, stu_count, width)
    stu_other = swap(stu_own, "core")

    parcel_two, factor = sweep_call(
        second_sweep_kernel,
        plan,
        where,
        [tea_unit, weights, first, near_total, far_total],
        1,
        part_columns,
        [
            parcel(plan.tea_lanes + plan.stu_lanes),
            jax.ShapeDtypeStruct((1, part_columns), F32),
        ],
        "second_sweep",
    )
    second = exchange(parcel_two, everyone)
    factors = [factor]
    for step in range(1, halves):
        factors.append(
            lax.ppermute(factor, "half", [(h, (h + step) % halves) for h in range(halves)])
        )
    if halves == 2:
        factors = [jnp.where(half == step, factors[0], factors[1]) for step in range(2)]
    elif halves > 2:
        factors = [jnp.stack(factors)[(half - step) % halves] for step in range(halves)]
    factor = jnp.concatenate(factors, 1)
    unit, turned, paired = pair(
        plan, where, stu_own, stu_other, tie(first, parcel_two), tea_unit
    )
    second, unit, turned, paired = lax.optimization_barrier((second, unit, turned, paired))

    rows_of = (unit, turned, paired, first, second, factor, weights)
    own_part, other_part, proto_all = near_gradients(
        plan, where, *rows_of, flipped, stu_own, stu_other
    )
    summed = (own_part + swap(other_part, "core")) * 128.0
    sent = summed.astype(F16).reshape(chips * protos, stu_count // protos, width)
    came = exchange(sent, ("chip", "protos"))
    rows = jnp.sum(came.astype(F32), 0) * (1.0 / 128.0)
    if protos == 2:
        far = swap(rows, "protos")
        grad_unit = jnp.concatenate(
            [jnp.where(proto == 0, rows, far), jnp.where(proto == 0, far, rows)], 0
        )
    else:
        grad_unit = gather(rows, "protos", protos)
    stu_full = students.astype(F32)
    u_norm = jnp.sqrt(jnp.sum(stu_full * stu_full, 1, keepdims=True) + epsilon)
    grad_students = grad_unit / u_norm

    share = width // (all_chips * 2)
    pieces = []
    proto_all = tie(proto_all, sent)
    for part in range(halves):
        proto_part = far_gradients(plan, where, part, *rows_of, raw, norm, proto_all)
        sent = proto_part.astype(F16).reshape(chips * 2, share, part_columns + LANES)
        sent = tie(sent, came)
        proto_all = tie(proto_all, sent)
        pieces.append(exchange(sent, ("chip", "core")).astype(F32))
    return (grad_students, join(pieces))


def solution(mesh):
    rows, protos = mesh.shape["rows"], mesh.shape["protos"]
    halves = HALVES
    split = Mesh(
        mesh.devices.reshape(halves, rows // (2 * halves), 2, protos),
        ("half", "chip", "core", "protos"),
    )
    over_rows = ("half", "chip", "core")
    in_specs = (
        P(over_rows, None),
        P(over_rows, None),
        P(None, "protos"),
        P(over_rows),
        P(over_rows),
    )
    out_specs = (P(over_rows, None), P(over_rows, "protos"))
    return jax.shard_map(
        body, mesh=split, in_specs=in_specs, out_specs=out_specs, check_vma=False
    )
```

time: 751 us -> 172 us (0.23)
  waiting for transfers between devices: 489 us -> 24.3 us
  Pallas kernels: 0 us -> 95.6 us
  other arithmetic: 96 us -> 11.3 us
  matrix products: 64.5 us -> 0 us
  local copies, waits for them, and re-layouts: 49.6 us -> 2.06 us
  starting transfers between devices: 19.9 us -> 36.5 us
  between operations: 14.4 us -> 0.81 us
  blocking collectives: 10 us -> 0 us
    reduce_scatter x1 -> x0, waiting for transfers between devices: 313 us -> none  [body(): lax.psum_scatter(lax.slice_in_dim(projected, 0, feature_share * lax.axis_...]
    psum x3 -> x0, waiting for transfers between devices: 169 us -> none  [the longest x2 169 us: body(): colsum = lax.psum(jnp.sum(exp_scores * row_factor[:, None], 0), 'rows')]
    pallas_call x0 -> x10, Pallas kernels: none -> 95.6 us  [the longest x2 30.3 us: far_gradients(): pl.pallas_call(functools.partial(far_kernel, plan=plan, sub=tile_of(colum...]
    dot_general x4 -> x0, matrix products: 64.5 us -> none  [the longest x1 24.8 us: body(): jnp.einsum('sd,sk->dk', stu_unit_b, grad_logits, preferred_element_type=j...]
    gather x4 -> x0, local copies, waits for them, and re-layouts: 44.2 us -> none  [the longest x1 38.7 us: body(): target_rows = balanced[moved_pairs]]
    div x6 -> x1, other arithmetic: 31.8 us -> 0.81 us  [body(): grad_students = grad_unit / u_norm]
    reduce_sum x6 -> x1, other arithmetic: 21.6 us -> 0.07 us  [body(): rows = jnp.sum(came.astype(F32), 0) * (1.0 / 128.0)]
    convert_element_type x1 -> x5, other arithmetic: 27.5 us -> 6.56 us  [the longest x2 4.25 us: body(): proto_part.astype(F16).reshape(chips * 2, share, part_columns + LANES)]
  transfers between devices with their start and end apart: 7 -> 14, of which waited for: 4 -> 8; matrix products, arithmetic and copies ran while one was open for 9% -> 5% of each run, Pallas kernels for 0% -> 29%
where the time goes in v2:
time: 172 us; the launch traced here: 171 us
  Pallas kernels  95.6 us (56%)
  starting transfers between devices  36.5 us (21%)
  waiting for transfers between devices  24.3 us (14%)
  other arithmetic  11.3 us (7%)
  local copies, waits for them, and re-layouts  2.06 us (1%)
    pallas_call x2, Pallas kernels, far_gradients(): pl.pallas_call(functools.partial(far_kernel, plan=plan, sub=tile_of(colum...  30.3 us
    pallas_call x1, Pallas kernels, near_gradients(): pl.pallas_call(functools.partial(near_kernel, plan=plan, sub=tile_of(colu...  28.6 us
    all_to_all x6, starting transfers between devices, exchange(): return lax.all_to_all(value, axes, split_axis=0, concat_axis=0, tiled=True)  24.9 us
    pallas_call x2, Pallas kernels, local_denominator(): pl.pallas_call(functools.partial(denominator_kernel, sub=tile_of(tile, 51...  14.5 us
    all_to_all x6, waiting for transfers between devices, exchange(): return lax.all_to_all(value, axes, split_axis=0, concat_axis=0, tiled=True)  13.6 us
    ppermute x4, waiting for transfers between devices, swap(): return lax.ppermute(value, axis, [(0, 1), (1, 0)])  8.65 us
    pallas_call x1, Pallas kernels, pair(): pl.pallas_call(functools.partial(pair_kernel, plan=plan), out_shape=[jax....  7.6 us
    pallas_call x2, Pallas kernels, sweep_call(): pl.pallas_call(functools.partial(kernel, plan=plan, sub=tile_of(columns,...  7.49 us
  transfers between devices with their start and end apart: 14, of which 8 were waited for; matrix products, arithmetic and copies ran while one was open for 5% of the time, Pallas kernels for 29%

profile of v2, /device:TPU:0, one launch (start us, length us, event | category | flops | bytes accessed | tf_op | source)
XLA Modules:
  0.0 170.6 jit_solution(9745967067767537876)
XLA Ops:
  0.6 4.1 %collective-permute-start.1 = (bf16[1,256,256]{2,1,0:T(8,128)(2,1)}, bf16[1,256,256]{2,1,0:T(8,128)(2,1)S(1)}, u32[]{:S(2)}, u32[]{:S(2)}) collective-permute-start(bf16[1,256,256]{2,1,0:T(8,128)(2,1)} %bitcast.11), channel_id=1, source_target_pairs={{0,16},{4,20},{8,24},{12,28},{16,0},{20,4},{24,8},{28,12},{1,17},{... | collective-permute-start | bytes 393224 | tf_op jit(solution)/shard_map/ppermute | solution.py:695
  4.8 5.4 %unit_columns.1 = (bf16[256,4096]{1,0:T(8,128)(2,1)S(1)}, bf16[4096,256]{1,0:T(8,128)(2,1)}, f32[1,4096]{1,0:T(1,128)S(1)}, bf16[256,4096]{1,0:T(8,128)(2,1)}) custom-call(s32[3]{0:T(128)S(1)} %pad_add_fusion.where_ref, bf16[256,32768]{1,0:T(8,128)(2,1)} %weights_ref.3), custom_call_target="tpu_custom_call" | custom-call | flops 8388608 | bytes 6291456 | tf_op jit(solution)/shard_map/unit_columns/pallas_call | solution.py:119
  11.3 1.2 collective-permute-start.2
  13.2 5.2 %all-to-all-start = ((bf16[8,64,256]{2,1,0:T(8,128)(2,1)}), bf16[8,64,256]{2,1,0:T(8,128)(2,1)S(1)}, u32[]{:S(2)}, u32[]{:S(2)}) async-start(bf16[8,64,256]{2,1,0:T(8,128)(2,1)} %tile.2), calls=%async_computation | async-start | bytes 524288 | tf_op jit(solution)/shard_map/all_to_all | solution.py:646
  18.4 7.2 %denominator.2.near_ref = f32[2,128]{1,0:T(2,128)S(1)} custom-call(bf16[256,256]{1,0:T(8,128)(2,1)S(1)} %copy-done, bf16[256,32768]{1,0:T(8,128)(2,1)} %weights_ref.3), custom_call_target="tpu_custom_call" | custom-call | flops 2147483648 | bytes 8388608 | tf_op jit(solution)/shard_map/denominator/pallas_call | solution.py:177
  26.5 2.0 %collective-permute-start.3 = (bf16[4,256,256]{2,1,0:T(8,128)(2,1)}, bf16[4,256,256]{2,1,0:T(8,128)(2,1)}, u32[]{:S(2)}, u32[]{:S(2)}) collective-permute-start(bf16[4,256,256]{2,1,0:T(8,128)(2,1)} %pad_maximum_fusion.1), channel_id=1, source_target_pairs={{0,4},{4,0},{8,12},{12,8},{16,20},{20,16},{24,28},{28,24},{1,5},{5... | collective-permute-start | bytes 1572872 | tf_op jit(solution)/shard_map/ppermute | solution.py:695
  28.6 1.5 collective-permute-done.other_ref
  30.1 3.8 %first_sweep.1 = (f32[32,10,128]{2,1,0:T(8,128)}, bf16[1024,256]{1,0:T(8,128)(2,1)S(1)}) custom-call(s32[3]{0:T(128)S(1)} %pad_add_fusion.where_ref, bf16[512,256]{1,0:T(8,128)(2,1)S(1)} %bitcast.16, bf16[512,256]{1,0:T(8,128)(2,1)S(1)} %collective-permute-done.other_ref, bf16[256,4096]{1,0:T(8,128)(2,1)S(1)} %get-tuple-element.31.weights_ref, ...), custom_call_target="tpu_custom_call" | custom-call | flops 1073741824 | bytes 1572864 | tf_op jit(solution)/shard_map/first_sweep/pallas_call | solution.py:247
  33.9 4.6 %all-to-all-start.1 = ((f32[32,10,128]{2,1,0:T(8,128)}), f32[32,10,128]{2,1,0:T(8,128)S(1)}, u32[]{:S(2)}, u32[]{:S(2)}) async-start(f32[32,10,128]{2,1,0:T(8,128)} %get-tuple-element.35), calls=%async_computation.1 | async-start | bytes 524288 | tf_op jit(solution)/shard_map/all_to_all | solution.py:646
  38.5 1.7 collective-permute-done.3
  40.1 2.2 %pad_maximum_fusion = bf16[8,256,256]{2,1,0:T(8,128)(2,1)} fusion(bf16[4,256,256]{2,1,0:T(8,128)(2,1)} %collective-permute-done.3, bf16[2,256,256]{2,1,0:T(8,128)(2,1)S(1)} %collective-permute-done.2, bf16[1,256,256]{2,1,0:T(8,128)(2,1)S(1)} %collective-permute-done.1, bf16[1,256,256]{2,1,0:T(8,128)(2,1)S(1)} %bitcast.14), kind=kLoop, calls=%fused_computation | loop fusion | flops 1572864 | bytes 2097152 | tf_op jit(solution)/shard_map/concatenate | solution.py:700
  42.3 7.2 %denominator.3.far_ref = f32[2,128]{1,0:T(2,128)S(1)} custom-call(bf16[256,256]{1,0:T(8,128)(2,1)S(1)} %copy-done, bf16[256,32768]{1,0:T(8,128)(2,1)} %weights_ref.3), custom_call_target="tpu_custom_call" | custom-call | flops 2147483648 | bytes 8388608 | tf_op jit(solution)/shard_map/denominator/pallas_call | solution.py:177
  49.6 3.7 %second_sweep.1 = (f32[32,10,128]{2,1,0:T(8,128)}, f32[1,2048]{1,0:T(1,128)S(1)}) custom-call(s32[3]{0:T(128)S(1)} %pad_add_fusion.where_ref, bf16[1024,256]{1,0:T(8,128)(2,1)S(1)} %get-tuple-element.34.unit_ref.teacher_ref, bf16[256,4096]{1,0:T(8,128)(2,1)S(1)} %get-tuple-element.31.weights_ref, f32[32,10,128]{2,1,0:T(8,128)S(1)} %all-to-all-done.1.came_ref.first_ref, ...), custom_call_target="tpu_custom_call" | custom-call | flops 1073741824 | bytes 1572864 | tf_op jit(solution)/shard_map/second_sweep/pallas_call | solution.py:247
  53.3 2.6 %collective-permute-start.5 = (f32[1,2048]{1,0:T(1,128)S(1)}, f32[1,2048]{1,0:T(1,128)S(1)}, u32[]{:S(2)}, u32[]{:S(2)}) collective-permute-start(f32[1,2048]{1,0:T(1,128)S(1)} %get-tuple-element.49), channel_id=1, source_target_pairs={{0,16},{16,0},{1,17},{17,1},{2,18},{18,2},{3,19},{19,3},{4,20},{20... | collective-permute-start | bytes 24584 | tf_op jit(solution)/shard_map/ppermute | solution.py:722
  55.9 3.9 %all-to-all-start.2 = ((f32[32,10,128]{2,1,0:T(8,128)}), f32[32,10,128]{2,1,0:T(8,128)S(1)}, u32[]{:S(2)}, u32[]{:S(2)}) async-start(f32[32,10,128]{2,1,0:T(8,128)} %get-tuple-element.37), calls=%async_computation.2 | async-start | bytes 524288 | tf_op jit(solution)/shard_map/all_to_all | solution.py:646
  60.5 7.6 %pair.1 = (bf16[2,2,1024,256]{3,2,1,0:T(8,128)(2,1)}, bf16[2,2,256,1024]{3,2,1,0:T(8,128)(2,1)}, bf16[2,2,1024,256]{3,2,1,0:T(8,128)(2,1)}) custom-call(s32[3]{0:T(128)} %copy-done.2, bf16[4,2,256,256]{3,2,1,0:T(8,128)(2,1)} %bitcast.7.own_ref.own_raw_ref, bf16[4,2,256,256]{3,2,1,0:T(8,128)(2,1)} %collective-permute-done.4.other_ref.other_raw_ref, ...), custom_call_target="tpu_custom_call" | custom-call | flops 2147483648 | bytes 8388608 | tf_op jit(solution)/shard_map/pair/pallas_call | solution.py:301
  68.1 2.3 %all-to-all-done.2.second_ref = f32[32,10,128]{2,1,0:T(8,128)S(1)} async-done(((f32[32,10,128]{2,1,0:T(8,128)}), f32[32,10,128]{2,1,0:T(8,128)S(1)}, u32[]{:S(2)}, u32[]{:S(2)}) %all-to-all-start.2) | async-done | bytes 163872 | tf_op jit(solution)/shard_map/all_to_all | solution.py:646
  71.1 28.6 %near_gradients.1 = (f32[1024,256]{1,0:T(8,128)}, f32[1024,256]{1,0:T(8,128)}, f32[256,4096]{1,0:T(8,128)}) custom-call(s32[3]{0:T(128)} %copy-done.2, bf16[2,2,1024,256]{3,2,1,0:T(8,128)(2,1)} %get-tuple-element.45.unit_ref, bf16[2,2,256,1024]{3,2,1,0:T(8,128)(2,1)} %get-tuple-element.46.turned_ref, bf16[2,2,1024,256]{3,2,1,0:T(8,128)(2,1)} %get-tuple-element.47.paired_ref, ...), custom_call_target="tpu_custom_call" | custom-call | flops 17179869184 | bytes 8388608 | tf_op jit(solution)/shard_map/near_gradients/pallas_call | solution.py:465
  99.8 2.8 %collective-permute-done.6 = f32[1024,256]{1,0:T(8,128)S(1)} collective-permute-done((f32[1024,256]{1,0:T(8,128)}, f32[1024,256]{1,0:T(8,128)S(1)}, u32[]{:S(2)}, u32[]{:S(2)}) %collective-permute-start.6) | collective-permute-done | bytes 1048608 | tf_op jit(solution)/shard_map/ppermute | solution.py:642
  102.5 2.2 %multiply_convert_fusion = f16[1024,256]{1,0:T(8,128)(2,1)} fusion(f32[1024,256]{1,0:T(8,128)} %get-tuple-element.51, f32[1024,256]{1,0:T(8,128)S(1)} %collective-permute-done.6), kind=kLoop, calls=%fused_computation.2 | loop fusion | flops 786432 | bytes 2621440 | tf_op jit(solution)/shard_map/convert_element_type | solution.py:739
  104.7 3.7 %all-to-all-start.3 = ((f16[8,128,256]{2,1,0:T(8,128)(2,1)}), f16[8,128,256]{2,1,0:T(8,128)(2,1)S(1)}, u32[]{:S(2)}, u32[]{:S(2)}) async-start(f16[8,128,256]{2,1,0:T(8,128)(2,1)} %bitcast.8), calls=%async_computation.3 | async-start | bytes 1048576 | tf_op jit(solution)/shard_map/all_to_all | solution.py:646
  108.4 15.1 %far_gradients.2 = f32[128,2176]{1,0:T(8,128)} custom-call(s32[3]{0:T(128)} %copy-done.2, bf16[2,2,1024,256]{3,2,1,0:T(8,128)(2,1)} %get-tuple-element.45.unit_ref, bf16[2,2,256,1024]{3,2,1,0:T(8,128)(2,1)} %get-tuple-element.46.turned_ref, bf16[2,2,1024,256]{3,2,1,0:T(8,128)(2,1)} %get-tuple-element.47.paired_ref, f32[32,10,128]{2,1,0:T(8,128)} %copy-done.1, ...), custom_call_target="tpu_custom_call" | custom-call | flops 6442450944 | bytes 4194304 | tf_op jit(solution)/shard_map/far_gradients/pallas_call | solution.py:573
  123.5 2.1 %convert_element_type.24 = f16[128,2176]{1,0:T(8,128)(2,1)} convert(f32[128,2176]{1,0:T(8,128)} %far_gradients.2) | non-fusion elementwise | flops 278528 | bytes 1671168 | tf_op jit(solution)/shard_map/convert_element_type | solution.py:758
  125.7 15.2 %far_gradients.3 = f32[128,2176]{1,0:T(8,128)} custom-call(s32[3]{0:T(128)} %copy-done.2, bf16[2,2,1024,256]{3,2,1,0:T(8,128)(2,1)} %get-tuple-element.45.unit_ref, bf16[2,2,256,1024]{3,2,1,0:T(8,128)(2,1)} %get-tuple-element.46.turned_ref, bf16[2,2,1024,256]{3,2,1,0:T(8,128)(2,1)} %get-tuple-element.47.paired_ref, f32[32,10,128]{2,1,0:T(8,128)} %copy-done.1, ...), custom_call_target="tpu_custom_call" | custom-call | flops 6442450944 | bytes 4194304 | tf_op jit(solution)/shard_map/far_gradients/pallas_call | solution.py:573
  140.8 2.1 %convert_element_type.26 = f16[128,2176]{1,0:T(8,128)(2,1)} convert(f32[128,2176]{1,0:T(8,128)} %far_gradients.3) | non-fusion elementwise | flops 278528 | bytes 1671168 | tf_op jit(solution)/shard_map/convert_element_type | solution.py:758
  142.9 3.9 %all-to-all-start.5 = ((f16[8,16,2176]{2,1,0:T(8,128)(2,1)}), f16[8,16,2176]{2,1,0:T(8,128)(2,1)S(1)}, u32[]{:S(2)}, u32[]{:S(2)}) async-start(f16[8,16,2176]{2,1,0:T(8,128)(2,1)} %bitcast.10), calls=%async_computation.5 | async-start | bytes 1114112 | tf_op jit(solution)/shard_map/all_to_all | solution.py:646
  146.9 9.1 %all-to-all-done.5 = f16[8,16,2176]{2,1,0:T(8,128)(2,1)S(1)} async-done(((f16[8,16,2176]{2,1,0:T(8,128)(2,1)}), f16[8,16,2176]{2,1,0:T(8,128)(2,1)S(1)}, u32[]{:S(2)}, u32[]{:S(2)}) %all-to-all-start.5) | async-done | bytes 557088 | tf_op jit(solution)/shard_map/all_to_all | solution.py:646
  156.0 3.5 %all-to-all-start.4 = ((f16[8,16,2176]{2,1,0:T(8,128)(2,1)}), f16[8,16,2176]{2,1,0:T(8,128)(2,1)S(1)}, u32[]{:S(2)}, u32[]{:S(2)}) async-start(f16[8,16,2176]{2,1,0:T(8,128)(2,1)} %bitcast.9), calls=%async_computation.4 | async-start | bytes 1114112 | tf_op jit(solution)/shard_map/all_to_all | solution.py:646
  159.7 1.5 collective-permute-start.7
  161.2 4.4 %collective-permute-done.7 = f32[128,256]{1,0:T(8,128)S(1)} collective-permute-done((f32[128,256]{1,0:T(8,128)S(1)}, f32[128,256]{1,0:T(8,128)S(1)}, u32[]{:S(2)}, u32[]{:S(2)}) %collective-permute-start.7) | collective-permute-done | bytes 131104 | tf_op jit(solution)/shard_map/ppermute | solution.py:642
  166.5 2.2 %all-to-all-done.4 = f16[8,16,2176]{2,1,0:T(8,128)(2,1)S(1)} async-done(((f16[8,16,2176]{2,1,0:T(8,128)(2,1)}), f16[8,16,2176]{2,1,0:T(8,128)(2,1)S(1)}, u32[]{:S(2)}, u32[]{:S(2)}) %all-to-all-start.4) | async-done | bytes 557088 | tf_op jit(solution)/shard_map/all_to_all | solution.py:646
  168.8 1.9 %join.1 = f32[16,32768]{1,0:T(8,128)} custom-call(f32[8,16,2176]{2,1,0:T(8,128)S(1)} %convert_element_type.25.refs_0_, f32[8,16,2176]{2,1,0:T(8,128)S(1)} %convert_element_type.27.refs_1_), custom_call_target="tpu_custom_call" | custom-call | flops 524288 | bytes 4194304 | tf_op jit(solution)/shard_map/join/pallas_call | solution.py:625
  (44 shorter events, 5.4 us)
Async XLA Ops:
  0.6 10.6 %collective-permute-start.1 = (bf16[1,256,256]{2,1,0:T(8,128)(2,1)}, bf16[1,256,256]{2,1,0:T(8,128)(2,1)S(1)}, u32[]{:S(2)}, u32[]{:S(2)}) collective-permute-start(bf16[1,256,256]{2,1,0:T(8,128)(2,1)} %bitcast.11), channel_id=1, source_target_pairs={{0,16},{4,20},{8,24},{12,28},{16,0},{20,4},{24,8},{28,12},{1,17},{... | collective-permute-start | bytes 393224 | tf_op jit(solution)/shard_map/ppermute | solution.py:695
  4.8 44.8 %copy-start.2 = (s32[3]{0:T(128)}, s32[3]{0:T(128)S(1)}, u32[]{:S(2)}) copy-start(s32[3]{0:T(128)S(1)} %pad_add_fusion.where_ref) | copy-start | bytes 40
  4.8 6.4 %copy-start = (bf16[256,256]{1,0:T(8,128)(2,1)S(1)}, bf16[256,256]{1,0:T(8,128)(2,1)}, u32[]{:S(2)}) copy-start(bf16[256,256]{1,0:T(8,128)(2,1)} %students_ref.1) | copy-start | bytes 393220
  4.8 7.7 %copy-start.9 = (bf16[64,256]{1,0:T(8,128)(2,1)S(1)}, bf16[64,256]{1,0:T(8,128)(2,1)}, u32[]{:S(2)}) copy-start(bf16[64,256]{1,0:T(8,128)(2,1)} %param.5) | copy-start | bytes 98308
  10.2 0.6 copy-start.4
  10.8 38.8 %copy-start.3 = (bf16[256,4096]{1,0:T(8,128)(2,1)}, bf16[256,4096]{1,0:T(8,128)(2,1)S(1)}, u32[]{:S(2)}) copy-start(bf16[256,4096]{1,0:T(8,128)(2,1)S(1)} %get-tuple-element.31.weights_ref) | copy-start | bytes 6291460
  11.3 14.4 %collective-permute-start.2 = (bf16[2,256,256]{2,1,0:T(8,128)(2,1)S(1)}, bf16[2,256,256]{2,1,0:T(8,128)(2,1)S(1)}, u32[]{:S(2)}, u32[]{:S(2)}) collective-permute-start(bf16[2,256,256]{2,1,0:T(8,128)(2,1)S(1)} %pad_maximum_fusion.2), channel_id=1, source_target_pairs={{0,8},{4,12},{8,0},{12,4},{16,24},{20,28},{24,16},{28,20},{1,9},{5... | collective-permute-start | bytes 786440 | tf_op jit(solution)/shard_map/ppermute | solution.py:695
  13.2 15.4 %all-to-all-start = ((bf16[8,64,256]{2,1,0:T(8,128)(2,1)}), bf16[8,64,256]{2,1,0:T(8,128)(2,1)S(1)}, u32[]{:S(2)}, u32[]{:S(2)}) async-start(bf16[8,64,256]{2,1,0:T(8,128)(2,1)} %tile.2), calls=%async_computation | async-start | bytes 524288 | tf_op jit(solution)/shard_map/all_to_all | solution.py:646
  18.4 11.7 %copy-start.5 = (s32[256]{0:T(256)S(1)}, s32[256]{0:T(256)}, u32[]{:S(2)}) copy-start(s32[256]{0:T(256)} %param.8) | copy-start | bytes 3076
  18.4 11.7 %copy-start.6 = (s32[256]{0:T(256)S(1)}, s32[256]{0:T(256)}, u32[]{:S(2)}) copy-start(s32[256]{0:T(256)} %param.9) | copy-start | bytes 3076
  26.5 13.6 %collective-permute-start.3 = (bf16[4,256,256]{2,1,0:T(8,128)(2,1)}, bf16[4,256,256]{2,1,0:T(8,128)(2,1)}, u32[]{:S(2)}, u32[]{:S(2)}) collective-permute-start(bf16[4,256,256]{2,1,0:T(8,128)(2,1)} %pad_maximum_fusion.1), channel_id=1, source_target_pairs={{0,4},{4,0},{8,12},{12,8},{16,20},{20,16},{24,28},{28,24},{1,5},{5... | collective-permute-start | bytes 1572872 | tf_op jit(solution)/shard_map/ppermute | solution.py:695
  28.6 1.5 collective-permute-start
  33.9 15.7 %copy-start.7 = (bf16[1024,256]{1,0:T(8,128)(2,1)}, bf16[1024,256]{1,0:T(8,128)(2,1)S(1)}, u32[]{:S(2)}) copy-start(bf16[1024,256]{1,0:T(8,128)(2,1)S(1)} %get-tuple-element.34.unit_ref.teacher_ref) | copy-start | bytes 1572868
  33.9 15.6 %all-to-all-start.1 = ((f32[32,10,128]{2,1,0:T(8,128)}), f32[32,10,128]{2,1,0:T(8,128)S(1)}, u32[]{:S(2)}, u32[]{:S(2)}) async-start(f32[32,10,128]{2,1,0:T(8,128)} %get-tuple-element.35), calls=%async_computation.1 | async-start | bytes 524288 | tf_op jit(solution)/shard_map/all_to_all | solution.py:646
  42.3 18.2 %collective-permute-start.4 = (bf16[4,2,256,256]{3,2,1,0:T(8,128)(2,1)}, bf16[4,2,256,256]{3,2,1,0:T(8,128)(2,1)}, u32[]{:S(2)}, u32[]{:S(2)}) collective-permute-start(bf16[4,2,256,256]{3,2,1,0:T(8,128)(2,1)} %bitcast.7.own_ref.own_raw_ref), channel_id=1, source_target_pairs={{0,2},{2,0},{1,3},{3,1},{4,6},{6,4},{5,7},{7,5},{8,10},{10,8},{9,1... | collective-permute-start | bytes 3145736 | tf_op jit(solution)/shard_map/ppermute | solution.py:642
  49.6 6.3 %copy-start.1 = (f32[32,10,128]{2,1,0:T(8,128)}, f32[32,10,128]{2,1,0:T(8,128)S(1)}, u32[]{:S(2)}) copy-start(f32[32,10,128]{2,1,0:T(8,128)S(1)} %all-to-all-done.1.came_ref.first_ref) | copy-start | bytes 491524
  53.3 6.6 %collective-permute-start.5 = (f32[1,2048]{1,0:T(1,128)S(1)}, f32[1,2048]{1,0:T(1,128)S(1)}, u32[]{:S(2)}, u32[]{:S(2)}) collective-permute-start(f32[1,2048]{1,0:T(1,128)S(1)} %get-tuple-element.49), channel_id=1, source_target_pairs={{0,16},{16,0},{1,17},{17,1},{2,18},{18,2},{3,19},{19,3},{4,20},{20... | collective-permute-start | bytes 24584 | tf_op jit(solution)/shard_map/ppermute | solution.py:722
  55.9 14.5 %all-to-all-start.2 = ((f32[32,10,128]{2,1,0:T(8,128)}), f32[32,10,128]{2,1,0:T(8,128)S(1)}, u32[]{:S(2)}, u32[]{:S(2)}) async-start(f32[32,10,128]{2,1,0:T(8,128)} %get-tuple-element.37), calls=%async_computation.2 | async-start | bytes 524288 | tf_op jit(solution)/shard_map/all_to_all | solution.py:646
  70.4 0.7 copy-start.8
  99.7 2.9 %collective-permute-start.6 = (f32[1024,256]{1,0:T(8,128)}, f32[1024,256]{1,0:T(8,128)S(1)}, u32[]{:S(2)}, u32[]{:S(2)}) collective-permute-start(f32[1024,256]{1,0:T(8,128)} %get-tuple-element.52), channel_id=1, source_target_pairs={{0,2},{2,0},{1,3},{3,1},{4,6},{6,4},{5,7},{7,5},{8,10},{10,8},{9,1... | collective-permute-start | bytes 3145736 | tf_op jit(solution)/shard_map/ppermute | solution.py:642
  104.7 20.9 %all-to-all-start.3 = ((f16[8,128,256]{2,1,0:T(8,128)(2,1)}), f16[8,128,256]{2,1,0:T(8,128)(2,1)S(1)}, u32[]{:S(2)}, u32[]{:S(2)}) async-start(f16[8,128,256]{2,1,0:T(8,128)(2,1)} %bitcast.8), calls=%async_computation.3 | async-start | bytes 1048576 | tf_op jit(solution)/shard_map/all_to_all | solution.py:646
  142.9 13.1 %all-to-all-start.5 = ((f16[8,16,2176]{2,1,0:T(8,128)(2,1)}), f16[8,16,2176]{2,1,0:T(8,128)(2,1)S(1)}, u32[]{:S(2)}, u32[]{:S(2)}) async-start(f16[8,16,2176]{2,1,0:T(8,128)(2,1)} %bitcast.10), calls=%async_computation.5 | async-start | bytes 1114112 | tf_op jit(solution)/shard_map/all_to_all | solution.py:646
  156.0 12.7 %all-to-all-start.4 = ((f16[8,16,2176]{2,1,0:T(8,128)(2,1)}), f16[8,16,2176]{2,1,0:T(8,128)(2,1)S(1)}, u32[]{:S(2)}, u32[]{:S(2)}) async-start(f16[8,16,2176]{2,1,0:T(8,128)(2,1)} %bitcast.9), calls=%async_computation.4 | async-start | bytes 1114112 | tf_op jit(solution)/shard_map/all_to_all | solution.py:646
  159.7 5.9 %collective-permute-start.7 = (f32[128,256]{1,0:T(8,128)S(1)}, f32[128,256]{1,0:T(8,128)S(1)}, u32[]{:S(2)}, u32[]{:S(2)}) collective-permute-start(f32[128,256]{1,0:T(8,128)S(1)} %broadcast_multiply_fusion), channel_id=1, source_target_pairs={{0,1},{1,0},{2,3},{3,2},{4,5},{5,4},{6,7},{7,6},{8,9},{9,8},{10,11... | collective-permute-start | bytes 393224 | tf_op jit(solution)/shard_map/ppermute | solution.py:642

commit v3 on v2

--- a/solution.py
+++ b/solution.py
@@ -21,9 +21,9 @@
 F16 = jnp.float16
 
 
-def params(limit):
+def params(limit, grid=1):
     return pltpu.CompilerParams(
-        vmem_limit_bytes=limit * MIB, dimension_semantics=("arbitrary",)
+        vmem_limit_bytes=limit * MIB, dimension_semantics=("arbitrary",) * grid
     )
 
 
@@ -207,8 +207,9 @@
 
 
 def first_sweep_kernel(
-    where_ref, own_ref, other_ref, weights_ref, pairing_ref, layout_ref, parcel_ref, unit_ref, *, plan, sub
+    where_ref, own_ref, other_ref, weights_ref, pairing_ref, layout_ref, parcel_ref, unit_ref, mark_ref, *, plan, sub
 ):
+    mark_ref[...] = jnp.zeros_like(mark_ref)
     half = own_ref.shape[0]
     unit_ref[:half, :] = unit_rows(own_ref[...]).astype(BF16)
     unit_ref[half:, :] = unit_rows(other_ref[...]).astype(BF16)
@@ -266,7 +267,8 @@
     )(where, *operands)
 
 
-def pair_kernel(where_ref, own_ref, other_ref, came_ref, teacher_ref, unit_ref, turned_ref, paired_ref, *, plan):
+def pair_kernel(where_ref, own_ref, other_ref, came_ref, teacher_ref, unit_ref, turned_ref, paired_ref, mark_ref, *, plan):
+    mark_ref[...] = jnp.zeros_like(mark_ref)
     where = (where_ref[0], where_ref[1], where_ref[2])
     apart = plan.halves - 1 - pl.program_id(0)
     teachers = teacher_ref.shape[0]
@@ -304,6 +306,7 @@
             jax.ShapeDtypeStruct((plan.halves, 2, plan.block, width), BF16),
             jax.ShapeDtypeStruct((plan.halves, 2, width, plan.block), BF16),
             jax.ShapeDtypeStruct((plan.halves, 2, plan.block, width), BF16),
+            jax.ShapeDtypeStruct((8, LANES), F32),
         ],
         grid_spec=pltpu.PrefetchScalarGridSpec(
             num_scalar_prefetch=1,
@@ -318,9 +321,10 @@
                 rows,
                 pl.BlockSpec((1, 2, width, plan.block), lambda g, w: (g, 0, 0, 0)),
                 rows,
-            ],
-        ),
-        compiler_params=params(56),
+                pl.BlockSpec((8, LANES), lambda g, w: (0, 0)),
+            ],
+        ),
+        compiler_params=params(50),
         cost_estimate=pl.CostEstimate(
             flops=4 * plan.halves * plan.block * width * teachers.shape[0],
             bytes_accessed=16 * plan.halves * plan.block * width,
@@ -352,7 +356,7 @@
 
 def gradient_products(
     unit_ref, turned_ref, paired_ref, factor_ref, weights_ref, flipped_ref, shares_ref, scale,
-    grads, sub, fresh,
+    grads, sub, earlier,
 ):
     columns = weights_ref.shape[1]
     tile = tile_of(columns, 4 * sub)
@@ -379,14 +383,14 @@
                 share = dot(grad, flipped_ref[span, :])
                 shares = share if shares is None else shares + share
             share = dot(turned_ref[0, 0], grad)
-            grads[:, span] = jnp.where(fresh, 0.0, grads[:, span]) + share
+            grads[:, span] = earlier(span) + share
         return shares
 
     @pl.loop(0, columns // tile)
     def _(step):
         shares = products(step, None)
         if shares_ref is not None:
-            shares_ref[...] = jnp.where(step == 0, 0.0, shares_ref[...]) + shares
+            shares_ref[...] += shares
 
 
 def near_kernel(
@@ -412,19 +416,23 @@
     sub,
 ):
     where = (where_ref[0], where_ref[1], where_ref[2])
-    side = pl.program_id(0)
+    part, side = pl.program_id(0), pl.program_id(1)
     count = plan.stu_count
 
-    @pl.when(side == 0)
+    @pl.when((part == 0) & (side == 0))
     def _():
         row_factor[...] = as_columns(
             (loss_scale / student_temp) / plan.teacher_totals(where, second_ref)
         )
 
-    fill_scale(plan, where, 0, side, first_ref, second_ref, row_factor, scale)
+    @pl.when(part == 0)
+    def _():
+        fill_scale(plan, where, 0, side, first_ref, second_ref, row_factor, scale.at[side])
+        shares[side] = jnp.zeros(shares.shape[1:], F32)
+
     gradient_products(
-        unit_ref, turned_ref, paired_ref, factor_ref, weights_ref, flipped_ref, shares, scale,
-        grads_ref, sub, side == 0,
+        unit_ref, turned_ref, paired_ref, factor_ref, weights_ref, flipped_ref, shares.at[side],
+        scale.at[side], grads_ref, sub, lambda span: jnp.where(side == 0, 0.0, grads_ref[:, span]),
     )
 
     def finish(raw_ref, out_ref):
@@ -432,62 +440,68 @@
             rows = slice(place * count, (place + 1) * count)
             chip = where[1] ^ reverse_bits(place, plan.chips)
             unit = unit_rows(raw_ref[place, 0])
-            share = shares[rows]
+            share = shares[side, rows, :]
             share = share - unit * jnp.sum(unit * share, 1, keepdims=True)
             out_ref[pl.ds(pl.multiple_of(chip * count, count), count), :] = share
 
-    @pl.when(side == 0)
+    @pl.when((part == pl.num_programs(0) - 1) & (side == 0))
     def _():
         finish(own_raw_ref, own_ref)
 
-    @pl.when(side == 1)
+    @pl.when((part == pl.num_programs(0) - 1) & (side == 1))
     def _():
         finish(other_raw_ref, other_ref)
 
 
 def whole_spec(array):
     return pl.BlockSpec(
-        array.shape, lambda p, w: (0,) * array.ndim, pipeline_mode=pl.Buffered(1)
-    )
+        array.shape, lambda q, p, w: (0,) * array.ndim, pipeline_mode=pl.Buffered(1)
+    )
+
+
+def parts_of(columns):
+    return 2 if columns % (2 * LANES) == 0 else 1
 
 
 def near_gradients(plan, where, unit, turned, paired, first, second, factor, weights, flipped, own, other):
     width, columns = weights.shape
+    parts = parts_of(columns)
+    each = columns // parts
     last = plan.halves - 1
-    rows = pl.BlockSpec((1, 1, plan.block, width), lambda p, w: (last, p, 0, 0))
+    rows = pl.BlockSpec((1, 1, plan.block, width), lambda q, p, w: (last, p, 0, 0))
+    across = pl.BlockSpec((width, each), lambda q, p, w: (0, q))
     raw = pl.BlockSpec(
         (plan.chips, 1, plan.stu_count, width),
-        lambda p, w: (0, 0, 0, 0),
+        lambda q, p, w: (0, 0, 0, 0),
         pipeline_mode=pl.Buffered(1),
     )
     students = jax.ShapeDtypeStruct((plan.block, width), F32)
-    out_shape = [students, students, jax.ShapeDtypeStruct((width, columns), F32)]
     return pl.pallas_call(
-        functools.partial(near_kernel, plan=plan, sub=tile_of(columns, 256)),
-        out_shape=out_shape,
+        functools.partial(near_kernel, plan=plan, sub=tile_of(each, 256)),
+        out_shape=[students, students, jax.ShapeDtypeStruct((width, columns), F32)],
         grid_spec=pltpu.PrefetchScalarGridSpec(
             num_scalar_prefetch=1,
-            grid=(2,),
+            grid=(parts, 2),
             in_specs=[
                 rows,
-                pl.BlockSpec((1, 1, width, plan.block), lambda p, w: (last, p, 0, 0)),
+                pl.BlockSpec((1, 1, width, plan.block), lambda q, p, w: (last, p, 0, 0)),
                 rows,
                 whole_spec(first),
                 whole_spec(second),
-                whole_spec(factor),
-                whole_spec(weights),
-                whole_spec(flipped),
+                pl.BlockSpec((1, each), lambda q, p, w: (0, q)),
+                across,
+                pl.BlockSpec((each, width), lambda q, p, w: (q, 0)),
                 raw,
                 raw,
             ],
-            out_specs=[whole_spec(o) for o in out_shape],
+            out_specs=[whole_spec(students), whole_spec(students), across],
             scratch_shapes=[
-                pltpu.VMEM((2, plan.block, LANES), F32),
-                pltpu.VMEM((plan.block, width), F32),
+                pltpu.VMEM((2, 2, plan.block, LANES), F32),
+                pltpu.VMEM((2, plan.block, width), F32),
                 pltpu.VMEM((plan.tea_lanes * LANES, LANES), F32),
             ],
         ),
-        compiler_params=params(56),
+        compiler_params=params(50, 2),
         cost_estimate=pl.CostEstimate(
             flops=16 * plan.block * width * columns,
             bytes_accessed=8 * width * columns,
@@ -518,25 +532,28 @@
     sub,
 ):
     where = (where_ref[0], where_ref[1], where_ref[2])
-    block = pl.program_id(0)
+    part, block = pl.program_id(0), pl.program_id(1)
     columns = weights_ref.shape[1]
 
-    @pl.when(block == 0)
+    @pl.when((part == 0) & (block == 0))
     def _():
         row_factor[...] = as_columns(
             (loss_scale / student_temp) / plan.teacher_totals(where, second_ref)
         )
-        grads[...] = before_ref[...]
-
-    fill_scale(
-        plan, where, plan.halves - 1 - block // 2, block % 2, first_ref, second_ref, row_factor, scale
-    )
+
+    @pl.when(part == 0)
+    def _():
+        apart = plan.halves - 1 - block // 2
+        fill_scale(
+            plan, where, apart, block % 2, first_ref, second_ref, row_factor, scale.at[block]
+        )
+
     gradient_products(
-        unit_ref, turned_ref, paired_ref, factor_ref, weights_ref, None, None, scale, grads, sub,
-        False,
-    )
-
-    @pl.when(block == pl.num_programs(0) - 1)
+        unit_ref, turned_ref, paired_ref, factor_ref, weights_ref, None, None, scale.at[block],
+        grads, sub, lambda span: jnp.where(block == 0, before_ref[:, span], grads[:, span]),
+    )
+
+    @pl.when(block == pl.num_programs(1) - 1)
     def _():
         kept = grads.shape[0] // plan.halves
         mine = pl.ds(pl.multiple_of(where[0] * kept, kept), kept)
@@ -562,40 +579,42 @@
 
 
 def far_gradients(
-    plan, where, part, unit, turned, paired, first, second, factor, weights, raw, norm, before
+    plan, where, unit, turned, paired, first, second, factor, weights, raw, norm, before
 ):
-    width = weights.shape[0]
-    parts = plan.halves
-    columns = weights.shape[1] // parts
-    rows = pl.BlockSpec((1, 1, plan.block, width), lambda p, w: (p // 2, p % 2, 0, 0))
-    span = lambda p, w: (0, part)
+    width, columns = weights.shape
+    parts = parts_of(columns)
+    each = columns // parts
+    blocks = 2 * (plan.halves - 1)
     kept = width // plan.halves
+    rows = pl.BlockSpec((1, 1, plan.block, width), lambda q, p, w: (p // 2, p % 2, 0, 0))
+    across = pl.BlockSpec((width, each), lambda q, p, w: (0, q))
+    thin = pl.BlockSpec((1, each), lambda q, p, w: (0, q))
     return pl.pallas_call(
-        functools.partial(far_kernel, plan=plan, sub=tile_of(columns, 256)),
-        out_shape=jax.ShapeDtypeStruct((kept, columns + LANES), F32),
+        functools.partial(far_kernel, plan=plan, sub=tile_of(each, 256)),
+        out_shape=jax.ShapeDtypeStruct((kept, parts * (each + LANES)), F32),
         grid_spec=pltpu.PrefetchScalarGridSpec(
             num_scalar_prefetch=1,
-            grid=(2 * (plan.halves - 1),),
+            grid=(parts, blocks),
             in_specs=[
                 rows,
-                pl.BlockSpec((1, 1, width, plan.block), lambda p, w: (p // 2, p % 2, 0, 0)),
+                pl.BlockSpec((1, 1, width, plan.block), lambda q, p, w: (p // 2, p % 2, 0, 0)),
                 rows,
                 whole_spec(first),
                 whole_spec(second),
-                pl.BlockSpec((1, columns), span),
-                pl.BlockSpec((width, columns), span),
-                pl.BlockSpec((width, columns), span),
-                pl.BlockSpec((1, columns), span),
-                pl.BlockSpec((width, columns), span),
-            ],
-            out_specs=pl.BlockSpec((kept, columns + LANES), lambda p, w: (0, 0)),
+                thin,
+                across,
+                across,
+                thin,
+                across,
+            ],
+            out_specs=pl.BlockSpec((kept, each + LANES), lambda q, p, w: (0, q)),
             scratch_shapes=[
-                pltpu.VMEM((2, plan.block, LANES), F32),
-                pltpu.VMEM((width, columns), F32),
+                pltpu.VMEM((blocks, 2, plan.block, LANES), F32),
+                pltpu.VMEM((width, each), F32),
                 pltpu.VMEM((plan.tea_lanes * LANES, LANES), F32),
             ],
         ),
-        compiler_params=params(56),
+        compiler_params=params(56, 2),
         cost_estimate=pl.CostEstimate(
             flops=12 * (plan.halves - 1) * plan.block * width * columns,
             bytes_accessed=8 * width * columns,
@@ -605,28 +624,27 @@
     )(where, unit, turned, paired, first, second, factor, weights, raw, norm, before)
 
 
-def join_kernel(*refs):
-    out_ref = refs[-1]
-    count, _, length = refs[0].shape
-    columns = length - LANES
-    start = 0
-    for sender in range(count):
-        for ref in refs[:-1]:
-            factor = jnp.exp2(ref[sender, :, columns:])
-            out_ref[:, start : start + columns] = ref[sender, :, :columns] * widen(factor, columns)
-            start += columns
-
-
-def join(pieces):
-    senders, share, length = pieces[0].shape
-    columns = (length - LANES) * len(pieces)
+def join_kernel(came_ref, out_ref, *, parts):
+    count, _, length = came_ref.shape
+    step = length // parts
+    columns = step - LANES
+    for number in range(count * parts):
+        sender, start = number // parts, number % parts * step
+        factor = jnp.exp2(came_ref[sender, :, start + columns : start + step])
+        out_ref[:, number * columns : (number + 1) * columns] = came_ref[
+            sender, :, start : start + columns
+        ] * widen(factor, columns)
+
+
+def join(came, parts):
+    senders, share, length = came.shape
+    columns = length - parts * LANES
     each = tile_of(senders, 2)
-    spec = pl.BlockSpec((each, share, length), lambda i: (i, 0, 0))
     return pl.pallas_call(
-        join_kernel,
+        functools.partial(join_kernel, parts=parts),
         out_shape=jax.ShapeDtypeStruct((share, senders * columns), F32),
         grid=(senders // each,),
-        in_specs=[spec] * len(pieces),
+        in_specs=[pl.BlockSpec((each, share, length), lambda i: (i, 0, 0))],
         out_specs=pl.BlockSpec((share, each * columns), lambda i: (0, i)),
         compiler_params=params(16),
         cost_estimate=pl.CostEstimate(
@@ -635,7 +653,7 @@
             transcendentals=0,
         ),
         name="join",
-    )(*pieces)
+    )(came)
 
 
 def swap(value, axis):
@@ -669,26 +687,26 @@
 
     tea_own = gather(teacher, ("half", "chip"), all_chips)
     weights, flipped, norm, raw = unit_columns(where, prototypes, columns)
-    near_total = local_denominator(tie(students, weights), prototypes, 0, 2)
-    tea_own = tie(tea_own, near_total)
+    near_total = local_denominator(tie(students, norm), prototypes, 0, 2)
     tea_other = swap(tea_own, "core")
-    parcel_one, tea_unit = sweep_call(
+    parcel_one, tea_unit, mark = sweep_call(
         first_sweep_kernel,
         plan,
-        where,
+        tie(where, near_total),
         [tea_own, tea_other, weights, pairing.reshape(1, -1), layout.reshape(1, -1)],
         2,
         part_columns,
         [
             parcel(plan.tea_lanes + plan.stu_lanes),
             jax.ShapeDtypeStruct((2 * plan.tea_rows, width), BF16),
+            jax.ShapeDtypeStruct((8, LANES), F32),
         ],
         "first_sweep",
     )
     first = exchange(parcel_one, everyone)
-    far_total = local_denominator(tie(students, tea_unit), prototypes, 1, 2)
-
-    markers = [weights, near_total, parcel_one]
+    far_total = local_denominator(tie(students, mark), prototypes, 1, 2)
+
+    markers = [norm, near_total, mark]
     gathered = students[None]
     bit = all_chips // 2
     while bit:
@@ -716,6 +734,10 @@
         "second_sweep",
     )
     second = exchange(parcel_two, everyone)
+    unit, turned, paired, _ = pair(
+        plan, where, stu_own, stu_other, tie(first, parcel_two), tea_unit
+    )
+    second, unit, turned, paired = lax.optimization_barrier((second, unit, turned, paired))
     factors = [factor]
     for step in range(1, halves):
         factors.append(
@@ -726,10 +748,6 @@
     elif halves > 2:
         factors = [jnp.stack(factors)[(half - step) % halves] for step in range(halves)]
     factor = jnp.concatenate(factors, 1)
-    unit, turned, paired = pair(
-        plan, where, stu_own, stu_other, tie(first, parcel_two), tea_unit
-    )
-    second, unit, turned, paired = lax.optimization_barrier((second, unit, turned, paired))
 
     rows_of = (unit, turned, paired, first, second, factor, weights)
     own_part, other_part, proto_all = near_gradients(
@@ -738,6 +756,11 @@
     summed = (own_part + swap(other_part, "core")) * 128.0
     sent = summed.astype(F16).reshape(chips * protos, stu_count // protos, width)
     came = exchange(sent, ("chip", "protos"))
+    proto_part = far_gradients(plan, tie(where, sent), *rows_of, raw, norm, proto_all)
+    share = width // (all_chips * 2)
+    sent = proto_part.astype(F16).reshape(chips * 2, share, -1)
+    grad_protos = join(exchange(sent, ("chip", "core")).astype(F32), parts_of(columns))
+
     rows = jnp.sum(came.astype(F32), 0) * (1.0 / 128.0)
     if protos == 2:
         far = swap(rows, "protos")
@@ -748,18 +771,7 @@
         grad_unit = gather(rows, "protos", protos)
     stu_full = students.astype(F32)
     u_norm = jnp.sqrt(jnp.sum(stu_full * stu_full, 1, keepdims=True) + epsilon)
-    grad_students = grad_unit / u_norm
-
-    share = width // (all_chips * 2)
-    pieces = []
-    proto_all = tie(proto_all, sent)
-    for part in range(halves):
-        proto_part = far_gradients(plan, where, part, *rows_of, raw, norm, proto_all)
-        sent = proto_part.astype(F16).reshape(chips * 2, share, part_columns + LANES)
-        sent = tie(sent, came)
-        proto_all = tie(proto_all, sent)
-        pieces.append(exchange(sent, ("chip", "core")).astype(F32))
-    return (grad_students, join(pieces))
+    return (grad_unit / u_norm, grad_protos)
 
 
 def solution(mesh):

time: 172 us -> 155 us (0.901)
  Pallas kernels: 95.6 us -> 89.1 us
  starting transfers between devices: 36.5 us -> 30.3 us
  other arithmetic: 11.3 us -> 5.17 us
  local copies, waits for them, and re-layouts: 2.06 us -> 5.41 us
    all_to_all x6 -> x5, starting transfers between devices: 24.9 us -> 19.5 us  [exchange(): return lax.all_to_all(value, axes, split_axis=0, concat_axis=0, tiled=True)]
    pallas_call x4 -> x3, Pallas kernels: 60.7 us -> 55.4 us  [the longest x1 27.6 us: near_gradients(): pl.pallas_call(functools.partial(near_kernel, plan=plan, sub=tile_of(each...]
    unnamed x20 -> x26, local copies, waits for them, and re-layouts: 1.34 us -> 4.69 us
    concatenate x3, other arithmetic: 3.05 us -> 0.19 us  [body(): gathered = jnp.concatenate([gathered, came], 0)]
    ppermute x3, waiting for transfers between devices: 2.11 us -> 0.01 us  [body(): lax.ppermute(gathered, ('half', 'chip'), [(q, q ^ bit) for q in range(all...]
    convert_element_type x4 -> x2, other arithmetic: 4.4 us -> 2.87 us  [the longest x1 2.73 us: body(): sent = proto_part.astype(F16).reshape(chips * 2, share, -1)]
    all_to_all x6 -> x5, waiting for transfers between devices: 13.6 us -> 14.8 us  [exchange(): return lax.all_to_all(value, axes, split_axis=0, concat_axis=0, tiled=True)]
  transfers between devices with their start and end apart: 14 -> 13, of which waited for: 8 -> 7; matrix products, arithmetic and copies ran while one was open for 5% -> 3% of each run, Pallas kernels for 29% -> 39%
where the time goes in v3:
time: 155 us
  Pallas kernels  89.1 us (57%)
  starting transfers between devices  30.3 us (20%)
  waiting for transfers between devices  23.8 us (15%)
  local copies, waits for them, and re-layouts  5.41 us (3%)
  other arithmetic  5.17 us (3%)
    pallas_call x1, Pallas kernels, near_gradients(): pl.pallas_call(functools.partial(near_kernel, plan=plan, sub=tile_of(each...  27.6 us
    pallas_call x1, Pallas kernels, far_gradients(): pl.pallas_call(functools.partial(far_kernel, plan=plan, sub=tile_of(each,...  25.9 us
    all_to_all x5, starting transfers between devices, exchange(): return lax.all_to_all(value, axes, split_axis=0, concat_axis=0, tiled=True)  19.5 us
    all_to_all x5, waiting for transfers between devices, exchange(): return lax.all_to_all(value, axes, split_axis=0, concat_axis=0, tiled=True)  14.8 us
    pallas_call x2, Pallas kernels, local_denominator(): pl.pallas_call(functools.partial(denominator_kernel, sub=tile_of(tile, 51...  14.5 us
    ppermute x4, waiting for transfers between devices, swap(): return lax.ppermute(value, axis, [(0, 1), (1, 0)])  8.52 us
    ppermute x3, starting transfers between devices, body(): lax.ppermute(gathered, ('half', 'chip'), [(q, q ^ bit) for q in range(all...  7.83 us
    pallas_call x2, Pallas kernels, sweep_call(): pl.pallas_call(functools.partial(kernel, plan=plan, sub=tile_of(columns,...  7.44 us
  transfers between devices with their start and end apart: 13, of which 7 were waited for; matrix products, arithmetic and copies ran while one was open for 3% of the time, Pallas kernels for 39%

profile of v3, /device:TPU:0, one launch (start us, length us, event | category | flops | bytes accessed | tf_op | source)
XLA Modules:
  0.0 154.6 jit_solution(15573213851587564391)
XLA Ops:
  0.6 4.1 %collective-permute-start.1 = (bf16[1,256,256]{2,1,0:T(8,128)(2,1)}, bf16[1,256,256]{2,1,0:T(8,128)(2,1)S(1)}, u32[]{:S(2)}, u32[]{:S(2)}) collective-permute-start(bf16[1,256,256]{2,1,0:T(8,128)(2,1)} %bitcast.10), channel_id=1, source_target_pairs={{0,16},{4,20},{8,24},{12,28},{16,0},{20,4},{24,8},{28,12},{1,17},{... | collective-permute-start | bytes 393224 | tf_op jit(solution)/shard_map/ppermute | solution.py:713
  4.8 5.5 %unit_columns.1 = (bf16[256,4096]{1,0:T(8,128)(2,1)S(1)}, bf16[4096,256]{1,0:T(8,128)(2,1)}, f32[1,4096]{1,0:T(1,128)S(1)}, bf16[256,4096]{1,0:T(8,128)(2,1)}) custom-call(s32[3]{0:T(128)S(1)} %pad_add_fusion.where_ref, bf16[256,32768]{1,0:T(8,128)(2,1)} %weights_ref.3), custom_call_target="tpu_custom_call" | custom-call | flops 8388608 | bytes 6291456 | tf_op jit(solution)/shard_map/unit_columns/pallas_call | solution.py:119
  10.3 1.4 copy-done.5
  11.7 1.6 %collective-permute-start.2 = (bf16[2,256,256]{2,1,0:T(8,128)(2,1)S(1)}, bf16[2,256,256]{2,1,0:T(8,128)(2,1)S(1)}, u32[]{:S(2)}, u32[]{:S(2)}) collective-permute-start(bf16[2,256,256]{2,1,0:T(8,128)(2,1)S(1)} %pad_maximum_fusion.2), channel_id=1, source_target_pairs={{0,8},{4,12},{8,0},{12,4},{16,24},{20,28},{24,16},{28,20},{1,9},{5... | collective-permute-start | bytes 786440 | tf_op jit(solution)/shard_map/ppermute | solution.py:713
  13.4 0.7 tile.2
  14.1 4.3 %all-to-all-start = ((bf16[8,64,256]{2,1,0:T(8,128)(2,1)}), bf16[8,64,256]{2,1,0:T(8,128)(2,1)S(1)}, u32[]{:S(2)}, u32[]{:S(2)}) async-start(bf16[8,64,256]{2,1,0:T(8,128)(2,1)} %tile.2), calls=%async_computation | async-start | bytes 524288 | tf_op jit(solution)/shard_map/all_to_all | solution.py:664
  18.4 7.2 %denominator.2.near_ref = f32[2,128]{1,0:T(2,128)S(1)} custom-call(bf16[256,256]{1,0:T(8,128)(2,1)S(1)} %copy-done, bf16[256,32768]{1,0:T(8,128)(2,1)} %weights_ref.3), custom_call_target="tpu_custom_call" | custom-call | flops 2147483648 | bytes 8388608 | tf_op jit(solution)/shard_map/denominator/pallas_call | solution.py:177
  25.7 2.1 %collective-permute-start.3 = (bf16[4,256,256]{2,1,0:T(8,128)(2,1)S(1)}, bf16[4,256,256]{2,1,0:T(8,128)(2,1)S(1)}, u32[]{:S(2)}, u32[]{:S(2)}) collective-permute-start(bf16[4,256,256]{2,1,0:T(8,128)(2,1)S(1)} %pad_maximum_fusion.1), channel_id=1, source_target_pairs={{0,4},{4,0},{8,12},{12,8},{16,20},{20,16},{24,28},{28,24},{1,5},{5... | collective-permute-start | bytes 1572872 | tf_op jit(solution)/shard_map/ppermute | solution.py:713
  27.8 1.5 collective-permute-done.other_ref
  29.4 1.6 %copy-done.6 = bf16[256,4096]{1,0:T(8,128)(2,1)S(1)} copy-done((bf16[256,4096]{1,0:T(8,128)(2,1)S(1)}, bf16[256,4096]{1,0:T(8,128)(2,1)}, u32[]{:S(2)}) %copy-start.6) | copy-done | bytes 2097176
  31.0 3.8 %first_sweep.1 = (f32[32,10,128]{2,1,0:T(8,128)}, bf16[1024,256]{1,0:T(8,128)(2,1)S(1)}, f32[8,128]{1,0:T(8,128)}) custom-call(s32[3]{0:T(128)S(1)} %pad_add_fusion.where_ref, bf16[512,256]{1,0:T(8,128)(2,1)S(1)} %bitcast.18, bf16[512,256]{1,0:T(8,128)(2,1)S(1)} %collective-permute-done.other_ref, bf16[256,4096]{1,0:T(8,128)(2,1)S(1)} %copy-done.6, ...), custom_call_target="tpu_custom_call" | custom-call | flops 1073741824 | bytes 1572864 | tf_op jit(solution)/shard_map/first_sweep/pallas_call | solution.py:248
  34.8 4.6 %all-to-all-start.1 = ((f32[32,10,128]{2,1,0:T(8,128)}), f32[32,10,128]{2,1,0:T(8,128)S(1)}, u32[]{:S(2)}, u32[]{:S(2)}) async-start(f32[32,10,128]{2,1,0:T(8,128)} %get-tuple-element.34), calls=%async_computation.1 | async-start | bytes 524288 | tf_op jit(solution)/shard_map/all_to_all | solution.py:664
  39.8 7.2 %denominator.3.far_ref = f32[2,128]{1,0:T(2,128)S(1)} custom-call(bf16[256,256]{1,0:T(8,128)(2,1)S(1)} %copy-done, bf16[256,32768]{1,0:T(8,128)(2,1)} %weights_ref.3), custom_call_target="tpu_custom_call" | custom-call | flops 2147483648 | bytes 8388608 | tf_op jit(solution)/shard_map/denominator/pallas_call | solution.py:177
  47.0 3.0 %all-to-all-done.1.came_ref.first_ref = f32[32,10,128]{2,1,0:T(8,128)S(1)} async-done(((f32[32,10,128]{2,1,0:T(8,128)}), f32[32,10,128]{2,1,0:T(8,128)S(1)}, u32[]{:S(2)}, u32[]{:S(2)}) %all-to-all-start.1) | async-done | bytes 163872 | tf_op jit(solution)/shard_map/all_to_all | solution.py:664
  50.1 1.7 %copy-done.7 = bf16[256,4096]{1,0:T(8,128)(2,1)S(1)} copy-done((bf16[256,4096]{1,0:T(8,128)(2,1)S(1)}, bf16[256,4096]{1,0:T(8,128)(2,1)}, u32[]{:S(2)}) %copy-start.7) | copy-done | bytes 2097176
  51.7 3.6 %second_sweep.1 = (f32[32,10,128]{2,1,0:T(8,128)}, f32[1,2048]{1,0:T(1,128)S(1)}) custom-call(s32[3]{0:T(128)S(1)} %pad_add_fusion.where_ref, bf16[1024,256]{1,0:T(8,128)(2,1)S(1)} %get-tuple-element.33.unit_ref.teacher_ref, bf16[256,4096]{1,0:T(8,128)(2,1)S(1)} %copy-done.7, f32[32,10,128]{2,1,0:T(8,128)S(1)} %all-to-all-done.1.came_ref.first_ref, ...), custom_call_target="tpu_custom_call" | custom-call | flops 1073741824 | bytes 1572864 | tf_op jit(solution)/shard_map/second_sweep/pallas_call | solution.py:248
  55.4 1.0 collective-permute-start.5
  56.3 3.0 %all-to-all-start.2 = ((f32[32,10,128]{2,1,0:T(8,128)}), f32[32,10,128]{2,1,0:T(8,128)S(1)}, u32[]{:S(2)}, u32[]{:S(2)}) async-start(f32[32,10,128]{2,1,0:T(8,128)} %get-tuple-element.37), calls=%async_computation.2 | async-start | bytes 524288 | tf_op jit(solution)/shard_map/all_to_all | solution.py:664
  60.0 6.3 %pair.1 = (bf16[2,2,1024,256]{3,2,1,0:T(8,128)(2,1)}, bf16[2,2,256,1024]{3,2,1,0:T(8,128)(2,1)}, bf16[2,2,1024,256]{3,2,1,0:T(8,128)(2,1)}, f32[8,128]{1,0:T(8,128)}) custom-call(s32[3]{0:T(128)S(1)} %pad_add_fusion.where_ref, bf16[4,2,256,256]{3,2,1,0:T(8,128)(2,1)S(1)} %bitcast.15, ...), custom_call_target="tpu_custom_call" | custom-call | flops 2147483648 | bytes 8388608 | tf_op jit(solution)/shard_map/pair/pallas_call | solution.py:303
  66.3 3.6 %all-to-all-done.2.second_ref = f32[32,10,128]{2,1,0:T(8,128)S(1)} async-done(((f32[32,10,128]{2,1,0:T(8,128)}), f32[32,10,128]{2,1,0:T(8,128)S(1)}, u32[]{:S(2)}, u32[]{:S(2)}) %all-to-all-start.2) | async-done | bytes 163872 | tf_op jit(solution)/shard_map/all_to_all | solution.py:664
  69.9 27.6 %near_gradients.1 = (f32[1024,256]{1,0:T(8,128)S(1)}, f32[1024,256]{1,0:T(8,128)S(1)}, f32[256,4096]{1,0:T(8,128)}) custom-call(s32[3]{0:T(128)S(1)} %pad_add_fusion.where_ref, bf16[2,2,1024,256]{3,2,1,0:T(8,128)(2,1)} %get-tuple-element.45.unit_ref, bf16[2,2,256,1024]{3,2,1,0:T(8,128)(2,1)} %get-tuple-element.46.turned_ref, ...), custom_call_target="tpu_custom_call" | custom-call | flops 17179869184 | bytes 8388608 | tf_op jit(solution)/shard_map/near_gradients/pallas_call | solution.py:479
  97.6 2.5 %collective-permute-done.6 = f32[1024,256]{1,0:T(8,128)S(1)} collective-permute-done((f32[1024,256]{1,0:T(8,128)S(1)}, f32[1024,256]{1,0:T(8,128)S(1)}, u32[]{:S(2)}, u32[]{:S(2)}) %collective-permute-start.6) | collective-permute-done | bytes 1048608 | tf_op jit(solution)/shard_map/ppermute | solution.py:660
  100.2 1.0 multiply_convert_fusion
  101.1 3.5 %all-to-all-start.3 = ((f16[8,128,256]{2,1,0:T(8,128)(2,1)}), f16[8,128,256]{2,1,0:T(8,128)(2,1)S(1)}, u32[]{:S(2)}, u32[]{:S(2)}) async-start(f16[8,128,256]{2,1,0:T(8,128)(2,1)} %bitcast.8), calls=%async_computation.3 | async-start | bytes 1048576 | tf_op jit(solution)/shard_map/all_to_all | solution.py:664
  104.6 25.9 %far_gradients.1 = f32[128,4352]{1,0:T(8,128)} custom-call(s32[3]{0:T(128)} %copy-done.4, bf16[2,2,1024,256]{3,2,1,0:T(8,128)(2,1)} %get-tuple-element.45.unit_ref, bf16[2,2,256,1024]{3,2,1,0:T(8,128)(2,1)} %get-tuple-element.46.turned_ref, bf16[2,2,1024,256]{3,2,1,0:T(8,128)(2,1)} %get-tuple-element.47.paired_ref, f32[32,10,128]{2,1,0:T(8,128)} %copy-done.1, ...), custom_call_target="tpu_custom_call" | custom-call | flops 12884901888 | bytes 8388608 | tf_op jit(solution)/shard_map/far_gradients/pallas_call | solution.py:592
  130.5 2.7 %convert_element_type.18 = f16[128,4352]{1,0:T(8,128)(2,1)} convert(f32[128,4352]{1,0:T(8,128)} %far_gradients.1) | non-fusion elementwise | flops 557056 | bytes 3342336 | tf_op jit(solution)/shard_map/convert_element_type | solution.py:761
  133.3 4.1 %all-to-all-start.4 = ((f16[8,16,4352]{2,1,0:T(8,128)(2,1)}), f16[8,16,4352]{2,1,0:T(8,128)(2,1)S(1)}, u32[]{:S(2)}, u32[]{:S(2)}) async-start(f16[8,16,4352]{2,1,0:T(8,128)(2,1)} %bitcast.9), calls=%async_computation.4 | async-start | bytes 2228224 | tf_op jit(solution)/shard_map/all_to_all | solution.py:664
  137.6 1.5 collective-permute-start.7
  139.1 4.4 %collective-permute-done.7 = f32[128,256]{1,0:T(8,128)S(1)} collective-permute-done((f32[128,256]{1,0:T(8,128)S(1)}, f32[128,256]{1,0:T(8,128)S(1)}, u32[]{:S(2)}, u32[]{:S(2)}) %collective-permute-start.7) | collective-permute-done | bytes 131104 | tf_op jit(solution)/shard_map/ppermute | solution.py:660
  143.6 0.8 maximum_divide_fusion
  144.4 8.1 %all-to-all-done.4 = f16[8,16,4352]{2,1,0:T(8,128)(2,1)S(1)} async-done(((f16[8,16,4352]{2,1,0:T(8,128)(2,1)}), f16[8,16,4352]{2,1,0:T(8,128)(2,1)S(1)}, u32[]{:S(2)}, u32[]{:S(2)}) %all-to-all-start.4) | async-done | bytes 1114144 | tf_op jit(solution)/shard_map/all_to_all | solution.py:664
  152.7 1.9 %join.1 = f32[16,32768]{1,0:T(8,128)} custom-call(f32[8,16,4352]{2,1,0:T(8,128)S(1)} %convert_element_type.19.came_ref), custom_call_target="tpu_custom_call" | custom-call | flops 524288 | bytes 4194304 | tf_op jit(solution)/shard_map/join/pallas_call | solution.py:643
  (45 shorter events, 1.7 us)
Async XLA Ops:
  0.6 11.0 %collective-permute-start.1 = (bf16[1,256,256]{2,1,0:T(8,128)(2,1)}, bf16[1,256,256]{2,1,0:T(8,128)(2,1)S(1)}, u32[]{:S(2)}, u32[]{:S(2)}) collective-permute-start(bf16[1,256,256]{2,1,0:T(8,128)(2,1)} %bitcast.10), channel_id=1, source_target_pairs={{0,16},{4,20},{8,24},{12,28},{16,0},{20,4},{24,8},{28,12},{1,17},{... | collective-permute-start | bytes 393224 | tf_op jit(solution)/shard_map/ppermute | solution.py:713
  4.8 65.1 %copy-start.4 = (s32[3]{0:T(128)}, s32[3]{0:T(128)S(1)}, u32[]{:S(2)}) copy-start(s32[3]{0:T(128)S(1)} %pad_add_fusion.where_ref) | copy-start | bytes 40
  4.8 6.9 %copy-start = (bf16[256,256]{1,0:T(8,128)(2,1)S(1)}, bf16[256,256]{1,0:T(8,128)(2,1)}, u32[]{:S(2)}) copy-start(bf16[256,256]{1,0:T(8,128)(2,1)} %students_ref.1) | copy-start | bytes 393220
  4.8 8.5 %copy-start.12 = (bf16[64,256]{1,0:T(8,128)(2,1)S(1)}, bf16[64,256]{1,0:T(8,128)(2,1)}, u32[]{:S(2)}) copy-start(bf16[64,256]{1,0:T(8,128)(2,1)} %param.5) | copy-start | bytes 98308
  10.3 1.4 copy-start.5
  11.7 2.4 %copy-start.9 = (f32[1,4096]{1,0:T(1,128)}, f32[1,4096]{1,0:T(1,128)S(1)}, u32[]{:S(2)}) copy-start(f32[1,4096]{1,0:T(1,128)S(1)} %get-tuple-element.29.norm_ref) | copy-start | bytes 49156
  11.7 14.0 %collective-permute-start.2 = (bf16[2,256,256]{2,1,0:T(8,128)(2,1)S(1)}, bf16[2,256,256]{2,1,0:T(8,128)(2,1)S(1)}, u32[]{:S(2)}, u32[]{:S(2)}) collective-permute-start(bf16[2,256,256]{2,1,0:T(8,128)(2,1)S(1)} %pad_maximum_fusion.2), channel_id=1, source_target_pairs={{0,8},{4,12},{8,0},{12,4},{16,24},{20,28},{24,16},{28,20},{1,9},{5... | collective-permute-start | bytes 786440 | tf_op jit(solution)/shard_map/ppermute | solution.py:713
  14.1 13.8 %all-to-all-start = ((bf16[8,64,256]{2,1,0:T(8,128)(2,1)}), bf16[8,64,256]{2,1,0:T(8,128)(2,1)S(1)}, u32[]{:S(2)}, u32[]{:S(2)}) async-start(bf16[8,64,256]{2,1,0:T(8,128)(2,1)} %tile.2), calls=%async_computation | async-start | bytes 524288 | tf_op jit(solution)/shard_map/all_to_all | solution.py:664
  18.4 11.0 %copy-start.10 = (s32[256]{0:T(256)S(1)}, s32[256]{0:T(256)}, u32[]{:S(2)}) copy-start(s32[256]{0:T(256)} %param.8) | copy-start | bytes 3076
  18.4 11.0 %copy-start.11 = (s32[256]{0:T(256)S(1)}, s32[256]{0:T(256)}, u32[]{:S(2)}) copy-start(s32[256]{0:T(256)} %param.9) | copy-start | bytes 3076
  25.7 13.6 %collective-permute-start.3 = (bf16[4,256,256]{2,1,0:T(8,128)(2,1)S(1)}, bf16[4,256,256]{2,1,0:T(8,128)(2,1)S(1)}, u32[]{:S(2)}, u32[]{:S(2)}) collective-permute-start(bf16[4,256,256]{2,1,0:T(8,128)(2,1)S(1)} %pad_maximum_fusion.1), channel_id=1, source_target_pairs={{0,4},{4,0},{8,12},{12,8},{16,20},{20,16},{24,28},{28,24},{1,5},{5... | collective-permute-start | bytes 1572872 | tf_op jit(solution)/shard_map/ppermute | solution.py:713
  27.8 1.5 collective-permute-start
  29.4 1.6 %copy-start.6 = (bf16[256,4096]{1,0:T(8,128)(2,1)S(1)}, bf16[256,4096]{1,0:T(8,128)(2,1)}, u32[]{:S(2)}) copy-start(bf16[256,4096]{1,0:T(8,128)(2,1)} %copy-done.5) | copy-start | bytes 6291460
  34.8 15.3 %all-to-all-start.1 = ((f32[32,10,128]{2,1,0:T(8,128)}), f32[32,10,128]{2,1,0:T(8,128)S(1)}, u32[]{:S(2)}, u32[]{:S(2)}) async-start(f32[32,10,128]{2,1,0:T(8,128)} %get-tuple-element.34), calls=%async_computation.1 | async-start | bytes 524288 | tf_op jit(solution)/shard_map/all_to_all | solution.py:664
  39.5 20.5 %collective-permute-start.4 = (bf16[4,2,256,256]{3,2,1,0:T(8,128)(2,1)S(1)}, bf16[4,2,256,256]{3,2,1,0:T(8,128)(2,1)S(1)}, u32[]{:S(2)}, u32[]{:S(2)}) collective-permute-start(bf16[4,2,256,256]{3,2,1,0:T(8,128)(2,1)S(1)} %bitcast.14), channel_id=1, source_target_pairs={{0,2},{2,0},{1,3},{3,1},{4,6},{6,4},{5,7},{7,5},{8,10},{10,8},{9,1... | collective-permute-start | bytes 3145736 | tf_op jit(solution)/shard_map/ppermute | solution.py:660
  50.0 19.8 %copy-start.1 = (f32[32,10,128]{2,1,0:T(8,128)}, f32[32,10,128]{2,1,0:T(8,128)S(1)}, u32[]{:S(2)}) copy-start(f32[32,10,128]{2,1,0:T(8,128)S(1)} %all-to-all-done.1.came_ref.first_ref) | copy-start | bytes 491524
  50.0 1.7 %copy-start.7 = (bf16[256,4096]{1,0:T(8,128)(2,1)S(1)}, bf16[256,4096]{1,0:T(8,128)(2,1)}, u32[]{:S(2)}) copy-start(bf16[256,4096]{1,0:T(8,128)(2,1)} %copy-done.5) | copy-start | bytes 6291460
  55.4 4.5 %collective-permute-start.5 = (f32[1,2048]{1,0:T(1,128)S(1)}, f32[1,2048]{1,0:T(1,128)S(1)}, u32[]{:S(2)}, u32[]{:S(2)}) collective-permute-start(f32[1,2048]{1,0:T(1,128)S(1)} %get-tuple-element.49), channel_id=1, source_target_pairs={{0,16},{16,0},{1,17},{17,1},{2,18},{18,2},{3,19},{19,3},{4,20},{20... | collective-permute-start | bytes 24584 | tf_op jit(solution)/shard_map/ppermute | solution.py:744
  56.3 13.5 %all-to-all-start.2 = ((f32[32,10,128]{2,1,0:T(8,128)}), f32[32,10,128]{2,1,0:T(8,128)S(1)}, u32[]{:S(2)}, u32[]{:S(2)}) async-start(f32[32,10,128]{2,1,0:T(8,128)} %get-tuple-element.37), calls=%async_computation.2 | async-start | bytes 524288 | tf_op jit(solution)/shard_map/all_to_all | solution.py:664
  59.9 9.9 %copy-start.3 = (f32[1,4096]{1,0:T(1,128)}, f32[1,4096]{1,0:T(1,128)S(1)}, u32[]{:S(2)}) copy-start(f32[1,4096]{1,0:T(1,128)S(1)} %pad_maximum_fusion.3.factor_ref) | copy-start | bytes 49156
  60.0 6.3 %copy-start.8 = (bf16[4,2,256,256]{3,2,1,0:T(8,128)(2,1)}, bf16[4,2,256,256]{3,2,1,0:T(8,128)(2,1)S(1)}, u32[]{:S(2)}) copy-start(bf16[4,2,256,256]{3,2,1,0:T(8,128)(2,1)S(1)} %collective-permute-done.4.other_ref.other_raw_ref) | copy-start | bytes 3145732
  69.9 27.6 %copy-start.2 = (f32[32,10,128]{2,1,0:T(8,128)}, f32[32,10,128]{2,1,0:T(8,128)S(1)}, u32[]{:S(2)}) copy-start(f32[32,10,128]{2,1,0:T(8,128)S(1)} %all-to-all-done.2.second_ref) | copy-start | bytes 491524
  97.5 2.7 %collective-permute-start.6 = (f32[1024,256]{1,0:T(8,128)S(1)}, f32[1024,256]{1,0:T(8,128)S(1)}, u32[]{:S(2)}, u32[]{:S(2)}) collective-permute-start(f32[1024,256]{1,0:T(8,128)S(1)} %get-tuple-element.52), channel_id=1, source_target_pairs={{0,2},{2,0},{1,3},{3,1},{4,6},{6,4},{5,7},{7,5},{8,10},{10,8},{9,1... | collective-permute-start | bytes 3145736 | tf_op jit(solution)/shard_map/ppermute | solution.py:660
  101.1 32.2 %all-to-all-start.3 = ((f16[8,128,256]{2,1,0:T(8,128)(2,1)}), f16[8,128,256]{2,1,0:T(8,128)(2,1)S(1)}, u32[]{:S(2)}, u32[]{:S(2)}) async-start(f16[8,128,256]{2,1,0:T(8,128)(2,1)} %bitcast.8), calls=%async_computation.3 | async-start | bytes 1048576 | tf_op jit(solution)/shard_map/all_to_all | solution.py:664
  133.3 19.3 %all-to-all-start.4 = ((f16[8,16,4352]{2,1,0:T(8,128)(2,1)}), f16[8,16,4352]{2,1,0:T(8,128)(2,1)S(1)}, u32[]{:S(2)}, u32[]{:S(2)}) async-start(f16[8,16,4352]{2,1,0:T(8,128)(2,1)} %bitcast.9), calls=%async_computation.4 | async-start | bytes 2228224 | tf_op jit(solution)/shard_map/all_to_all | solution.py:664
  137.6 6.0 %collective-permute-start.7 = (f32[128,256]{1,0:T(8,128)S(1)}, f32[128,256]{1,0:T(8,128)S(1)}, u32[]{:S(2)}, u32[]{:S(2)}) collective-permute-start(f32[128,256]{1,0:T(8,128)S(1)} %broadcast_multiply_fusion), channel_id=1, source_target_pairs={{0,1},{1,0},{2,3},{3,2},{4,5},{5,4},{6,7},{7,6},{8,9},{9,8},{10,11... | collective-permute-start | bytes 393224 | tf_op jit(solution)/shard_map/ppermute | solution.py:660

commit v4 on v3

--- a/solution.py
+++ b/solution.py
@@ -102,51 +102,16 @@
         return jnp.where(where[2] == 0, sums[0] + turned[1], sums[1] + turned[0])
 
 
-def columns_kernel(where_ref, raw_ref, unit_ref, flipped_ref, norm_ref, copy_ref):
-    copy_ref[...] = raw_ref[...]
-    full = raw_ref[...].astype(F32)
-    norm = jnp.sqrt(jnp.sum(full * full, 0, keepdims=True) + epsilon)
-    unit = full * (1.0 / norm)
-    unit_ref[...] = unit.astype(BF16)
-    flipped_ref[...] = jnp.transpose(unit.astype(BF16))
-    norm_ref[...] = norm
-
-
-def unit_columns(where, prototypes, columns):
-    width = prototypes.shape[0]
-    tile = tile_of(columns, 1024)
-    steps = columns // tile
-    return pl.pallas_call(
-        columns_kernel,
-        out_shape=[
-            jax.ShapeDtypeStruct((width, columns), BF16),
-            jax.ShapeDtypeStruct((columns, width), BF16),
-            jax.ShapeDtypeStruct((1, columns), F32),
-            jax.ShapeDtypeStruct((width, columns), BF16),
-        ],
-        grid_spec=pltpu.PrefetchScalarGridSpec(
-            num_scalar_prefetch=1,
-            grid=(steps,),
-            in_specs=[
-                pl.BlockSpec((width, tile), lambda j, w: (0, (w[1] * 2 + w[2]) * steps + j))
-            ],
-            out_specs=[
-                pl.BlockSpec((width, tile), lambda j, w: (0, j)),
-                pl.BlockSpec((tile, width), lambda j, w: (j, 0)),
-                pl.BlockSpec((1, tile), lambda j, w: (0, j)),
-                pl.BlockSpec((width, tile), lambda j, w: (0, j)),
-            ],
-        ),
-        compiler_params=params(50),
-        cost_estimate=pl.CostEstimate(
-            flops=8 * width * columns, bytes_accessed=6 * width * columns, transcendentals=0
-        ),
-        name="unit_columns",
-    )(where, prototypes)
-
-
-def denominator_kernel(students_ref, weights_ref, total_ref, unit, folded, *, sub):
+def denominator_kernel(where_ref, students_ref, weights_ref, *refs, sub):
+    total_ref, unit, folded = refs[-3:]
     step = pl.program_id(0)
+
+    if len(refs) > 3:
+        raw_ref, unit_ref, norm_ref = refs[:3]
+        full = raw_ref[...].astype(F32)
+        norm = jnp.sqrt(jnp.sum(full * full, 0, keepdims=True) + epsilon)
+        unit_ref[...] = (full * (1.0 / norm)).astype(BF16)
+        norm_ref[...] = norm
 
     @pl.when(step == 0)
     def _():
@@ -169,21 +134,44 @@
         total_ref[...] = as_rows(folded[...])
 
 
-def local_denominator(students, prototypes, part, parts):
+def local_denominator(where, students, prototypes, part, count, parts, mine=0):
     rows, width = students.shape
     columns = prototypes.shape[1] // parts
     tile = tile_of(columns, 4096)
     steps = columns // tile
+    before = part * steps
+    steps, columns = steps * count, columns * count
+    in_specs = [
+        pl.BlockSpec((rows, width), lambda j, w: (0, 0)),
+        pl.BlockSpec((width, tile), lambda j, w: (0, before + j)),
+    ]
+    out_specs = [pl.BlockSpec((rows // LANES, LANES), lambda j, w: (0, 0))]
+    out_shape = [jax.ShapeDtypeStruct((rows // LANES, LANES), F32)]
+    operands = [students, prototypes]
+    if mine:
+        each = mine // steps
+        operands.append(prototypes)
+        in_specs.append(
+            pl.BlockSpec((width, each), lambda j, w: (0, (w[1] * 2 + w[2]) * steps + j))
+        )
+        out_specs = [
+            pl.BlockSpec((width, each), lambda j, w: (0, j)),
+            pl.BlockSpec((1, each), lambda j, w: (0, j)),
+        ] + out_specs
+        out_shape = [
+            jax.ShapeDtypeStruct((width, mine), BF16),
+            jax.ShapeDtypeStruct((1, mine), F32),
+        ] + out_shape
     return pl.pallas_call(
         functools.partial(denominator_kernel, sub=tile_of(tile, 512)),
-        out_shape=jax.ShapeDtypeStruct((rows // LANES, LANES), F32),
-        grid=(steps,),
-        in_specs=[
-            pl.BlockSpec((rows, width), lambda j: (0, 0)),
-            pl.BlockSpec((width, tile), lambda j: (0, part * steps + j)),
-        ],
-        out_specs=pl.BlockSpec((rows // LANES, LANES), lambda j: (0, 0)),
-        scratch_shapes=[pltpu.VMEM((rows, width), BF16), pltpu.VMEM((rows, LANES), F32)],
+        out_shape=out_shape,
+        grid_spec=pltpu.PrefetchScalarGridSpec(
+            num_scalar_prefetch=1,
+            grid=(steps,),
+            in_specs=in_specs,
+            out_specs=out_specs,
+            scratch_shapes=[pltpu.VMEM((rows, width), BF16), pltpu.VMEM((rows, LANES), F32)],
+        ),
         compiler_params=params(50),
         cost_estimate=pl.CostEstimate(
             flops=2 * rows * width * columns,
@@ -191,7 +179,7 @@
             transcendentals=rows * columns,
         ),
         name="denominator",
-    )(students, prototypes)
+    )(where, *operands)
 
 
 def sweep_totals(units, weights_ref, column, sub, factor_ref):
@@ -267,18 +255,21 @@
     )(where, *operands)
 
 
-def pair_kernel(where_ref, own_ref, other_ref, came_ref, teacher_ref, unit_ref, turned_ref, paired_ref, mark_ref, *, plan):
-    mark_ref[...] = jnp.zeros_like(mark_ref)
+def pair_kernel(
+    where_ref, own_ref, other_ref, came_ref, teacher_ref, weights_ref, both_ref, turned_ref,
+    flipped_ref, *, plan
+):
     where = (where_ref[0], where_ref[1], where_ref[2])
     apart = plan.halves - 1 - pl.program_id(0)
     teachers = teacher_ref.shape[0]
     count = plan.stu_count
     lane = lax.broadcasted_iota(jnp.int32, (count, LANES), 1).astype(F32)
+    flipped_ref[...] = jnp.transpose(weights_ref[...])
     for side, ref in enumerate((own_ref, other_ref)):
         for place in range(plan.chips):
             rows = slice(place * count, (place + 1) * count)
             unit = unit_rows(ref[place, 0]).astype(BF16)
-            unit_ref[0, side, rows, :] = unit
+            both_ref[0, side, 0, rows, :] = unit
             turned_ref[0, side, :, rows] = jnp.transpose(unit)
             sender = plan.sender(where, apart, side, place)
             index = as_columns(came_ref[sender, plan.tea_lanes :, :])
@@ -291,22 +282,21 @@
                 ],
                 1,
             )
-            paired_ref[0, side, rows, :] = dot(chosen, teacher_ref[...]).astype(BF16)
-
-
-def pair(plan, where, own, other, came, teachers):
-    width = own.shape[3]
+            both_ref[0, side, 1, rows, :] = dot(chosen, teacher_ref[...]).astype(BF16)
+
+
+def pair(plan, where, own, other, came, teachers, weights):
+    width, columns = weights.shape
+    each = columns // plan.halves
     held = pl.BlockSpec(
         (plan.chips, 1, plan.stu_count, width), lambda g, w: (0, plan.halves - 1 - g, 0, 0)
     )
-    rows = pl.BlockSpec((1, 2, plan.block, width), lambda g, w: (g, 0, 0, 0))
     return pl.pallas_call(
         functools.partial(pair_kernel, plan=plan),
         out_shape=[
-            jax.ShapeDtypeStruct((plan.halves, 2, plan.block, width), BF16),
+            jax.ShapeDtypeStruct((plan.halves, 2, 2, plan.block, width), BF16),
             jax.ShapeDtypeStruct((plan.halves, 2, width, plan.block), BF16),
-            jax.ShapeDtypeStruct((plan.halves, 2, plan.block, width), BF16),
-            jax.ShapeDtypeStruct((8, LANES), F32),
+            jax.ShapeDtypeStruct((columns, width), BF16),
         ],
         grid_spec=pltpu.PrefetchScalarGridSpec(
             num_scalar_prefetch=1,
@@ -316,12 +306,12 @@
                 held,
                 pl.BlockSpec(came.shape, lambda g, w: (0, 0, 0)),
                 pl.BlockSpec(teachers.shape, lambda g, w: (0, 0)),
+                pl.BlockSpec((width, each), lambda g, w: (0, g)),
             ],
             out_specs=[
-                rows,
+                pl.BlockSpec((1, 2, 2, plan.block, width), lambda g, w: (g, 0, 0, 0, 0)),
                 pl.BlockSpec((1, 2, width, plan.block), lambda g, w: (g, 0, 0, 0)),
-                rows,
-                pl.BlockSpec((8, LANES), lambda g, w: (0, 0)),
+                pl.BlockSpec((each, width), lambda g, w: (g, 0)),
             ],
         ),
         compiler_params=params(50),
@@ -331,7 +321,7 @@
             transcendentals=0,
         ),
         name="pair",
-    )(where, own, other, came, teachers)
+    )(where, own, other, came, teachers, weights)
 
 
 def fill_scale(plan, where, apart, side, first_ref, second_ref, row_factor, scale):
@@ -355,18 +345,18 @@
 
 
 def gradient_products(
-    unit_ref, turned_ref, paired_ref, factor_ref, weights_ref, flipped_ref, shares_ref, scale,
-    grads, sub, earlier,
+    both_ref, turned_ref, factor_ref, weights_ref, flipped_ref, shares_ref, scale, grads, sub,
+    earlier,
 ):
     columns = weights_ref.shape[1]
-    tile = tile_of(columns, 4 * sub)
+    tile = tile_of(columns, 8 * sub)
 
     def products(step, shares):
         base = pl.multiple_of(step * tile, tile)
 
         def logits(start):
             weights = weights_ref[:, pl.ds(base + start, sub)]
-            return dot(unit_ref[0, 0], weights), dot(paired_ref[0, 0], weights)
+            return dot(both_ref[0, 0, 0], weights), dot(both_ref[0, 0, 1], weights)
 
         ahead = logits(0)
         for start in range(0, tile, sub):
@@ -395,9 +385,8 @@
 
 def near_kernel(
     where_ref,
-    unit_ref,
+    both_ref,
     turned_ref,
-    paired_ref,
     first_ref,
     second_ref,
     factor_ref,
@@ -431,7 +420,7 @@
         shares[side] = jnp.zeros(shares.shape[1:], F32)
 
     gradient_products(
-        unit_ref, turned_ref, paired_ref, factor_ref, weights_ref, flipped_ref, shares.at[side],
+        both_ref, turned_ref, factor_ref, weights_ref, flipped_ref, shares.at[side],
         scale.at[side], grads_ref, sub, lambda span: jnp.where(side == 0, 0.0, grads_ref[:, span]),
     )
 
@@ -463,12 +452,12 @@
     return 2 if columns % (2 * LANES) == 0 else 1
 
 
-def near_gradients(plan, where, unit, turned, paired, first, second, factor, weights, flipped, own, other):
+def near_gradients(plan, where, both, turned, first, second, factor, weights, flipped, own, other):
     width, columns = weights.shape
     parts = parts_of(columns)
     each = columns // parts
     last = plan.halves - 1
-    rows = pl.BlockSpec((1, 1, plan.block, width), lambda q, p, w: (last, p, 0, 0))
+    rows = pl.BlockSpec((1, 1, 2, plan.block, width), lambda q, p, w: (last, p, 0, 0, 0))
     across = pl.BlockSpec((width, each), lambda q, p, w: (0, q))
     raw = pl.BlockSpec(
         (plan.chips, 1, plan.stu_count, width),
@@ -485,7 +474,6 @@
             in_specs=[
                 rows,
                 pl.BlockSpec((1, 1, width, plan.block), lambda q, p, w: (last, p, 0, 0)),
-                rows,
                 whole_spec(first),
                 whole_spec(second),
                 pl.BlockSpec((1, each), lambda q, p, w: (0, q)),
@@ -508,14 +496,13 @@
             transcendentals=4 * plan.block * columns,
         ),
         name="near_gradients",
-    )(where, unit, turned, paired, first, second, factor, weights, flipped, own, other)
+    )(where, both, turned, first, second, factor, weights, flipped, own, other)
 
 
 def far_kernel(
     where_ref,
-    unit_ref,
+    both_ref,
     turned_ref,
-    paired_ref,
     first_ref,
     second_ref,
     factor_ref,
@@ -549,7 +536,7 @@
         )
 
     gradient_products(
-        unit_ref, turned_ref, paired_ref, factor_ref, weights_ref, None, None, scale.at[block],
+        both_ref, turned_ref, factor_ref, weights_ref, None, None, scale.at[block],
         grads, sub, lambda span: jnp.where(block == 0, before_ref[:, span], grads[:, span]),
     )
 
@@ -579,14 +566,14 @@
 
 
 def far_gradients(
-    plan, where, unit, turned, paired, first, second, factor, weights, raw, norm, before
+    plan, where, both, turned, first, second, factor, weights, prototypes, norm, before
 ):
     width, columns = weights.shape
     parts = parts_of(columns)
     each = columns // parts
     blocks = 2 * (plan.halves - 1)
     kept = width // plan.halves
-    rows = pl.BlockSpec((1, 1, plan.block, width), lambda q, p, w: (p // 2, p % 2, 0, 0))
+    rows = pl.BlockSpec((1, 1, 2, plan.block, width), lambda q, p, w: (p // 2, p % 2, 0, 0, 0))
     across = pl.BlockSpec((width, each), lambda q, p, w: (0, q))
     thin = pl.BlockSpec((1, each), lambda q, p, w: (0, q))
     return pl.pallas_call(
@@ -598,12 +585,11 @@
             in_specs=[
                 rows,
                 pl.BlockSpec((1, 1, width, plan.block), lambda q, p, w: (p // 2, p % 2, 0, 0)),
-                rows,
                 whole_spec(first),
                 whole_spec(second),
                 thin,
                 across,
-                across,
+                pl.BlockSpec((width, each), lambda q, p, w: (0, (w[1] * 2 + w[2]) * parts + q)),
                 thin,
                 across,
             ],
@@ -614,14 +600,14 @@
                 pltpu.VMEM((plan.tea_lanes * LANES, LANES), F32),
             ],
         ),
-        compiler_params=params(56, 2),
+        compiler_params=params(46, 2),
         cost_estimate=pl.CostEstimate(
             flops=12 * (plan.halves - 1) * plan.block * width * columns,
             bytes_accessed=8 * width * columns,
             transcendentals=4 * (plan.halves - 1) * plan.block * columns,
         ),
         name="far_gradients",
-    )(where, unit, turned, paired, first, second, factor, weights, raw, norm, before)
+    )(where, both, turned, first, second, factor, weights, prototypes, norm, before)
 
 
 def join_kernel(came_ref, out_ref, *, parts):
@@ -685,9 +671,11 @@
     where = jnp.stack([half, chip, core]).astype(jnp.int32)
     parcel = lambda lanes: jax.ShapeDtypeStruct((plan.devices, lanes, LANES), F32)
 
-    tea_own = gather(teacher, ("half", "chip"), all_chips)
-    weights, flipped, norm, raw = unit_columns(where, prototypes, columns)
-    near_total = local_denominator(tie(students, norm), prototypes, 0, 2)
+    tiled = jnp.tile(teacher, (all_chips, 1))
+    tea_own = exchange(tiled, ("half", "chip"))
+    weights, norm, near_total = local_denominator(
+        tie(where, tiled), students, prototypes, 0, 1, 4, columns
+    )
     tea_other = swap(tea_own, "core")
     parcel_one, tea_unit, mark = sweep_call(
         first_sweep_kernel,
@@ -704,10 +692,10 @@
         "first_sweep",
     )
     first = exchange(parcel_one, everyone)
-    far_total = local_denominator(tie(students, mark), prototypes, 1, 2)
-
-    markers = [norm, near_total, mark]
-    gathered = students[None]
+    (far_total,) = local_denominator(tie(where, mark), students, prototypes, 1, 3, 4)
+
+    markers = [near_total, mark, far_total]
+    gathered = tie(students, tiled)[None]
     bit = all_chips // 2
     while bit:
         came = lax.ppermute(
@@ -734,10 +722,10 @@
         "second_sweep",
     )
     second = exchange(parcel_two, everyone)
-    unit, turned, paired, _ = pair(
-        plan, where, stu_own, stu_other, tie(first, parcel_two), tea_unit
-    )
-    second, unit, turned, paired = lax.optimization_barrier((second, unit, turned, paired))
+    both, turned, flipped = pair(
+        plan, where, stu_own, stu_other, tie(first, parcel_two), tea_unit, weights
+    )
+    second, both, turned, flipped = lax.optimization_barrier((second, both, turned, flipped))
     factors = [factor]
     for step in range(1, halves):
         factors.append(
@@ -749,14 +737,14 @@
         factors = [jnp.stack(factors)[(half - step) % halves] for step in range(halves)]
     factor = jnp.concatenate(factors, 1)
 
-    rows_of = (unit, turned, paired, first, second, factor, weights)
+    rows_of = (both, turned, first, second, factor, weights)
     own_part, other_part, proto_all = near_gradients(
         plan, where, *rows_of, flipped, stu_own, stu_other
     )
     summed = (own_part + swap(other_part, "core")) * 128.0
     sent = summed.astype(F16).reshape(chips * protos, stu_count // protos, width)
     came = exchange(sent, ("chip", "protos"))
-    proto_part = far_gradients(plan, tie(where, sent), *rows_of, raw, norm, proto_all)
+    proto_part = far_gradients(plan, tie(where, sent), *rows_of, prototypes, norm, proto_all)
     share = width // (all_chips * 2)
     sent = proto_part.astype(F16).reshape(chips * 2, share, -1)
     grad_protos = join(exchange(sent, ("chip", "core")).astype(F32), parts_of(columns))

time: 155 us -> 152 us (0.981)
  Pallas kernels: 89.1 us -> 81.1 us
  local copies, waits for them, and re-layouts: 5.41 us -> 10.1 us
  waiting for transfers between devices: 23.8 us -> 25.8 us
    ppermute x3, waiting for transfers between devices: 0.01 us -> 6.55 us  [body(): lax.ppermute(gathered, ('half', 'chip'), [(q, q ^ bit) for q in range(all...]
    pallas_call x1 -> x0, Pallas kernels: 5.49 us -> none  [unit_columns(): pl.pallas_call(columns_kernel, out_shape=[jax.ShapeDtypeStruct((width, co...]
    pallas_call x1, Pallas kernels: 25.9 us -> 21.7 us  [far_gradients(): pl.pallas_call(functools.partial(far_kernel, plan=plan, sub=tile_of(each,...]
    unnamed x26 -> x20, local copies, waits for them, and re-layouts: 4.69 us -> 8.59 us
    all_to_all x5, waiting for transfers between devices: 14.8 us -> 10.9 us  [exchange(): return lax.all_to_all(value, axes, split_axis=0, concat_axis=0, tiled=True)]
    ppermute x3, starting transfers between devices: 7.83 us -> 4.47 us  [body(): lax.ppermute(gathered, ('half', 'chip'), [(q, q ^ bit) for q in range(all...]
    pallas_call x2, Pallas kernels: 14.5 us -> 16.7 us  [local_denominator(): pl.pallas_call(functools.partial(denominator_kernel, sub=tile_of(tile, 51...]
    all_to_all x5, starting transfers between devices: 19.5 us -> 21.5 us  [exchange(): return lax.all_to_all(value, axes, split_axis=0, concat_axis=0, tiled=True)]
  transfers between devices with their start and end apart: 13 -> 13, of which waited for: 7 -> 8; matrix products, arithmetic and copies ran while one was open for 3% -> 2% of each run, Pallas kernels for 39% -> 35%
where the time goes in v4:
time: 152 us; the launch traced here: 151 us
  Pallas kernels  81.1 us (53%)
  starting transfers between devices  29.1 us (19%)
  waiting for transfers between devices  25.8 us (17%)
  local copies, waits for them, and re-layouts  10.1 us (7%)
  other arithmetic  4.59 us (3%)
    pallas_call x1, Pallas kernels, near_gradients(): pl.pallas_call(functools.partial(near_kernel, plan=plan, sub=tile_of(each...  25.6 us
    pallas_call x1, Pallas kernels, far_gradients(): pl.pallas_call(functools.partial(far_kernel, plan=plan, sub=tile_of(each,...  21.7 us
    all_to_all x5, starting transfers between devices, exchange(): return lax.all_to_all(value, axes, split_axis=0, concat_axis=0, tiled=True)  21.5 us
    pallas_call x2, Pallas kernels, local_denominator(): pl.pallas_call(functools.partial(denominator_kernel, sub=tile_of(tile, 51...  16.7 us
    all_to_all x5, waiting for transfers between devices, exchange(): return lax.all_to_all(value, axes, split_axis=0, concat_axis=0, tiled=True)  10.9 us
    unnamed x20, local copies, waits for them, and re-layouts  8.59 us
    ppermute x4, waiting for transfers between devices, swap(): return lax.ppermute(value, axis, [(0, 1), (1, 0)])  8.39 us
    pallas_call x1, Pallas kernels, pair(): pl.pallas_call(functools.partial(pair_kernel, plan=plan), out_shape=[jax....  7.72 us
  transfers between devices with their start and end apart: 13, of which 8 were waited for; matrix products, arithmetic and copies ran while one was open for 2% of the time, Pallas kernels for 35%

profile of v4, /device:TPU:0, one launch (start us, length us, event | category | flops | bytes accessed | tf_op | source)
XLA Modules:
  0.0 151.5 jit_solution(2789137530198065589)
XLA Ops:
  0.6 1.5 tile.4
  2.1 7.3 %all-to-all-start = ((bf16[8,64,256]{2,1,0:T(8,128)(2,1)}), bf16[8,64,256]{2,1,0:T(8,128)(2,1)S(1)}, u32[]{:S(2)}, u32[]{:S(2)}) async-start(bf16[8,64,256]{2,1,0:T(8,128)(2,1)} %tile.4), calls=%async_computation | async-start | bytes 524288 | tf_op jit(solution)/shard_map/all_to_all | solution.py:650
  9.4 2.9 %collective-permute-start.1 = (bf16[1,256,256]{2,1,0:T(8,128)(2,1)}, bf16[1,256,256]{2,1,0:T(8,128)(2,1)S(1)}, u32[]{:S(2)}, u32[]{:S(2)}) collective-permute-start(bf16[1,256,256]{2,1,0:T(8,128)(2,1)} %bitcast.11), channel_id=1, source_target_pairs={{0,16},{4,20},{8,24},{12,28},{16,0},{20,4},{24,8},{28,12},{1,17},{... | collective-permute-start | bytes 393224 | tf_op jit(solution)/shard_map/ppermute | solution.py:701
  13.3 6.1 %denominator.2 = (bf16[256,4096]{1,0:T(8,128)(2,1)S(1)}, f32[1,4096]{1,0:T(1,128)S(1)}, f32[2,128]{1,0:T(2,128)S(1)}) custom-call(s32[3]{0:T(128)S(1)} %pad_add_fusion.where_ref, bf16[256,256]{1,0:T(8,128)(2,1)S(1)} %copy-done, bf16[256,32768]{1,0:T(8,128)(2,1)} %raw_ref.1, bf16[256,32768]{1,0:T(8,128)(2,1)} %raw_ref.1), custom_call_target="tpu_custom_call" | custom-call | flops 1073741824 | bytes 4194304 | tf_op jit(solution)/shard_map/denominator/pallas_call | solution.py:165
  19.4 1.3 copy-done.2
  20.7 3.2 %collective-permute-done.1 = bf16[1,256,256]{2,1,0:T(8,128)(2,1)S(1)} collective-permute-done((bf16[1,256,256]{2,1,0:T(8,128)(2,1)}, bf16[1,256,256]{2,1,0:T(8,128)(2,1)S(1)}, u32[]{:S(2)}, u32[]{:S(2)}) %collective-permute-start.1) | collective-permute-done | bytes 131104 | tf_op jit(solution)/shard_map/ppermute | solution.py:701
  24.0 1.4 collective-permute-done.other_ref
  25.5 1.6 %copy-done.3 = bf16[256,4096]{1,0:T(8,128)(2,1)S(1)} copy-done((bf16[256,4096]{1,0:T(8,128)(2,1)S(1)}, bf16[256,4096]{1,0:T(8,128)(2,1)}, u32[]{:S(2)}) %copy-start.3) | copy-done | bytes 2097176
  27.1 3.8 %first_sweep.1 = (f32[32,10,128]{2,1,0:T(8,128)}, bf16[1024,256]{1,0:T(8,128)(2,1)S(1)}, f32[8,128]{1,0:T(8,128)}) custom-call(s32[3]{0:T(128)S(1)} %pad_add_fusion.where_ref, bf16[512,256]{1,0:T(8,128)(2,1)S(1)} %bitcast.19, bf16[512,256]{1,0:T(8,128)(2,1)S(1)} %collective-permute-done.other_ref, bf16[256,4096]{1,0:T(8,128)(2,1)S(1)} %copy-done.3, ...), custom_call_target="tpu_custom_call" | custom-call | flops 1073741824 | bytes 1572864 | tf_op jit(solution)/shard_map/first_sweep/pallas_call | solution.py:236
  30.9 1.9 %collective-permute-done.2 = bf16[2,256,256]{2,1,0:T(8,128)(2,1)S(1)} collective-permute-done((bf16[2,256,256]{2,1,0:T(8,128)(2,1)S(1)}, bf16[2,256,256]{2,1,0:T(8,128)(2,1)S(1)}, u32[]{:S(2)}, u32[]{:S(2)}) %collective-permute-start.2) | collective-permute-done | bytes 262176 | tf_op jit(solution)/shard_map/ppermute | solution.py:701
  32.8 1.5 collective-permute-start.3
  34.3 2.8 %all-to-all-start.1 = ((f32[32,10,128]{2,1,0:T(8,128)}), f32[32,10,128]{2,1,0:T(8,128)S(1)}, u32[]{:S(2)}, u32[]{:S(2)}) async-start(f32[32,10,128]{2,1,0:T(8,128)} %get-tuple-element.34), calls=%async_computation.1 | async-start | bytes 524288 | tf_op jit(solution)/shard_map/all_to_all | solution.py:650
  37.0 10.7 %denominator.3.far_ref = f32[2,128]{1,0:T(2,128)S(1)} custom-call(s32[3]{0:T(128)S(1)} %pad_add_fusion.where_ref, bf16[256,256]{1,0:T(8,128)(2,1)S(1)} %copy-done.1, bf16[256,32768]{1,0:T(8,128)(2,1)} %raw_ref.1), custom_call_target="tpu_custom_call" | custom-call | flops 3221225472 | bytes 12582912 | tf_op jit(solution)/shard_map/denominator/pallas_call | solution.py:165
  47.7 1.4 collective-permute-done.3
  49.2 1.1 pad_maximum_fusion
  50.4 1.6 %copy-done.4 = bf16[256,4096]{1,0:T(8,128)(2,1)S(1)} copy-done((bf16[256,4096]{1,0:T(8,128)(2,1)S(1)}, bf16[256,4096]{1,0:T(8,128)(2,1)}, u32[]{:S(2)}) %copy-start.4) | copy-done | bytes 2097176
  52.0 3.6 %second_sweep.1 = (f32[32,10,128]{2,1,0:T(8,128)}, f32[1,2048]{1,0:T(1,128)S(1)}) custom-call(s32[3]{0:T(128)S(1)} %pad_add_fusion.where_ref, bf16[1024,256]{1,0:T(8,128)(2,1)S(1)} %get-tuple-element.33.unit_ref.teacher_ref, bf16[256,4096]{1,0:T(8,128)(2,1)S(1)} %copy-done.4, f32[32,10,128]{2,1,0:T(8,128)S(1)} %all-to-all-done.1.came_ref.first_ref, ...), custom_call_target="tpu_custom_call" | custom-call | flops 1073741824 | bytes 1572864 | tf_op jit(solution)/shard_map/second_sweep/pallas_call | solution.py:236
  55.6 1.4 collective-permute-start.5
  57.0 3.9 %all-to-all-start.2 = ((f32[32,10,128]{2,1,0:T(8,128)}), f32[32,10,128]{2,1,0:T(8,128)S(1)}, u32[]{:S(2)}, u32[]{:S(2)}) async-start(f32[32,10,128]{2,1,0:T(8,128)} %get-tuple-element.37), calls=%async_computation.2 | async-start | bytes 524288 | tf_op jit(solution)/shard_map/all_to_all | solution.py:650
  61.0 7.7 %pair.1 = (bf16[2,2,2,1024,256]{4,3,2,1,0:T(8,128)(2,1)}, bf16[2,2,256,1024]{3,2,1,0:T(8,128)(2,1)}, bf16[4096,256]{1,0:T(8,128)(2,1)}) custom-call(s32[3]{0:T(128)S(1)} %pad_add_fusion.where_ref, bf16[4,2,256,256]{3,2,1,0:T(8,128)(2,1)S(1)} %bitcast.16, bf16[4,2,256,256]{3,2,1,0:T(8,128)(2,1)S(1)} %collective-permute-done.4.other_ref.other_raw_ref, ...), custom_call_target="tpu_custom_call" | custom-call | flops 2147483648 | bytes 8388608 | tf_op jit(solution)/shard_map/pair/pallas_call | solution.py:294
  68.7 2.7 %all-to-all-done.2.second_ref = f32[32,10,128]{2,1,0:T(8,128)S(1)} async-done(((f32[32,10,128]{2,1,0:T(8,128)}), f32[32,10,128]{2,1,0:T(8,128)S(1)}, u32[]{:S(2)}, u32[]{:S(2)}) %all-to-all-start.2) | async-done | bytes 163872 | tf_op jit(solution)/shard_map/all_to_all | solution.py:650
  71.4 25.6 %near_gradients.1 = (f32[1024,256]{1,0:T(8,128)S(1)}, f32[1024,256]{1,0:T(8,128)S(1)}, f32[256,4096]{1,0:T(8,128)}) custom-call(s32[3]{0:T(128)S(1)} %pad_add_fusion.where_ref, bf16[2,2,2,1024,256]{4,3,2,1,0:T(8,128)(2,1)} %get-tuple-element.46.both_ref, bf16[2,2,256,1024]{3,2,1,0:T(8,128)(2,1)} %get-tuple-element.47.turned_ref, ...), custom_call_target="tpu_custom_call" | custom-call | flops 17179869184 | bytes 8388608 | tf_op jit(solution)/shard_map/near_gradients/pallas_call | solution.py:468
  97.2 2.5 %collective-permute-done.6 = f32[1024,256]{1,0:T(8,128)S(1)} collective-permute-done((f32[1024,256]{1,0:T(8,128)S(1)}, f32[1024,256]{1,0:T(8,128)S(1)}, u32[]{:S(2)}, u32[]{:S(2)}) %collective-permute-start.6) | collective-permute-done | bytes 1048608 | tf_op jit(solution)/shard_map/ppermute | solution.py:646
  100.7 3.7 %all-to-all-start.3 = ((f16[8,128,256]{2,1,0:T(8,128)(2,1)}), f16[8,128,256]{2,1,0:T(8,128)(2,1)S(1)}, u32[]{:S(2)}, u32[]{:S(2)}) async-start(f16[8,128,256]{2,1,0:T(8,128)(2,1)} %bitcast.9), calls=%async_computation.3 | async-start | bytes 1048576 | tf_op jit(solution)/shard_map/all_to_all | solution.py:650
  104.4 1.6 %copy-done.5 = bf16[256,4096]{1,0:T(8,128)(2,1)S(1)} copy-done((bf16[256,4096]{1,0:T(8,128)(2,1)S(1)}, bf16[256,4096]{1,0:T(8,128)(2,1)}, u32[]{:S(2)}) %copy-start.5) | copy-done | bytes 2097176
  106.0 1.6 %copy-done.9 = bf16[2,2,256,1024]{3,2,1,0:T(8,128)(2,1)S(1)} copy-done((bf16[2,2,256,1024]{3,2,1,0:T(8,128)(2,1)S(1)}, bf16[2,2,256,1024]{3,2,1,0:T(8,128)(2,1)}, u32[]{:S(2)}) %copy-start.9) | copy-done | bytes 2097176
  107.6 21.7 %far_gradients.1 = f32[128,4352]{1,0:T(8,128)S(1)} custom-call(s32[3]{0:T(128)S(1)} %pad_add_fusion.where_ref, bf16[2,2,2,1024,256]{4,3,2,1,0:T(8,128)(2,1)} %get-tuple-element.46.both_ref, bf16[2,2,256,1024]{3,2,1,0:T(8,128)(2,1)S(1)} %copy-done.9, f32[32,10,128]{2,1,0:T(8,128)S(1)} %all-to-all-done.1.came_ref.first_ref, ...), custom_call_target="tpu_custom_call" | custom-call | flops 12884901888 | bytes 8388608 | tf_op jit(solution)/shard_map/far_gradients/pallas_call | solution.py:579
  130.4 3.9 %all-to-all-start.4 = ((f16[8,16,4352]{2,1,0:T(8,128)(2,1)}), f16[8,16,4352]{2,1,0:T(8,128)(2,1)S(1)}, u32[]{:S(2)}, u32[]{:S(2)}) async-start(f16[8,16,4352]{2,1,0:T(8,128)(2,1)} %bitcast.10), calls=%async_computation.4 | async-start | bytes 2228224 | tf_op jit(solution)/shard_map/all_to_all | solution.py:650
  134.5 1.5 %collective-permute-start.7 = (f32[128,256]{1,0:T(8,128)S(1)}, f32[128,256]{1,0:T(8,128)S(1)}, u32[]{:S(2)}, u32[]{:S(2)}) collective-permute-start(f32[128,256]{1,0:T(8,128)S(1)} %broadcast_multiply_fusion), channel_id=1, source_target_pairs={{0,1},{1,0},{2,3},{3,2},{4,5},{5,4},{6,7},{7,6},{8,9},{9,8},{10,11... | collective-permute-start | bytes 393224 | tf_op jit(solution)/shard_map/ppermute | solution.py:646
  136.0 4.4 %collective-permute-done.7 = f32[128,256]{1,0:T(8,128)S(1)} collective-permute-done((f32[128,256]{1,0:T(8,128)S(1)}, f32[128,256]{1,0:T(8,128)S(1)}, u32[]{:S(2)}, u32[]{:S(2)}) %collective-permute-start.7) | collective-permute-done | bytes 131104 | tf_op jit(solution)/shard_map/ppermute | solution.py:646
  141.3 8.1 %all-to-all-done.4 = f16[8,16,4352]{2,1,0:T(8,128)(2,1)S(1)} async-done(((f16[8,16,4352]{2,1,0:T(8,128)(2,1)}), f16[8,16,4352]{2,1,0:T(8,128)(2,1)S(1)}, u32[]{:S(2)}, u32[]{:S(2)}) %all-to-all-start.4) | async-done | bytes 1114144 | tf_op jit(solution)/shard_map/all_to_all | solution.py:650
  149.6 1.9 %join.1 = f32[16,32768]{1,0:T(8,128)} custom-call(f32[8,16,4352]{2,1,0:T(8,128)S(1)} %convert_element_type.19.came_ref), custom_call_target="tpu_custom_call" | custom-call | flops 524288 | bytes 4194304 | tf_op jit(solution)/shard_map/join/pallas_call | solution.py:629
  (38 shorter events, 4.7 us)
Async XLA Ops:
  2.1 21.8 %all-to-all-start = ((bf16[8,64,256]{2,1,0:T(8,128)(2,1)}), bf16[8,64,256]{2,1,0:T(8,128)(2,1)S(1)}, u32[]{:S(2)}, u32[]{:S(2)}) async-start(bf16[8,64,256]{2,1,0:T(8,128)(2,1)} %tile.4), calls=%async_computation | async-start | bytes 524288 | tf_op jit(solution)/shard_map/all_to_all | solution.py:650
  9.4 14.5 %collective-permute-start.1 = (bf16[1,256,256]{2,1,0:T(8,128)(2,1)}, bf16[1,256,256]{2,1,0:T(8,128)(2,1)S(1)}, u32[]{:S(2)}, u32[]{:S(2)}) collective-permute-start(bf16[1,256,256]{2,1,0:T(8,128)(2,1)} %bitcast.11), channel_id=1, source_target_pairs={{0,16},{4,20},{8,24},{12,28},{16,0},{20,4},{24,8},{28,12},{1,17},{... | collective-permute-start | bytes 393224 | tf_op jit(solution)/shard_map/ppermute | solution.py:701
  12.4 0.9 copy-start
  13.3 10.6 %copy-start.1 = (bf16[256,256]{1,0:T(8,128)(2,1)S(1)}, bf16[256,256]{1,0:T(8,128)(2,1)}, u32[]{:S(2)}) copy-start(bf16[256,256]{1,0:T(8,128)(2,1)} %students_ref.3) | copy-start | bytes 393220
  13.3 12.2 %copy-start.7 = (s32[256]{0:T(256)S(1)}, s32[256]{0:T(256)}, u32[]{:S(2)}) copy-start(s32[256]{0:T(256)} %param.8) | copy-start | bytes 3076
  13.3 12.2 %copy-start.8 = (s32[256]{0:T(256)S(1)}, s32[256]{0:T(256)}, u32[]{:S(2)}) copy-start(s32[256]{0:T(256)} %param.9) | copy-start | bytes 3076
  19.4 1.3 copy-start.2
  23.9 1.5 %collective-permute-start = (bf16[512,256]{1,0:T(8,128)(2,1)S(1)}, bf16[512,256]{1,0:T(8,128)(2,1)S(1)}, u32[]{:S(2)}, u32[]{:S(2)}) collective-permute-start(bf16[512,256]{1,0:T(8,128)(2,1)S(1)} %bitcast.18), channel_id=1, source_target_pairs={{0,2},{2,0},{1,3},{3,1},{4,6},{6,4},{5,7},{7,5},{8,10},{10,8},{9,1... | collective-permute-start | bytes 786440 | tf_op jit(solution)/shard_map/ppermute | solution.py:646
  24.0 8.8 %collective-permute-start.2 = (bf16[2,256,256]{2,1,0:T(8,128)(2,1)S(1)}, bf16[2,256,256]{2,1,0:T(8,128)(2,1)S(1)}, u32[]{:S(2)}, u32[]{:S(2)}) collective-permute-start(bf16[2,256,256]{2,1,0:T(8,128)(2,1)S(1)} %pad_maximum_fusion.2), channel_id=1, source_target_pairs={{0,8},{4,12},{8,0},{12,4},{16,24},{20,28},{24,16},{28,20},{1,9},{5... | collective-permute-start | bytes 786440 | tf_op jit(solution)/shard_map/ppermute | solution.py:701
  25.5 1.6 %copy-start.3 = (bf16[256,4096]{1,0:T(8,128)(2,1)S(1)}, bf16[256,4096]{1,0:T(8,128)(2,1)}, u32[]{:S(2)}) copy-start(bf16[256,4096]{1,0:T(8,128)(2,1)} %copy-done.2) | copy-start | bytes 6291460
  32.8 16.4 %collective-permute-start.3 = (bf16[4,256,256]{2,1,0:T(8,128)(2,1)S(1)}, bf16[4,256,256]{2,1,0:T(8,128)(2,1)}, u32[]{:S(2)}, u32[]{:S(2)}) collective-permute-start(bf16[4,256,256]{2,1,0:T(8,128)(2,1)S(1)} %pad_maximum_fusion.1), channel_id=1, source_target_pairs={{0,4},{4,0},{8,12},{12,8},{16,20},{20,16},{24,28},{28,24},{1,5},{5... | collective-permute-start | bytes 1572872 | tf_op jit(solution)/shard_map/ppermute | solution.py:701
  34.3 16.1 %all-to-all-start.1 = ((f32[32,10,128]{2,1,0:T(8,128)}), f32[32,10,128]{2,1,0:T(8,128)S(1)}, u32[]{:S(2)}, u32[]{:S(2)}) async-start(f32[32,10,128]{2,1,0:T(8,128)} %get-tuple-element.34), calls=%async_computation.1 | async-start | bytes 524288 | tf_op jit(solution)/shard_map/all_to_all | solution.py:650
  50.3 10.7 %collective-permute-start.4 = (bf16[4,2,256,256]{3,2,1,0:T(8,128)(2,1)S(1)}, bf16[4,2,256,256]{3,2,1,0:T(8,128)(2,1)S(1)}, u32[]{:S(2)}, u32[]{:S(2)}) collective-permute-start(bf16[4,2,256,256]{3,2,1,0:T(8,128)(2,1)S(1)} %bitcast.15), channel_id=1, source_target_pairs={{0,2},{2,0},{1,3},{3,1},{4,6},{6,4},{5,7},{7,5},{8,10},{10,8},{9,1... | collective-permute-start | bytes 3145736 | tf_op jit(solution)/shard_map/ppermute | solution.py:646
  50.4 1.6 %copy-start.4 = (bf16[256,4096]{1,0:T(8,128)(2,1)S(1)}, bf16[256,4096]{1,0:T(8,128)(2,1)}, u32[]{:S(2)}) copy-start(bf16[256,4096]{1,0:T(8,128)(2,1)} %copy-done.2) | copy-start | bytes 6291460
  55.6 5.3 %collective-permute-start.5 = (f32[1,2048]{1,0:T(1,128)S(1)}, f32[1,2048]{1,0:T(1,128)S(1)}, u32[]{:S(2)}, u32[]{:S(2)}) collective-permute-start(f32[1,2048]{1,0:T(1,128)S(1)} %get-tuple-element.49), channel_id=1, source_target_pairs={{0,16},{16,0},{1,17},{17,1},{2,18},{18,2},{3,19},{19,3},{4,20},{20... | collective-permute-start | bytes 24584 | tf_op jit(solution)/shard_map/ppermute | solution.py:732
  57.0 14.4 %all-to-all-start.2 = ((f32[32,10,128]{2,1,0:T(8,128)}), f32[32,10,128]{2,1,0:T(8,128)S(1)}, u32[]{:S(2)}, u32[]{:S(2)}) async-start(f32[32,10,128]{2,1,0:T(8,128)} %get-tuple-element.37), calls=%async_computation.2 | async-start | bytes 524288 | tf_op jit(solution)/shard_map/all_to_all | solution.py:650
  61.0 7.7 %copy-start.6 = (bf16[4,2,256,256]{3,2,1,0:T(8,128)(2,1)}, bf16[4,2,256,256]{3,2,1,0:T(8,128)(2,1)S(1)}, u32[]{:S(2)}) copy-start(bf16[4,2,256,256]{3,2,1,0:T(8,128)(2,1)S(1)} %collective-permute-done.4.other_ref.other_raw_ref) | copy-start | bytes 3145732
  97.1 2.7 %collective-permute-start.6 = (f32[1024,256]{1,0:T(8,128)S(1)}, f32[1024,256]{1,0:T(8,128)S(1)}, u32[]{:S(2)}, u32[]{:S(2)}) collective-permute-start(f32[1024,256]{1,0:T(8,128)S(1)} %get-tuple-element.52), channel_id=1, source_target_pairs={{0,2},{2,0},{1,3},{3,1},{4,6},{6,4},{5,7},{7,5},{8,10},{10,8},{9,1... | collective-permute-start | bytes 3145736 | tf_op jit(solution)/shard_map/ppermute | solution.py:646
  100.7 29.7 %all-to-all-start.3 = ((f16[8,128,256]{2,1,0:T(8,128)(2,1)}), f16[8,128,256]{2,1,0:T(8,128)(2,1)S(1)}, u32[]{:S(2)}, u32[]{:S(2)}) async-start(f16[8,128,256]{2,1,0:T(8,128)(2,1)} %bitcast.9), calls=%async_computation.3 | async-start | bytes 1048576 | tf_op jit(solution)/shard_map/all_to_all | solution.py:650
  104.4 1.6 %copy-start.5 = (bf16[256,4096]{1,0:T(8,128)(2,1)S(1)}, bf16[256,4096]{1,0:T(8,128)(2,1)}, u32[]{:S(2)}) copy-start(bf16[256,4096]{1,0:T(8,128)(2,1)} %copy-done.2) | copy-start | bytes 6291460
  106.0 1.6 %copy-start.9 = (bf16[2,2,256,1024]{3,2,1,0:T(8,128)(2,1)S(1)}, bf16[2,2,256,1024]{3,2,1,0:T(8,128)(2,1)}, u32[]{:S(2)}) copy-start(bf16[2,2,256,1024]{3,2,1,0:T(8,128)(2,1)} %get-tuple-element.47.turned_ref) | copy-start | bytes 6291460
  130.4 19.1 %all-to-all-start.4 = ((f16[8,16,4352]{2,1,0:T(8,128)(2,1)}), f16[8,16,4352]{2,1,0:T(8,128)(2,1)S(1)}, u32[]{:S(2)}, u32[]{:S(2)}) async-start(f16[8,16,4352]{2,1,0:T(8,128)(2,1)} %bitcast.10), calls=%async_computation.4 | async-start | bytes 2228224 | tf_op jit(solution)/shard_map/all_to_all | solution.py:650
  134.5 6.0 %collective-permute-start.7 = (f32[128,256]{1,0:T(8,128)S(1)}, f32[128,256]{1,0:T(8,128)S(1)}, u32[]{:S(2)}, u32[]{:S(2)}) collective-permute-start(f32[128,256]{1,0:T(8,128)S(1)} %broadcast_multiply_fusion), channel_id=1, source_target_pairs={{0,1},{1,0},{2,3},{3,2},{4,5},{5,4},{6,7},{7,6},{8,9},{9,8},{10,11... | collective-permute-start | bytes 393224 | tf_op jit(solution)/shard_map/ppermute | solution.py:646

commit v5 on v4

--- a/solution.py
+++ b/solution.py
@@ -741,9 +741,13 @@
     own_part, other_part, proto_all = near_gradients(
         plan, where, *rows_of, flipped, stu_own, stu_other
     )
-    summed = (own_part + swap(other_part, "core")) * 128.0
-    sent = summed.astype(F16).reshape(chips * protos, stu_count // protos, width)
-    came = exchange(sent, ("chip", "protos"))
+    split = (chips, 1, protos, stu_count // protos, width)
+    sides = [
+        jnp.where(core == side, own_part, other_part).reshape(split) for side in range(2)
+    ]
+    sent = (jnp.concatenate(sides, 1) * 128.0).astype(F16)
+    sent = sent.reshape(chips * 2 * protos, stu_count // protos, width)
+    came = exchange(sent, ("chip", "core", "protos"))
     proto_part = far_gradients(plan, tie(where, sent), *rows_of, prototypes, norm, proto_all)
     share = width // (all_chips * 2)
     sent = proto_part.astype(F16).reshape(chips * 2, share, -1)

time: 152 us -> 150 us (0.987)
  waiting for transfers between devices: 25.8 us -> 23.9 us
    ppermute x4 -> x3, waiting for transfers between devices: 8.39 us -> 1.42 us  [swap(): return lax.ppermute(value, axis, [(0, 1), (1, 0)])]
    all_to_all x5, waiting for transfers between devices: 10.9 us -> 16.1 us  [exchange(): return lax.all_to_all(value, axes, split_axis=0, concat_axis=0, tiled=True)]
  transfers between devices with their start and end apart: 13 -> 12, of which waited for: 8 -> 6; matrix products, arithmetic and copies ran while one was open for 2% -> 1% of each run, Pallas kernels for 35% -> 37%
where the time goes in v5:
time: 150 us; the launch traced here: 149 us
  Pallas kernels  81.1 us (54%)
  starting transfers between devices  29.2 us (19%)
  waiting for transfers between devices  23.9 us (16%)
  local copies, waits for them, and re-layouts  10.1 us (7%)
  other arithmetic  4.03 us (3%)
    pallas_call x1, Pallas kernels, near_gradients(): pl.pallas_call(functools.partial(near_kernel, plan=plan, sub=tile_of(each...  25.7 us
    pallas_call x1, Pallas kernels, far_gradients(): pl.pallas_call(functools.partial(far_kernel, plan=plan, sub=tile_of(each,...  21.7 us
    all_to_all x5, starting transfers between devices, exchange(): return lax.all_to_all(value, axes, split_axis=0, concat_axis=0, tiled=True)  21.6 us
    pallas_call x2, Pallas kernels, local_denominator(): pl.pallas_call(functools.partial(denominator_kernel, sub=tile_of(tile, 51...  16.7 us
    all_to_all x5, waiting for transfers between devices, exchange(): return lax.all_to_all(value, axes, split_axis=0, concat_axis=0, tiled=True)  16.1 us
    unnamed x20, local copies, waits for them, and re-layouts  8.59 us
    pallas_call x1, Pallas kernels, pair(): pl.pallas_call(functools.partial(pair_kernel, plan=plan), out_shape=[jax....  7.72 us
    pallas_call x2, Pallas kernels, sweep_call(): pl.pallas_call(functools.partial(kernel, plan=plan, sub=tile_of(columns,...  7.43 us
  transfers between devices with their start and end apart: 12, of which 6 were waited for; matrix products, arithmetic and copies ran while one was open for 1% of the time, Pallas kernels for 37%

profile of v5, /device:TPU:0, one launch (start us, length us, event | category | flops | bytes accessed | tf_op | source)
XLA Modules:
  0.0 149.2 jit_solution(6870550502794158541)
XLA Ops:
  0.6 1.5 tile.4
  2.1 7.3 %all-to-all-start = ((bf16[8,64,256]{2,1,0:T(8,128)(2,1)}), bf16[8,64,256]{2,1,0:T(8,128)(2,1)S(1)}, u32[]{:S(2)}, u32[]{:S(2)}) async-start(bf16[8,64,256]{2,1,0:T(8,128)(2,1)} %tile.4), calls=%async_computation | async-start | bytes 524288 | tf_op jit(solution)/shard_map/all_to_all | solution.py:650
  9.4 2.9 %collective-permute-start.1 = (bf16[1,256,256]{2,1,0:T(8,128)(2,1)}, bf16[1,256,256]{2,1,0:T(8,128)(2,1)S(1)}, u32[]{:S(2)}, u32[]{:S(2)}) collective-permute-start(bf16[1,256,256]{2,1,0:T(8,128)(2,1)} %bitcast.17), channel_id=1, source_target_pairs={{0,16},{4,20},{8,24},{12,28},{16,0},{20,4},{24,8},{28,12},{1,17},{... | collective-permute-start | bytes 393224 | tf_op jit(solution)/shard_map/ppermute | solution.py:701
  12.4 0.9 copy-done
  13.3 6.1 %denominator.2 = (bf16[256,4096]{1,0:T(8,128)(2,1)S(1)}, f32[1,4096]{1,0:T(1,128)S(1)}, f32[2,128]{1,0:T(2,128)S(1)}) custom-call(s32[3]{0:T(128)S(1)} %pad_add_fusion.where_ref, bf16[256,256]{1,0:T(8,128)(2,1)S(1)} %copy-done, bf16[256,32768]{1,0:T(8,128)(2,1)} %raw_ref.1, bf16[256,32768]{1,0:T(8,128)(2,1)} %raw_ref.1), custom_call_target="tpu_custom_call" | custom-call | flops 1073741824 | bytes 4194304 | tf_op jit(solution)/shard_map/denominator/pallas_call | solution.py:165
  19.4 1.3 copy-done.2
  20.7 3.2 %collective-permute-done.1 = bf16[1,256,256]{2,1,0:T(8,128)(2,1)S(1)} collective-permute-done((bf16[1,256,256]{2,1,0:T(8,128)(2,1)}, bf16[1,256,256]{2,1,0:T(8,128)(2,1)S(1)}, u32[]{:S(2)}, u32[]{:S(2)}) %collective-permute-start.1) | collective-permute-done | bytes 131104 | tf_op jit(solution)/shard_map/ppermute | solution.py:701
  24.0 1.4 collective-permute-done.other_ref
  25.5 1.6 %copy-done.3 = bf16[256,4096]{1,0:T(8,128)(2,1)S(1)} copy-done((bf16[256,4096]{1,0:T(8,128)(2,1)S(1)}, bf16[256,4096]{1,0:T(8,128)(2,1)}, u32[]{:S(2)}) %copy-start.3) | copy-done | bytes 2097176
  27.1 3.8 %first_sweep.1 = (f32[32,10,128]{2,1,0:T(8,128)}, bf16[1024,256]{1,0:T(8,128)(2,1)S(1)}, f32[8,128]{1,0:T(8,128)}) custom-call(s32[3]{0:T(128)S(1)} %pad_add_fusion.where_ref, bf16[512,256]{1,0:T(8,128)(2,1)S(1)} %bitcast.25, bf16[512,256]{1,0:T(8,128)(2,1)S(1)} %collective-permute-done.other_ref, bf16[256,4096]{1,0:T(8,128)(2,1)S(1)} %copy-done.3, ...), custom_call_target="tpu_custom_call" | custom-call | flops 1073741824 | bytes 1572864 | tf_op jit(solution)/shard_map/first_sweep/pallas_call | solution.py:236
  30.8 1.9 %collective-permute-done.2 = bf16[2,256,256]{2,1,0:T(8,128)(2,1)S(1)} collective-permute-done((bf16[2,256,256]{2,1,0:T(8,128)(2,1)S(1)}, bf16[2,256,256]{2,1,0:T(8,128)(2,1)S(1)}, u32[]{:S(2)}, u32[]{:S(2)}) %collective-permute-start.2) | collective-permute-done | bytes 262176 | tf_op jit(solution)/shard_map/ppermute | solution.py:701
  32.8 1.5 collective-permute-start.3
  34.3 2.8 %all-to-all-start.1 = ((f32[32,10,128]{2,1,0:T(8,128)}), f32[32,10,128]{2,1,0:T(8,128)S(1)}, u32[]{:S(2)}, u32[]{:S(2)}) async-start(f32[32,10,128]{2,1,0:T(8,128)} %get-tuple-element.34), calls=%async_computation.1 | async-start | bytes 524288 | tf_op jit(solution)/shard_map/all_to_all | solution.py:650
  37.0 10.7 %denominator.3.far_ref = f32[2,128]{1,0:T(2,128)S(1)} custom-call(s32[3]{0:T(128)S(1)} %pad_add_fusion.where_ref, bf16[256,256]{1,0:T(8,128)(2,1)S(1)} %copy-done.1, bf16[256,32768]{1,0:T(8,128)(2,1)} %raw_ref.1), custom_call_target="tpu_custom_call" | custom-call | flops 3221225472 | bytes 12582912 | tf_op jit(solution)/shard_map/denominator/pallas_call | solution.py:165
  47.7 1.3 collective-permute-done.3
  49.3 1.6 %copy-done.4 = bf16[256,4096]{1,0:T(8,128)(2,1)S(1)} copy-done((bf16[256,4096]{1,0:T(8,128)(2,1)S(1)}, bf16[256,4096]{1,0:T(8,128)(2,1)}, u32[]{:S(2)}) %copy-start.4) | copy-done | bytes 2097176
  50.8 3.6 %second_sweep.1 = (f32[32,10,128]{2,1,0:T(8,128)}, f32[1,2048]{1,0:T(1,128)S(1)}) custom-call(s32[3]{0:T(128)S(1)} %pad_add_fusion.where_ref, bf16[1024,256]{1,0:T(8,128)(2,1)S(1)} %get-tuple-element.33.unit_ref.teacher_ref, bf16[256,4096]{1,0:T(8,128)(2,1)S(1)} %copy-done.4, f32[32,10,128]{2,1,0:T(8,128)S(1)} %all-to-all-done.1.came_ref.first_ref, ...), custom_call_target="tpu_custom_call" | custom-call | flops 1073741824 | bytes 1572864 | tf_op jit(solution)/shard_map/second_sweep/pallas_call | solution.py:236
  54.5 1.5 collective-permute-start.5
  56.0 3.9 %all-to-all-start.2 = ((f32[32,10,128]{2,1,0:T(8,128)}), f32[32,10,128]{2,1,0:T(8,128)S(1)}, u32[]{:S(2)}, u32[]{:S(2)}) async-start(f32[32,10,128]{2,1,0:T(8,128)} %get-tuple-element.37), calls=%async_computation.2 | async-start | bytes 524288 | tf_op jit(solution)/shard_map/all_to_all | solution.py:650
  60.0 7.7 %pair.1 = (bf16[2,2,2,1024,256]{4,3,2,1,0:T(8,128)(2,1)}, bf16[2,2,256,1024]{3,2,1,0:T(8,128)(2,1)}, bf16[4096,256]{1,0:T(8,128)(2,1)}) custom-call(s32[3]{0:T(128)S(1)} %pad_add_fusion.where_ref, bf16[4,2,256,256]{3,2,1,0:T(8,128)(2,1)S(1)} %bitcast.22, bf16[4,2,256,256]{3,2,1,0:T(8,128)(2,1)S(1)} %collective-permute-done.4.other_ref.other_raw_ref, ...), custom_call_target="tpu_custom_call" | custom-call | flops 2147483648 | bytes 8388608 | tf_op jit(solution)/shard_map/pair/pallas_call | solution.py:294
  67.7 2.7 %all-to-all-done.2.second_ref = f32[32,10,128]{2,1,0:T(8,128)S(1)} async-done(((f32[32,10,128]{2,1,0:T(8,128)}), f32[32,10,128]{2,1,0:T(8,128)S(1)}, u32[]{:S(2)}, u32[]{:S(2)}) %all-to-all-start.2) | async-done | bytes 163872 | tf_op jit(solution)/shard_map/all_to_all | solution.py:650
  70.4 25.7 %near_gradients.1 = (f32[1024,256]{1,0:T(8,128)S(1)}, f32[1024,256]{1,0:T(8,128)S(1)}, f32[256,4096]{1,0:T(8,128)}) custom-call(s32[3]{0:T(128)S(1)} %pad_add_fusion.where_ref, bf16[2,2,2,1024,256]{4,3,2,1,0:T(8,128)(2,1)} %get-tuple-element.46.both_ref, bf16[2,2,256,1024]{3,2,1,0:T(8,128)(2,1)} %get-tuple-element.47.turned_ref, ...), custom_call_target="tpu_custom_call" | custom-call | flops 17179869184 | bytes 8388608 | tf_op jit(solution)/shard_map/near_gradients/pallas_call | solution.py:468
  96.2 1.2 fusion
  97.4 3.9 %all-to-all-start.3 = ((f16[16,128,256]{2,1,0:T(8,128)(2,1)}), f16[16,128,256]{2,1,0:T(8,128)(2,1)S(1)}, u32[]{:S(2)}, u32[]{:S(2)}) async-start(f16[16,128,256]{2,1,0:T(8,128)(2,1)} %bitcast.13), calls=%async_computation.3 | async-start | bytes 2097152 | tf_op jit(solution)/shard_map/all_to_all | solution.py:650
  101.3 1.6 %copy-done.5 = bf16[256,4096]{1,0:T(8,128)(2,1)S(1)} copy-done((bf16[256,4096]{1,0:T(8,128)(2,1)S(1)}, bf16[256,4096]{1,0:T(8,128)(2,1)}, u32[]{:S(2)}) %copy-start.5) | copy-done | bytes 2097176
  102.9 1.6 %copy-done.9 = bf16[2,2,256,1024]{3,2,1,0:T(8,128)(2,1)S(1)} copy-done((bf16[2,2,256,1024]{3,2,1,0:T(8,128)(2,1)S(1)}, bf16[2,2,256,1024]{3,2,1,0:T(8,128)(2,1)}, u32[]{:S(2)}) %copy-start.9) | copy-done | bytes 2097176
  104.5 21.7 %far_gradients.1 = f32[128,4352]{1,0:T(8,128)S(1)} custom-call(s32[3]{0:T(128)S(1)} %pad_add_fusion.where_ref, bf16[2,2,2,1024,256]{4,3,2,1,0:T(8,128)(2,1)} %get-tuple-element.46.both_ref, bf16[2,2,256,1024]{3,2,1,0:T(8,128)(2,1)S(1)} %copy-done.9, f32[32,10,128]{2,1,0:T(8,128)S(1)} %all-to-all-done.1.came_ref.first_ref, ...), custom_call_target="tpu_custom_call" | custom-call | flops 12884901888 | bytes 8388608 | tf_op jit(solution)/shard_map/far_gradients/pallas_call | solution.py:579
  126.2 1.1 convert_element_type.23
  127.3 3.8 %all-to-all-start.4 = ((f16[8,16,4352]{2,1,0:T(8,128)(2,1)}), f16[8,16,4352]{2,1,0:T(8,128)(2,1)S(1)}, u32[]{:S(2)}, u32[]{:S(2)}) async-start(f16[8,16,4352]{2,1,0:T(8,128)(2,1)} %bitcast.14), calls=%async_computation.4 | async-start | bytes 2228224 | tf_op jit(solution)/shard_map/all_to_all | solution.py:650
  131.4 1.5 %collective-permute-start.6 = (f32[128,256]{1,0:T(8,128)S(1)}, f32[128,256]{1,0:T(8,128)S(1)}, u32[]{:S(2)}, u32[]{:S(2)}) collective-permute-start(f32[128,256]{1,0:T(8,128)S(1)} %broadcast_multiply_fusion), channel_id=1, source_target_pairs={{0,1},{1,0},{2,3},{3,2},{4,5},{5,4},{6,7},{7,6},{8,9},{9,8},{10,11... | collective-permute-start | bytes 393224 | tf_op jit(solution)/shard_map/ppermute | solution.py:646
  133.0 13.3 %all-to-all-done.4 = f16[8,16,4352]{2,1,0:T(8,128)(2,1)S(1)} async-done(((f16[8,16,4352]{2,1,0:T(8,128)(2,1)}), f16[8,16,4352]{2,1,0:T(8,128)(2,1)S(1)}, u32[]{:S(2)}, u32[]{:S(2)}) %all-to-all-start.4) | async-done | bytes 1114144 | tf_op jit(solution)/shard_map/all_to_all | solution.py:650
  146.5 1.9 %join.1 = f32[16,32768]{1,0:T(8,128)} custom-call(f32[8,16,4352]{2,1,0:T(8,128)S(1)} %convert_element_type.24.came_ref), custom_call_target="tpu_custom_call" | custom-call | flops 524288 | bytes 4194304 | tf_op jit(solution)/shard_map/join/pallas_call | solution.py:629
  (37 shorter events, 1.9 us)
Async XLA Ops:
  2.1 21.8 %all-to-all-start = ((bf16[8,64,256]{2,1,0:T(8,128)(2,1)}), bf16[8,64,256]{2,1,0:T(8,128)(2,1)S(1)}, u32[]{:S(2)}, u32[]{:S(2)}) async-start(bf16[8,64,256]{2,1,0:T(8,128)(2,1)} %tile.4), calls=%async_computation | async-start | bytes 524288 | tf_op jit(solution)/shard_map/all_to_all | solution.py:650
  9.4 14.5 %collective-permute-start.1 = (bf16[1,256,256]{2,1,0:T(8,128)(2,1)}, bf16[1,256,256]{2,1,0:T(8,128)(2,1)S(1)}, u32[]{:S(2)}, u32[]{:S(2)}) collective-permute-start(bf16[1,256,256]{2,1,0:T(8,128)(2,1)} %bitcast.17), channel_id=1, source_target_pairs={{0,16},{4,20},{8,24},{12,28},{16,0},{20,4},{24,8},{28,12},{1,17},{... | collective-permute-start | bytes 393224 | tf_op jit(solution)/shard_map/ppermute | solution.py:701
  12.4 0.9 copy-start
  13.3 10.6 %copy-start.1 = (bf16[256,256]{1,0:T(8,128)(2,1)S(1)}, bf16[256,256]{1,0:T(8,128)(2,1)}, u32[]{:S(2)}) copy-start(bf16[256,256]{1,0:T(8,128)(2,1)} %students_ref.3) | copy-start | bytes 393220
  13.3 12.2 %copy-start.7 = (s32[256]{0:T(256)S(1)}, s32[256]{0:T(256)}, u32[]{:S(2)}) copy-start(s32[256]{0:T(256)} %param.8) | copy-start | bytes 3076
  13.3 12.2 %copy-start.8 = (s32[256]{0:T(256)S(1)}, s32[256]{0:T(256)}, u32[]{:S(2)}) copy-start(s32[256]{0:T(256)} %param.9) | copy-start | bytes 3076
  19.4 1.3 copy-start.2
  23.9 1.5 %collective-permute-start = (bf16[512,256]{1,0:T(8,128)(2,1)S(1)}, bf16[512,256]{1,0:T(8,128)(2,1)S(1)}, u32[]{:S(2)}, u32[]{:S(2)}) collective-permute-start(bf16[512,256]{1,0:T(8,128)(2,1)S(1)} %bitcast.24), channel_id=1, source_target_pairs={{0,2},{2,0},{1,3},{3,1},{4,6},{6,4},{5,7},{7,5},{8,10},{10,8},{9,1... | collective-permute-start | bytes 786440 | tf_op jit(solution)/shard_map/ppermute | solution.py:646
  24.0 8.8 %collective-permute-start.2 = (bf16[2,256,256]{2,1,0:T(8,128)(2,1)S(1)}, bf16[2,256,256]{2,1,0:T(8,128)(2,1)S(1)}, u32[]{:S(2)}, u32[]{:S(2)}) collective-permute-start(bf16[2,256,256]{2,1,0:T(8,128)(2,1)S(1)} %pad_maximum_fusion.2), channel_id=1, source_target_pairs={{0,8},{4,12},{8,0},{12,4},{16,24},{20,28},{24,16},{28,20},{1,9},{5... | collective-permute-start | bytes 786440 | tf_op jit(solution)/shard_map/ppermute | solution.py:701
  25.5 1.6 %copy-start.3 = (bf16[256,4096]{1,0:T(8,128)(2,1)S(1)}, bf16[256,4096]{1,0:T(8,128)(2,1)}, u32[]{:S(2)}) copy-start(bf16[256,4096]{1,0:T(8,128)(2,1)} %copy-done.2) | copy-start | bytes 6291460
  32.8 16.2 %collective-permute-start.3 = (bf16[4,256,256]{2,1,0:T(8,128)(2,1)S(1)}, bf16[4,256,256]{2,1,0:T(8,128)(2,1)S(1)}, u32[]{:S(2)}, u32[]{:S(2)}) collective-permute-start(bf16[4,256,256]{2,1,0:T(8,128)(2,1)S(1)} %pad_maximum_fusion.1), channel_id=1, source_target_pairs={{0,4},{4,0},{8,12},{12,8},{16,20},{20,16},{24,28},{28,24},{1,5},{5... | collective-permute-start | bytes 1572872 | tf_op jit(solution)/shard_map/ppermute | solution.py:701
  34.3 15.0 %all-to-all-start.1 = ((f32[32,10,128]{2,1,0:T(8,128)}), f32[32,10,128]{2,1,0:T(8,128)S(1)}, u32[]{:S(2)}, u32[]{:S(2)}) async-start(f32[32,10,128]{2,1,0:T(8,128)} %get-tuple-element.34), calls=%async_computation.1 | async-start | bytes 524288 | tf_op jit(solution)/shard_map/all_to_all | solution.py:650
  49.2 10.8 %collective-permute-start.4 = (bf16[4,2,256,256]{3,2,1,0:T(8,128)(2,1)S(1)}, bf16[4,2,256,256]{3,2,1,0:T(8,128)(2,1)S(1)}, u32[]{:S(2)}, u32[]{:S(2)}) collective-permute-start(bf16[4,2,256,256]{3,2,1,0:T(8,128)(2,1)S(1)} %bitcast.21), channel_id=1, source_target_pairs={{0,2},{2,0},{1,3},{3,1},{4,6},{6,4},{5,7},{7,5},{8,10},{10,8},{9,1... | collective-permute-start | bytes 3145736 | tf_op jit(solution)/shard_map/ppermute | solution.py:646
  49.2 1.6 %copy-start.4 = (bf16[256,4096]{1,0:T(8,128)(2,1)S(1)}, bf16[256,4096]{1,0:T(8,128)(2,1)}, u32[]{:S(2)}) copy-start(bf16[256,4096]{1,0:T(8,128)(2,1)} %copy-done.2) | copy-start | bytes 6291460
  54.5 5.4 %collective-permute-start.5 = (f32[1,2048]{1,0:T(1,128)S(1)}, f32[1,2048]{1,0:T(1,128)S(1)}, u32[]{:S(2)}, u32[]{:S(2)}) collective-permute-start(f32[1,2048]{1,0:T(1,128)S(1)} %get-tuple-element.49), channel_id=1, source_target_pairs={{0,16},{16,0},{1,17},{17,1},{2,18},{18,2},{3,19},{19,3},{4,20},{20... | collective-permute-start | bytes 24584 | tf_op jit(solution)/shard_map/ppermute | solution.py:732
  56.0 14.4 %all-to-all-start.2 = ((f32[32,10,128]{2,1,0:T(8,128)}), f32[32,10,128]{2,1,0:T(8,128)S(1)}, u32[]{:S(2)}, u32[]{:S(2)}) async-start(f32[32,10,128]{2,1,0:T(8,128)} %get-tuple-element.37), calls=%async_computation.2 | async-start | bytes 524288 | tf_op jit(solution)/shard_map/all_to_all | solution.py:650
  60.0 7.7 %copy-start.6 = (bf16[4,2,256,256]{3,2,1,0:T(8,128)(2,1)}, bf16[4,2,256,256]{3,2,1,0:T(8,128)(2,1)S(1)}, u32[]{:S(2)}) copy-start(bf16[4,2,256,256]{3,2,1,0:T(8,128)(2,1)S(1)} %collective-permute-done.4.other_ref.other_raw_ref) | copy-start | bytes 3145732
  97.4 29.9 %all-to-all-start.3 = ((f16[16,128,256]{2,1,0:T(8,128)(2,1)}), f16[16,128,256]{2,1,0:T(8,128)(2,1)S(1)}, u32[]{:S(2)}, u32[]{:S(2)}) async-start(f16[16,128,256]{2,1,0:T(8,128)(2,1)} %bitcast.13), calls=%async_computation.3 | async-start | bytes 2097152 | tf_op jit(solution)/shard_map/all_to_all | solution.py:650
  101.3 1.6 %copy-start.5 = (bf16[256,4096]{1,0:T(8,128)(2,1)S(1)}, bf16[256,4096]{1,0:T(8,128)(2,1)}, u32[]{:S(2)}) copy-start(bf16[256,4096]{1,0:T(8,128)(2,1)} %copy-done.2) | copy-start | bytes 6291460
  102.9 1.6 %copy-start.9 = (bf16[2,2,256,1024]{3,2,1,0:T(8,128)(2,1)S(1)}, bf16[2,2,256,1024]{3,2,1,0:T(8,128)(2,1)}, u32[]{:S(2)}) copy-start(bf16[2,2,256,1024]{3,2,1,0:T(8,128)(2,1)} %get-tuple-element.47.turned_ref) | copy-start | bytes 6291460
  127.3 19.0 %all-to-all-start.4 = ((f16[8,16,4352]{2,1,0:T(8,128)(2,1)}), f16[8,16,4352]{2,1,0:T(8,128)(2,1)S(1)}, u32[]{:S(2)}, u32[]{:S(2)}) async-start(f16[8,16,4352]{2,1,0:T(8,128)(2,1)} %bitcast.14), calls=%async_computation.4 | async-start | bytes 2228224 | tf_op jit(solution)/shard_map/all_to_all | solution.py:650
  131.4 16.9 %collective-permute-start.6 = (f32[128,256]{1,0:T(8,128)S(1)}, f32[128,256]{1,0:T(8,128)S(1)}, u32[]{:S(2)}, u32[]{:S(2)}) collective-permute-start(f32[128,256]{1,0:T(8,128)S(1)} %broadcast_multiply_fusion), channel_id=1, source_target_pairs={{0,1},{1,0},{2,3},{3,2},{4,5},{5,4},{6,7},{7,6},{8,9},{9,8},{10,11... | collective-permute-start | bytes 393224 | tf_op jit(solution)/shard_map/ppermute | solution.py:646

commit v6 on v5

--- a/solution.py
+++ b/solution.py
@@ -674,7 +674,7 @@
     tiled = jnp.tile(teacher, (all_chips, 1))
     tea_own = exchange(tiled, ("half", "chip"))
     weights, norm, near_total = local_denominator(
-        tie(where, tiled), students, prototypes, 0, 1, 4, columns
+        where, students, prototypes, 0, 1, 4, columns
     )
     tea_other = swap(tea_own, "core")
     parcel_one, tea_unit, mark = sweep_call(
@@ -695,7 +695,7 @@
     (far_total,) = local_denominator(tie(where, mark), students, prototypes, 1, 3, 4)
 
     markers = [near_total, mark, far_total]
-    gathered = tie(students, tiled)[None]
+    gathered = students[None]
     bit = all_chips // 2
     while bit:
         came = lax.ppermute(

time: 150 us -> 150 us (level)
  no operation moved by 1% of the time
where the time goes in v6:
time: 150 us; the launch traced here: 149 us
  Pallas kernels  81.1 us (54%)
  starting transfers between devices  29.2 us (19%)
  waiting for transfers between devices  23.9 us (16%)
  local copies, waits for them, and re-layouts  10.1 us (7%)
  other arithmetic  4.03 us (3%)
    pallas_call x1, Pallas kernels, near_gradients(): pl.pallas_call(functools.partial(near_kernel, plan=plan, sub=tile_of(each...  25.7 us
    pallas_call x1, Pallas kernels, far_gradients(): pl.pallas_call(functools.partial(far_kernel, plan=plan, sub=tile_of(each,...  21.7 us
    all_to_all x5, starting transfers between devices, exchange(): return lax.all_to_all(value, axes, split_axis=0, concat_axis=0, tiled=True)  21.6 us
    pallas_call x2, Pallas kernels, local_denominator(): pl.pallas_call(functools.partial(denominator_kernel, sub=tile_of(tile, 51...  16.7 us
    all_to_all x5, waiting for transfers between devices, exchange(): return lax.all_to_all(value, axes, split_axis=0, concat_axis=0, tiled=True)  16.1 us
    unnamed x20, local copies, waits for them, and re-layouts  8.59 us
    pallas_call x1, Pallas kernels, pair(): pl.pallas_call(functools.partial(pair_kernel, plan=plan), out_shape=[jax....  7.72 us
    pallas_call x2, Pallas kernels, sweep_call(): pl.pallas_call(functools.partial(kernel, plan=plan, sub=tile_of(columns,...  7.43 us
  transfers between devices with their start and end apart: 12, of which 6 were waited for; matrix products, arithmetic and copies ran while one was open for 1% of the time, Pallas kernels for 37%

profile of v6, /device:TPU:0, one launch (start us, length us, event | category | flops | bytes accessed | tf_op | source)
XLA Modules:
  0.0 149.2 jit_solution(6870550502794158541)
XLA Ops:
  0.6 1.5 tile.2
  2.1 7.3 %all-to-all-start = ((bf16[8,64,256]{2,1,0:T(8,128)(2,1)}), bf16[8,64,256]{2,1,0:T(8,128)(2,1)S(1)}, u32[]{:S(2)}, u32[]{:S(2)}) async-start(bf16[8,64,256]{2,1,0:T(8,128)(2,1)} %tile.2), calls=%async_computation | async-start | bytes 524288 | tf_op jit(solution)/shard_map/all_to_all | solution.py:650
  9.4 2.9 %collective-permute-start.1 = (bf16[1,256,256]{2,1,0:T(8,128)(2,1)}, bf16[1,256,256]{2,1,0:T(8,128)(2,1)S(1)}, u32[]{:S(2)}, u32[]{:S(2)}) collective-permute-start(bf16[1,256,256]{2,1,0:T(8,128)(2,1)} %bitcast.16), channel_id=1, source_target_pairs={{0,16},{4,20},{8,24},{12,28},{16,0},{20,4},{24,8},{28,12},{1,17},{... | collective-permute-start | bytes 393224 | tf_op jit(solution)/shard_map/ppermute | solution.py:701
  12.4 0.9 copy-done
  13.3 6.1 %denominator.2 = (bf16[256,4096]{1,0:T(8,128)(2,1)S(1)}, f32[1,4096]{1,0:T(1,128)S(1)}, f32[2,128]{1,0:T(2,128)S(1)}) custom-call(s32[3]{0:T(128)S(1)} %pad_add_fusion.where_ref, bf16[256,256]{1,0:T(8,128)(2,1)S(1)} %copy-done, bf16[256,32768]{1,0:T(8,128)(2,1)} %raw_ref.1, bf16[256,32768]{1,0:T(8,128)(2,1)} %raw_ref.1), custom_call_target="tpu_custom_call" | custom-call | flops 1073741824 | bytes 4194304 | tf_op jit(solution)/shard_map/denominator/pallas_call | solution.py:165
  19.4 1.3 copy-done.2
  20.7 3.2 %collective-permute-done.1 = bf16[1,256,256]{2,1,0:T(8,128)(2,1)S(1)} collective-permute-done((bf16[1,256,256]{2,1,0:T(8,128)(2,1)}, bf16[1,256,256]{2,1,0:T(8,128)(2,1)S(1)}, u32[]{:S(2)}, u32[]{:S(2)}) %collective-permute-start.1) | collective-permute-done | bytes 131104 | tf_op jit(solution)/shard_map/ppermute | solution.py:701
  24.0 1.4 collective-permute-done.other_ref
  25.5 1.6 %copy-done.3 = bf16[256,4096]{1,0:T(8,128)(2,1)S(1)} copy-done((bf16[256,4096]{1,0:T(8,128)(2,1)S(1)}, bf16[256,4096]{1,0:T(8,128)(2,1)}, u32[]{:S(2)}) %copy-start.3) | copy-done | bytes 2097176
  27.1 3.8 %first_sweep.1 = (f32[32,10,128]{2,1,0:T(8,128)}, bf16[1024,256]{1,0:T(8,128)(2,1)S(1)}, f32[8,128]{1,0:T(8,128)}) custom-call(s32[3]{0:T(128)S(1)} %pad_add_fusion.where_ref, bf16[512,256]{1,0:T(8,128)(2,1)S(1)} %bitcast.24, bf16[512,256]{1,0:T(8,128)(2,1)S(1)} %collective-permute-done.other_ref, bf16[256,4096]{1,0:T(8,128)(2,1)S(1)} %copy-done.3, ...), custom_call_target="tpu_custom_call" | custom-call | flops 1073741824 | bytes 1572864 | tf_op jit(solution)/shard_map/first_sweep/pallas_call | solution.py:236
  30.8 1.9 %collective-permute-done.2 = bf16[2,256,256]{2,1,0:T(8,128)(2,1)S(1)} collective-permute-done((bf16[2,256,256]{2,1,0:T(8,128)(2,1)S(1)}, bf16[2,256,256]{2,1,0:T(8,128)(2,1)S(1)}, u32[]{:S(2)}, u32[]{:S(2)}) %collective-permute-start.2) | collective-permute-done | bytes 262176 | tf_op jit(solution)/shard_map/ppermute | solution.py:701
  32.8 1.5 collective-permute-start.3
  34.3 2.8 %all-to-all-start.1 = ((f32[32,10,128]{2,1,0:T(8,128)}), f32[32,10,128]{2,1,0:T(8,128)S(1)}, u32[]{:S(2)}, u32[]{:S(2)}) async-start(f32[32,10,128]{2,1,0:T(8,128)} %get-tuple-element.31), calls=%async_computation.1 | async-start | bytes 524288 | tf_op jit(solution)/shard_map/all_to_all | solution.py:650
  37.0 10.7 %denominator.3.far_ref = f32[2,128]{1,0:T(2,128)S(1)} custom-call(s32[3]{0:T(128)S(1)} %pad_add_fusion.where_ref, bf16[256,256]{1,0:T(8,128)(2,1)S(1)} %copy-done.1, bf16[256,32768]{1,0:T(8,128)(2,1)} %raw_ref.1), custom_call_target="tpu_custom_call" | custom-call | flops 3221225472 | bytes 12582912 | tf_op jit(solution)/shard_map/denominator/pallas_call | solution.py:165
  47.7 1.3 collective-permute-done.3
  49.3 1.6 %copy-done.4 = bf16[256,4096]{1,0:T(8,128)(2,1)S(1)} copy-done((bf16[256,4096]{1,0:T(8,128)(2,1)S(1)}, bf16[256,4096]{1,0:T(8,128)(2,1)}, u32[]{:S(2)}) %copy-start.4) | copy-done | bytes 2097176
  50.8 3.6 %second_sweep.1 = (f32[32,10,128]{2,1,0:T(8,128)}, f32[1,2048]{1,0:T(1,128)S(1)}) custom-call(s32[3]{0:T(128)S(1)} %pad_add_fusion.where_ref, bf16[1024,256]{1,0:T(8,128)(2,1)S(1)} %get-tuple-element.30.unit_ref.teacher_ref, bf16[256,4096]{1,0:T(8,128)(2,1)S(1)} %copy-done.4, f32[32,10,128]{2,1,0:T(8,128)S(1)} %all-to-all-done.1.came_ref.first_ref, ...), custom_call_target="tpu_custom_call" | custom-call | flops 1073741824 | bytes 1572864 | tf_op jit(solution)/shard_map/second_sweep/pallas_call | solution.py:236
  54.5 1.5 collective-permute-start.5
  56.0 3.9 %all-to-all-start.2 = ((f32[32,10,128]{2,1,0:T(8,128)}), f32[32,10,128]{2,1,0:T(8,128)S(1)}, u32[]{:S(2)}, u32[]{:S(2)}) async-start(f32[32,10,128]{2,1,0:T(8,128)} %get-tuple-element.34), calls=%async_computation.2 | async-start | bytes 524288 | tf_op jit(solution)/shard_map/all_to_all | solution.py:650
  60.0 7.7 %pair.1 = (bf16[2,2,2,1024,256]{4,3,2,1,0:T(8,128)(2,1)}, bf16[2,2,256,1024]{3,2,1,0:T(8,128)(2,1)}, bf16[4096,256]{1,0:T(8,128)(2,1)}) custom-call(s32[3]{0:T(128)S(1)} %pad_add_fusion.where_ref, bf16[4,2,256,256]{3,2,1,0:T(8,128)(2,1)S(1)} %bitcast.21, bf16[4,2,256,256]{3,2,1,0:T(8,128)(2,1)S(1)} %collective-permute-done.4.other_ref.other_raw_ref, ...), custom_call_target="tpu_custom_call" | custom-call | flops 2147483648 | bytes 8388608 | tf_op jit(solution)/shard_map/pair/pallas_call | solution.py:294
  67.7 2.7 %all-to-all-done.2.second_ref = f32[32,10,128]{2,1,0:T(8,128)S(1)} async-done(((f32[32,10,128]{2,1,0:T(8,128)}), f32[32,10,128]{2,1,0:T(8,128)S(1)}, u32[]{:S(2)}, u32[]{:S(2)}) %all-to-all-start.2) | async-done | bytes 163872 | tf_op jit(solution)/shard_map/all_to_all | solution.py:650
  70.4 25.7 %near_gradients.1 = (f32[1024,256]{1,0:T(8,128)S(1)}, f32[1024,256]{1,0:T(8,128)S(1)}, f32[256,4096]{1,0:T(8,128)}) custom-call(s32[3]{0:T(128)S(1)} %pad_add_fusion.where_ref, bf16[2,2,2,1024,256]{4,3,2,1,0:T(8,128)(2,1)} %get-tuple-element.42.both_ref, bf16[2,2,256,1024]{3,2,1,0:T(8,128)(2,1)} %get-tuple-element.43.turned_ref, ...), custom_call_target="tpu_custom_call" | custom-call | flops 17179869184 | bytes 8388608 | tf_op jit(solution)/shard_map/near_gradients/pallas_call | solution.py:468
  96.2 1.2 fusion
  97.4 3.9 %all-to-all-start.3 = ((f16[16,128,256]{2,1,0:T(8,128)(2,1)}), f16[16,128,256]{2,1,0:T(8,128)(2,1)S(1)}, u32[]{:S(2)}, u32[]{:S(2)}) async-start(f16[16,128,256]{2,1,0:T(8,128)(2,1)} %bitcast.12), calls=%async_computation.3 | async-start | bytes 2097152 | tf_op jit(solution)/shard_map/all_to_all | solution.py:650
  101.3 1.6 %copy-done.5 = bf16[256,4096]{1,0:T(8,128)(2,1)S(1)} copy-done((bf16[256,4096]{1,0:T(8,128)(2,1)S(1)}, bf16[256,4096]{1,0:T(8,128)(2,1)}, u32[]{:S(2)}) %copy-start.5) | copy-done | bytes 2097176
  102.9 1.6 %copy-done.9 = bf16[2,2,256,1024]{3,2,1,0:T(8,128)(2,1)S(1)} copy-done((bf16[2,2,256,1024]{3,2,1,0:T(8,128)(2,1)S(1)}, bf16[2,2,256,1024]{3,2,1,0:T(8,128)(2,1)}, u32[]{:S(2)}) %copy-start.9) | copy-done | bytes 2097176
  104.5 21.7 %far_gradients.1 = f32[128,4352]{1,0:T(8,128)S(1)} custom-call(s32[3]{0:T(128)S(1)} %pad_add_fusion.where_ref, bf16[2,2,2,1024,256]{4,3,2,1,0:T(8,128)(2,1)} %get-tuple-element.42.both_ref, bf16[2,2,256,1024]{3,2,1,0:T(8,128)(2,1)S(1)} %copy-done.9, f32[32,10,128]{2,1,0:T(8,128)S(1)} %all-to-all-done.1.came_ref.first_ref, ...), custom_call_target="tpu_custom_call" | custom-call | flops 12884901888 | bytes 8388608 | tf_op jit(solution)/shard_map/far_gradients/pallas_call | solution.py:579
  126.2 1.1 convert_element_type.23
  127.3 3.8 %all-to-all-start.4 = ((f16[8,16,4352]{2,1,0:T(8,128)(2,1)}), f16[8,16,4352]{2,1,0:T(8,128)(2,1)S(1)}, u32[]{:S(2)}, u32[]{:S(2)}) async-start(f16[8,16,4352]{2,1,0:T(8,128)(2,1)} %bitcast.13), calls=%async_computation.4 | async-start | bytes 2228224 | tf_op jit(solution)/shard_map/all_to_all | solution.py:650
  131.4 1.5 %collective-permute-start.6 = (f32[128,256]{1,0:T(8,128)S(1)}, f32[128,256]{1,0:T(8,128)S(1)}, u32[]{:S(2)}, u32[]{:S(2)}) collective-permute-start(f32[128,256]{1,0:T(8,128)S(1)} %broadcast_multiply_fusion), channel_id=1, source_target_pairs={{0,1},{1,0},{2,3},{3,2},{4,5},{5,4},{6,7},{7,6},{8,9},{9,8},{10,11... | collective-permute-start | bytes 393224 | tf_op jit(solution)/shard_map/ppermute | solution.py:646
  133.0 13.3 %all-to-all-done.4 = f16[8,16,4352]{2,1,0:T(8,128)(2,1)S(1)} async-done(((f16[8,16,4352]{2,1,0:T(8,128)(2,1)}), f16[8,16,4352]{2,1,0:T(8,128)(2,1)S(1)}, u32[]{:S(2)}, u32[]{:S(2)}) %all-to-all-start.4) | async-done | bytes 1114144 | tf_op jit(solution)/shard_map/all_to_all | solution.py:650
  146.5 1.9 %join.1 = f32[16,32768]{1,0:T(8,128)} custom-call(f32[8,16,4352]{2,1,0:T(8,128)S(1)} %convert_element_type.24.came_ref), custom_call_target="tpu_custom_call" | custom-call | flops 524288 | bytes 4194304 | tf_op jit(solution)/shard_map/join/pallas_call | solution.py:629
  (37 shorter events, 1.9 us)
Async XLA Ops:
  2.1 21.8 %all-to-all-start = ((bf16[8,64,256]{2,1,0:T(8,128)(2,1)}), bf16[8,64,256]{2,1,0:T(8,128)(2,1)S(1)}, u32[]{:S(2)}, u32[]{:S(2)}) async-start(bf16[8,64,256]{2,1,0:T(8,128)(2,1)} %tile.2), calls=%async_computation | async-start | bytes 524288 | tf_op jit(solution)/shard_map/all_to_all | solution.py:650
  9.4 14.5 %collective-permute-start.1 = (bf16[1,256,256]{2,1,0:T(8,128)(2,1)}, bf16[1,256,256]{2,1,0:T(8,128)(2,1)S(1)}, u32[]{:S(2)}, u32[]{:S(2)}) collective-permute-start(bf16[1,256,256]{2,1,0:T(8,128)(2,1)} %bitcast.16), channel_id=1, source_target_pairs={{0,16},{4,20},{8,24},{12,28},{16,0},{20,4},{24,8},{28,12},{1,17},{... | collective-permute-start | bytes 393224 | tf_op jit(solution)/shard_map/ppermute | solution.py:701
  12.4 0.9 copy-start
  13.3 10.6 %copy-start.1 = (bf16[256,256]{1,0:T(8,128)(2,1)S(1)}, bf16[256,256]{1,0:T(8,128)(2,1)}, u32[]{:S(2)}) copy-start(bf16[256,256]{1,0:T(8,128)(2,1)} %students_ref.3) | copy-start | bytes 393220
  13.3 12.2 %copy-start.7 = (s32[256]{0:T(256)S(1)}, s32[256]{0:T(256)}, u32[]{:S(2)}) copy-start(s32[256]{0:T(256)} %param.8) | copy-start | bytes 3076
  13.3 12.2 %copy-start.8 = (s32[256]{0:T(256)S(1)}, s32[256]{0:T(256)}, u32[]{:S(2)}) copy-start(s32[256]{0:T(256)} %param.9) | copy-start | bytes 3076
  19.4 1.3 copy-start.2
  23.9 1.5 %collective-permute-start = (bf16[512,256]{1,0:T(8,128)(2,1)S(1)}, bf16[512,256]{1,0:T(8,128)(2,1)S(1)}, u32[]{:S(2)}, u32[]{:S(2)}) collective-permute-start(bf16[512,256]{1,0:T(8,128)(2,1)S(1)} %bitcast.23), channel_id=1, source_target_pairs={{0,2},{2,0},{1,3},{3,1},{4,6},{6,4},{5,7},{7,5},{8,10},{10,8},{9,1... | collective-permute-start | bytes 786440 | tf_op jit(solution)/shard_map/ppermute | solution.py:646
  24.0 8.8 %collective-permute-start.2 = (bf16[2,256,256]{2,1,0:T(8,128)(2,1)S(1)}, bf16[2,256,256]{2,1,0:T(8,128)(2,1)S(1)}, u32[]{:S(2)}, u32[]{:S(2)}) collective-permute-start(bf16[2,256,256]{2,1,0:T(8,128)(2,1)S(1)} %pad_maximum_fusion.2), channel_id=1, source_target_pairs={{0,8},{4,12},{8,0},{12,4},{16,24},{20,28},{24,16},{28,20},{1,9},{5... | collective-permute-start | bytes 786440 | tf_op jit(solution)/shard_map/ppermute | solution.py:701
  25.5 1.6 %copy-start.3 = (bf16[256,4096]{1,0:T(8,128)(2,1)S(1)}, bf16[256,4096]{1,0:T(8,128)(2,1)}, u32[]{:S(2)}) copy-start(bf16[256,4096]{1,0:T(8,128)(2,1)} %copy-done.2) | copy-start | bytes 6291460
  32.8 16.2 %collective-permute-start.3 = (bf16[4,256,256]{2,1,0:T(8,128)(2,1)S(1)}, bf16[4,256,256]{2,1,0:T(8,128)(2,1)S(1)}, u32[]{:S(2)}, u32[]{:S(2)}) collective-permute-start(bf16[4,256,256]{2,1,0:T(8,128)(2,1)S(1)} %pad_maximum_fusion.1), channel_id=1, source_target_pairs={{0,4},{4,0},{8,12},{12,8},{16,20},{20,16},{24,28},{28,24},{1,5},{5... | collective-permute-start | bytes 1572872 | tf_op jit(solution)/shard_map/ppermute | solution.py:701
  34.3 15.0 %all-to-all-start.1 = ((f32[32,10,128]{2,1,0:T(8,128)}), f32[32,10,128]{2,1,0:T(8,128)S(1)}, u32[]{:S(2)}, u32[]{:S(2)}) async-start(f32[32,10,128]{2,1,0:T(8,128)} %get-tuple-element.31), calls=%async_computation.1 | async-start | bytes 524288 | tf_op jit(solution)/shard_map/all_to_all | solution.py:650
  49.2 10.8 %collective-permute-start.4 = (bf16[4,2,256,256]{3,2,1,0:T(8,128)(2,1)S(1)}, bf16[4,2,256,256]{3,2,1,0:T(8,128)(2,1)S(1)}, u32[]{:S(2)}, u32[]{:S(2)}) collective-permute-start(bf16[4,2,256,256]{3,2,1,0:T(8,128)(2,1)S(1)} %bitcast.20), channel_id=1, source_target_pairs={{0,2},{2,0},{1,3},{3,1},{4,6},{6,4},{5,7},{7,5},{8,10},{10,8},{9,1... | collective-permute-start | bytes 3145736 | tf_op jit(solution)/shard_map/ppermute | solution.py:646
  49.2 1.6 %copy-start.4 = (bf16[256,4096]{1,0:T(8,128)(2,1)S(1)}, bf16[256,4096]{1,0:T(8,128)(2,1)}, u32[]{:S(2)}) copy-start(bf16[256,4096]{1,0:T(8,128)(2,1)} %copy-done.2) | copy-start | bytes 6291460
  54.5 5.4 %collective-permute-start.5 = (f32[1,2048]{1,0:T(1,128)S(1)}, f32[1,2048]{1,0:T(1,128)S(1)}, u32[]{:S(2)}, u32[]{:S(2)}) collective-permute-start(f32[1,2048]{1,0:T(1,128)S(1)} %get-tuple-element.45), channel_id=1, source_target_pairs={{0,16},{16,0},{1,17},{17,1},{2,18},{18,2},{3,19},{19,3},{4,20},{20... | collective-permute-start | bytes 24584 | tf_op jit(solution)/shard_map/ppermute | solution.py:732
  56.0 14.4 %all-to-all-start.2 = ((f32[32,10,128]{2,1,0:T(8,128)}), f32[32,10,128]{2,1,0:T(8,128)S(1)}, u32[]{:S(2)}, u32[]{:S(2)}) async-start(f32[32,10,128]{2,1,0:T(8,128)} %get-tuple-element.34), calls=%async_computation.2 | async-start | bytes 524288 | tf_op jit(solution)/shard_map/all_to_all | solution.py:650
  60.0 7.7 %copy-start.6 = (bf16[4,2,256,256]{3,2,1,0:T(8,128)(2,1)}, bf16[4,2,256,256]{3,2,1,0:T(8,128)(2,1)S(1)}, u32[]{:S(2)}) copy-start(bf16[4,2,256,256]{3,2,1,0:T(8,128)(2,1)S(1)} %collective-permute-done.4.other_ref.other_raw_ref) | copy-start | bytes 3145732
  97.4 29.9 %all-to-all-start.3 = ((f16[16,128,256]{2,1,0:T(8,128)(2,1)}), f16[16,128,256]{2,1,0:T(8,128)(2,1)S(1)}, u32[]{:S(2)}, u32[]{:S(2)}) async-start(f16[16,128,256]{2,1,0:T(8,128)(2,1)} %bitcast.12), calls=%async_computation.3 | async-start | bytes 2097152 | tf_op jit(solution)/shard_map/all_to_all | solution.py:650
  101.3 1.6 %copy-start.5 = (bf16[256,4096]{1,0:T(8,128)(2,1)S(1)}, bf16[256,4096]{1,0:T(8,128)(2,1)}, u32[]{:S(2)}) copy-start(bf16[256,4096]{1,0:T(8,128)(2,1)} %copy-done.2) | copy-start | bytes 6291460
  102.9 1.6 %copy-start.9 = (bf16[2,2,256,1024]{3,2,1,0:T(8,128)(2,1)S(1)}, bf16[2,2,256,1024]{3,2,1,0:T(8,128)(2,1)}, u32[]{:S(2)}) copy-start(bf16[2,2,256,1024]{3,2,1,0:T(8,128)(2,1)} %get-tuple-element.43.turned_ref) | copy-start | bytes 6291460
  127.3 19.0 %all-to-all-start.4 = ((f16[8,16,4352]{2,1,0:T(8,128)(2,1)}), f16[8,16,4352]{2,1,0:T(8,128)(2,1)S(1)}, u32[]{:S(2)}, u32[]{:S(2)}) async-start(f16[8,16,4352]{2,1,0:T(8,128)(2,1)} %bitcast.13), calls=%async_computation.4 | async-start | bytes 2228224 | tf_op jit(solution)/shard_map/all_to_all | solution.py:650
  131.4 16.9 %collective-permute-start.6 = (f32[128,256]{1,0:T(8,128)S(1)}, f32[128,256]{1,0:T(8,128)S(1)}, u32[]{:S(2)}, u32[]{:S(2)}) collective-permute-start(f32[128,256]{1,0:T(8,128)S(1)} %broadcast_multiply_fusion), channel_id=1, source_target_pairs={{0,1},{1,0},{2,3},{3,2},{4,5},{5,4},{6,7},{7,6},{8,9},{9,8},{10,11... | collective-permute-start | bytes 393224 | tf_op jit(solution)/shard_map/ppermute | solution.py:646
